TPU v7x, 32 devices: a whole 2x2x4 slice. The times are simulated.
32 devices in a mesh: rows: 2 (over x), heads: 8 (over z, y), seq: 2 (over core).
Axes of the slice: x: 2, y: 2, z: 4, core: 2. Of those that a mesh axis runs over, the one named last changes fastest.
Arguments:
- inputs: bfloat16 [4, 2, 2, 1024, 2048], P(None, 'rows', 'seq', 'heads'), may hold values from -6 to 6
- segment_ids: int32 [4, 2, 2048], P(None, 'rows'), may hold values from 0 to 6, as said below
- cotangent: bfloat16 [4, 2, 2, 1024, 2048], P(None, 'rows', 'seq', 'heads'), may hold values from -6 to 6
- attn_gain: bfloat16 [2048], P(('rows', 'heads', 'seq')), may hold values from 0.5 to 1.5
- ffn_gain: bfloat16 [2048], P(('rows', 'heads', 'seq')), may hold values from 0.5 to 1.5
- query_weight: bfloat16 [2048, 2048], P(('rows', 'seq'), 'heads'), may hold values from -0.125 to 0.125
- key_weight: bfloat16 [2048, 512], P(('rows', 'seq')), may hold values from -0.125 to 0.125
- value_weight: bfloat16 [2048, 512], P(('rows', 'seq')), may hold values from -0.125 to 0.125
- output_weight: bfloat16 [2048, 2048], P('heads', ('rows', 'seq')), may hold values from -1 to 1
- query_down: bfloat16 [2048, 8], P(('rows', 'heads', 'seq')), may hold values from -0.125 to 0.125
- query_lift: bfloat16 [8, 2048], P(('rows', 'seq'), 'heads'), may hold values from -1.5 to 1.5
- key_down: bfloat16 [2048, 8], P(('rows', 'heads', 'seq')), may hold values from -0.125 to 0.125
- key_lift: bfloat16 [8, 512], P(('rows', 'seq')), may hold values from -1.5 to 1.5
- value_down: bfloat16 [2048, 8], P(('rows', 'heads', 'seq')), may hold values from -0.125 to 0.125
- value_lift: bfloat16 [8, 512], P(('rows', 'seq')), may hold values from -1.5 to 1.5
- output_down: bfloat16 [2048, 8], P('heads', ('rows', 'seq')), may hold values from -1 to 1
- output_lift: bfloat16 [8, 2048], P(None, ('rows', 'heads', 'seq')), may hold values from -1.5 to 1.5
- feature_maps: bfloat16 [32, 64, 64], P('heads', ('rows', 'seq')), may hold values from -0.75 to 0.75
- gate_weight: bfloat16 [2048, 8192], P(('rows', 'seq'), 'heads'), may hold values from -0.125 to 0.125
- up_weight: bfloat16 [2048, 8192], P(('rows', 'seq'), 'heads'), may hold values from -0.125 to 0.125
- down_weight: bfloat16 [8192, 2048], P('heads', ('rows', 'seq')), may hold values from -0.0625 to 0.0625
Outputs:
- output: bfloat16 [4, 2, 2, 1024, 2048], P(None, 'rows', 'seq', 'heads')
- input_grad: float32 [4, 2, 2, 1024, 2048], P(None, 'rows', 'seq', 'heads')
- attn_gain_grad: float32 [2048], P(('rows', 'heads', 'seq'))
- ffn_gain_grad: float32 [2048], P(('rows', 'heads', 'seq'))
- query_weight_grad: float32 [2048, 2048], P(('rows', 'seq'), 'heads')
- key_weight_grad: float32 [2048, 512], P(('rows', 'seq'))
- value_weight_grad: float32 [2048, 512], P(('rows', 'seq'))
- output_weight_grad: float32 [2048, 2048], P('heads', ('rows', 'seq'))
- query_down_grad: float32 [2048, 8], P(('rows', 'heads', 'seq'))
- query_lift_grad: float32 [8, 2048], P(('rows', 'seq'), 'heads')
- key_down_grad: float32 [2048, 8], P(('rows', 'heads', 'seq'))
- key_lift_grad: float32 [8, 512], P(('rows', 'seq'))
- value_down_grad: float32 [2048, 8], P(('rows', 'heads', 'seq'))
- value_lift_grad: float32 [8, 512], P(('rows', 'seq'))
- output_down_grad: float32 [2048, 8], P('heads', ('rows', 'seq'))
- output_lift_grad: float32 [8, 2048], P(None, ('rows', 'heads', 'seq'))
- feature_maps_grad: float32 [32, 64, 64], P('heads', ('rows', 'seq'))
- gate_weight_grad: float32 [2048, 8192], P(('rows', 'seq'), 'heads')
- up_weight_grad: float32 [2048, 8192], P(('rows', 'seq'), 'heads')
- down_weight_grad: float32 [8192, 2048], P('heads', ('rows', 'seq'))
Inputs may be any that keep to these rules, and one draw needn't show every extreme that they name: `segment_ids`: each row's segment ids start at 0 on its first token and never fall from one token to the next.
All inputs are finite; a program needn't handle non-finite values.
Results may differ from a plain program's by a relative error of at most 0.014.
Values may be sent and summed in bfloat16 or wider, within the bound.
No kernel may reach another device: no remote copies, remote signals or barrier semaphores. Data moves between devices by JAX's collectives and lax.ppermute only.
A program may use at most 704 MiB of HBM per device.

v0:
```python
import jax
import jax.numpy as jnp
from jax import lax
from jax.sharding import PartitionSpec as P

HEADS = 32
KV = 8
HD = 64
WINDOW = 64


highest = lax.Precision.HIGHEST


def from_behind(value, axis, steps):
    count = lax.axis_size(axis)
    first, last = (max(0, -steps), min(count, count - steps))
    return lax.ppermute(value, axis, [(source, source + steps) for source in range(first, last)])


def entering(array, axis, join, neutral, backward):
    count = lax.axis_size(axis)
    place = lax.axis_index(axis)
    ahead = count - 1 - place if backward else place
    gathered = jax.tree.map(
        lambda a, kind: lax.all_gather(a.astype(kind), axis),
        array,
        jax.tree.map(lambda a: jnp.bfloat16 if a.dtype == jnp.float32 else a.dtype, array),
    )
    state = jax.tree.map(lambda a, e: jnp.zeros_like(a) + jnp.asarray(e, a.dtype), array, neutral)

    def one(lap, state):
        source = count - 1 - lap if backward else lap
        return join(
            state,
            jax.tree.map(
                lambda a, own: lax.dynamic_index_in_dim(a, source, 0, False).astype(own.dtype),
                gathered,
                array,
            ),
        )

    return lax.fori_loop(0, ahead, one, state)


def matmul_low(left, right):
    return jnp.dot(left, right, preferred_element_type=jnp.float32)


def matmul_high(left, right):
    return jnp.dot(left, right, precision=highest, preferred_element_type=jnp.float32)


def feature_map(vectors, maps):
    logits = jnp.einsum("che,hef->chf", vectors, maps, precision=highest)
    return jnp.concatenate(
        [jax.nn.softmax(logits, axis=-1), jax.nn.softmax(-logits, axis=-1)], axis=-1
    )


def block_terms(features, values, segment):
    lasts = segment[:, -1]
    keeper = jnp.where(segment == lasts[:, None], 1.0, 0.0)
    weighted = features * keeper[:, :, None, None]
    states = jnp.einsum("nwhf,nwhe->nhfe", weighted, values, precision=highest)
    return (states, jnp.sum(weighted, axis=1), lasts[:, None, None, None])


def link_states(earlier, latter):
    early_states, early_totals, early_tags = earlier
    late_states, late_totals, late_tags = latter
    joined = jnp.where(early_tags == late_tags, 1.0, 0.0)
    vacant = late_tags < 0.0
    states = jnp.where(vacant, early_states, late_states + joined * early_states)
    totals = jnp.where(vacant[..., 0], early_totals, late_totals + joined[..., 0] * early_totals)
    return (states, totals, jnp.where(vacant, early_tags, late_tags))


def window_attend(queries, key_rows, value_rows, key_segment, query_segment, maps, initial):
    length, head_count, head_width = queries.shape
    block_count = length // WINDOW
    query_features = feature_map(queries, maps)
    key_features = feature_map(key_rows, maps)
    feat_width = key_features.shape[-1]
    key_blocks = key_rows.reshape(block_count + 1, WINDOW, head_count, head_width)
    value_blocks = value_rows.reshape(block_count + 1, WINDOW, head_count, head_width)
    feature_blocks = key_features.reshape(block_count + 1, WINDOW, head_count, feat_width)
    segment_blocks = key_segment.reshape(block_count + 1, WINDOW)
    terms = block_terms(feature_blocks, value_blocks, segment_blocks)
    empty = (
        jnp.zeros_like(terms[0][:1]),
        jnp.zeros_like(terms[1][:1]),
        jnp.full_like(terms[2][:1], -1.0),
    )
    ordered = jax.tree.map(
        lambda first, others: jnp.concatenate([first, others[: block_count - 1]], axis=0),
        empty,
        terms,
    )
    states = link_states(initial, lax.associative_scan(link_states, ordered))
    query_blocks = queries.reshape(block_count, WINDOW, head_count, head_width)
    query_feat_blocks = query_features.reshape(block_count, WINDOW, head_count, feat_width)
    own_segment = query_segment.reshape(block_count, WINDOW)
    pair_keys = jnp.concatenate([key_blocks[:-1], key_blocks[1:]], axis=1)
    pair_values = jnp.concatenate([value_blocks[:-1], value_blocks[1:]], axis=1)
    pair_features = jnp.concatenate([feature_blocks[:-1], feature_blocks[1:]], axis=1)
    pair_segment = jnp.concatenate([segment_blocks[:-1], segment_blocks[1:]], axis=1)
    places = jnp.arange(WINDOW)
    slots = jnp.arange(2 * WINDOW)
    earlier_block = slots[None, :] < WINDOW
    offsets = slots[None, :] % WINDOW
    inside = jnp.where(earlier_block, offsets > places[:, None], offsets <= places[:, None])
    linear = earlier_block & (offsets <= places[:, None])
    matched = own_segment[:, :, None] == pair_segment[:, None, :]
    window_mask = (inside[None] & matched)[:, None]
    linear_mask = jnp.where(linear[None] & matched, 1.0, 0.0)[:, None]
    scores = jnp.einsum(
        "nqhe,nkhe->nhqk", query_blocks, pair_keys, precision=highest
    ) * head_width ** (-0.5)
    peak = jnp.max(jnp.where(window_mask, scores, -1e30), axis=-1, keepdims=True)
    weights = jnp.where(window_mask, jnp.exp(jnp.where(window_mask, scores - peak, 0.0)), 0.0)
    linear_weights = (
        jnp.einsum("nqhf,nkhf->nhqk", query_feat_blocks, pair_features, precision=highest)
        * linear_mask
    )
    carried = jnp.where(own_segment == states[2][:, 0, 0, 0][:, None], 1.0, 0.0)
    state_num = (
        jnp.einsum("nqhf,nhfe->nqhe", query_feat_blocks, states[0], precision=highest)
        * carried[:, :, None, None]
    )
    state_den = (
        jnp.einsum("nqhf,nhf->nqh", query_feat_blocks, states[1], precision=highest)
        * carried[:, :, None]
    )
    damping = jnp.exp(-jnp.transpose(peak[..., 0], (0, 2, 1)))
    numerator = jnp.einsum("nhqk,nkhe->nqhe", weights, pair_values, precision=highest) + damping[
        ..., None
    ] * (jnp.einsum("nhqk,nkhe->nqhe", linear_weights, pair_values, precision=highest) + state_num)
    denominator = jnp.transpose(jnp.sum(weights, axis=-1), (0, 2, 1)) + damping * (
        jnp.transpose(jnp.sum(linear_weights, axis=-1), (0, 2, 1)) + state_den
    )
    return (numerator / denominator[..., None]).reshape(length, head_count * head_width)


def element_row(prev_keys, prev_values, key_heads, value_heads, key_segment, maps):
    local_len, head_count, head_width = key_heads.shape
    block_count = local_len // WINDOW
    key_span = jnp.concatenate([prev_keys, key_heads], axis=0)[:local_len]
    value_span = jnp.concatenate([prev_values, value_heads], axis=0)[:local_len]
    features = feature_map(key_span, maps)
    terms = block_terms(
        features.reshape(block_count, WINDOW, head_count, -1),
        value_span.reshape(block_count, WINDOW, head_count, head_width),
        key_segment[:local_len].reshape(block_count, WINDOW),
    )
    prefix = lax.associative_scan(link_states, terms)
    return jax.tree.map(lambda member: member[-1], prefix)


def attend_row(
    queries,
    key_heads,
    value_heads,
    prev_keys,
    prev_values,
    maps,
    start_states,
    start_totals,
    start_tags,
    key_segment,
    query_segment,
):
    return window_attend(
        queries,
        jnp.concatenate([prev_keys, key_heads], axis=0),
        jnp.concatenate([prev_values, value_heads], axis=0),
        key_segment,
        query_segment,
        maps,
        (start_states, start_totals, start_tags),
    )


def norm_forward(values, gain):
    scale = lax.rsqrt(jnp.mean(values * values, axis=-1, keepdims=True) + 1e-05)
    return (values * scale * gain, scale)


def norm_backward(values, gain, scale, grad_normed):
    unit = values * scale
    scaled = grad_normed * gain
    grad_values = scale * (scaled - unit * jnp.mean(scaled * unit, axis=-1, keepdims=True))
    return (grad_values, jnp.sum(grad_normed * unit, axis=(0, 1)))


def gather_rows(values):
    return lax.all_gather(values, "heads", axis=1, tiled=True)


def reduce_rows(values):
    return lax.psum_scatter(values, "heads", scatter_dimension=1, tiled=True)


def gather_back(values):
    return lax.all_gather(values, "heads", axis=1, tiled=True)


def reduce_back(values):
    return lax.psum_scatter(values, "heads", scatter_dimension=1, tiled=True)


def reduce_grads(local, group):
    (
        gain_one_g,
        gain_two_g,
        query_g,
        key_g,
        value_g,
        output_g,
        query_down_g,
        query_raise_g,
        key_down_g,
        key_raise_g,
        value_down_g,
        value_raise_g,
        output_low_g,
        output_raise_g,
        maps_g,
        gate_g,
        upper_g,
        lower_g,
    ) = local
    column_count = KV * HD

    def place(part_grad):
        zeros_full = jnp.zeros((part_grad.shape[0], column_count), jnp.float32)
        return lax.dynamic_update_slice_in_dim(zeros_full, part_grad, group * part_grad.shape[1], 1)

    placed = (place(key_g), place(value_g), place(key_raise_g), place(value_raise_g))
    placed = (
        lax.psum(placed[0].astype(jnp.bfloat16), "heads").astype(jnp.float32),
        lax.psum(placed[1].astype(jnp.bfloat16), "heads").astype(jnp.float32),
        lax.psum(placed[2].astype(jnp.bfloat16), "heads").astype(jnp.float32),
        lax.psum(placed[3].astype(jnp.bfloat16), "heads").astype(jnp.float32),
    )
    reduced = (
        lax.psum_scatter(
            query_g.astype(jnp.bfloat16), ("rows", "seq"), scatter_dimension=0, tiled=True
        ).astype(jnp.float32),
        lax.psum_scatter(
            placed[0].astype(jnp.bfloat16), ("rows", "seq"), scatter_dimension=0, tiled=True
        ).astype(jnp.float32),
        lax.psum_scatter(
            placed[1].astype(jnp.bfloat16), ("rows", "seq"), scatter_dimension=0, tiled=True
        ).astype(jnp.float32),
        lax.psum_scatter(
            query_raise_g.astype(jnp.bfloat16), ("rows", "seq"), scatter_dimension=0, tiled=True
        ).astype(jnp.float32),
        lax.psum_scatter(
            placed[2].astype(jnp.bfloat16), ("rows", "seq"), scatter_dimension=0, tiled=True
        ).astype(jnp.float32),
        lax.psum_scatter(
            placed[3].astype(jnp.bfloat16), ("rows", "seq"), scatter_dimension=0, tiled=True
        ).astype(jnp.float32),
        lax.psum_scatter(
            gate_g.astype(jnp.bfloat16), ("rows", "seq"), scatter_dimension=0, tiled=True
        ).astype(jnp.float32),
        lax.psum_scatter(
            upper_g.astype(jnp.bfloat16), ("rows", "seq"), scatter_dimension=0, tiled=True
        ).astype(jnp.float32),
        lax.psum_scatter(
            output_g.astype(jnp.bfloat16), ("rows", "seq"), scatter_dimension=1, tiled=True
        ).astype(jnp.float32),
        lax.psum_scatter(
            output_low_g.astype(jnp.bfloat16), ("rows", "seq"), scatter_dimension=1, tiled=True
        ).astype(jnp.float32),
        lax.psum_scatter(
            lower_g.astype(jnp.bfloat16), ("rows", "seq"), scatter_dimension=1, tiled=True
        ).astype(jnp.float32),
        lax.psum_scatter(
            maps_g.astype(jnp.bfloat16), ("rows", "seq"), scatter_dimension=1, tiled=True
        ).astype(jnp.float32),
    )
    key_sum, value_sum, key_raise_sum, value_raise_sum = (
        reduced[1],
        reduced[2],
        reduced[4],
        reduced[5],
    )
    minor = (
        lax.psum_scatter(gain_one_g, ("rows", "heads", "seq"), scatter_dimension=0, tiled=True),
        lax.psum_scatter(gain_two_g, ("rows", "heads", "seq"), scatter_dimension=0, tiled=True),
        lax.psum_scatter(query_down_g, ("rows", "heads", "seq"), scatter_dimension=0, tiled=True),
        lax.psum_scatter(key_down_g, ("rows", "heads", "seq"), scatter_dimension=0, tiled=True),
        lax.psum_scatter(value_down_g, ("rows", "heads", "seq"), scatter_dimension=0, tiled=True),
        lax.psum_scatter(output_raise_g, ("rows", "heads", "seq"), scatter_dimension=1, tiled=True),
    )
    return (
        minor[0],
        minor[1],
        reduced[0],
        key_sum,
        value_sum,
        reduced[8],
        minor[2],
        reduced[3],
        minor[3],
        key_raise_sum,
        minor[4],
        value_raise_sum,
        reduced[9],
        minor[5],
        reduced[11],
        reduced[6],
        reduced[7],
        reduced[10],
    )


def micro_batch(layer_in, grad_in, row_segment, weights):
    (
        gain_one,
        gain_two,
        query_mat,
        key_mat,
        value_mat,
        output_mat,
        down_mats,
        query_raise,
        key_raise,
        value_raise,
        output_low,
        output_raise,
        maps,
        gate_mat,
        upper_mat,
        lower_mat,
    ) = weights
    row_count, token_share, model_width = layer_in.shape
    local_len = token_share * lax.axis_size("heads")
    seq_index = lax.axis_index("seq")
    per_device = maps.shape[0]
    head_width = key_mat.shape[1]
    rank_width = down_mats.shape[1] // 3
    token_total = row_count * local_len
    own_segment = lax.dynamic_slice_in_dim(row_segment, seq_index * local_len, local_len, 1)
    prev_start = jnp.maximum(seq_index * local_len - WINDOW, 0)
    prev_segment = jnp.where(
        seq_index > 0, lax.dynamic_slice_in_dim(row_segment, prev_start, WINDOW, 1), -1
    )
    query_segment = own_segment.astype(jnp.float32)
    key_segment = jnp.concatenate([prev_segment, own_segment], axis=1).astype(jnp.float32)
    residual_in = layer_in.astype(jnp.float32)
    normed_one, scale_one = norm_forward(residual_in, gain_one)
    flat_rows = gather_rows(normed_one.astype(jnp.bfloat16)).reshape(token_total, model_width)
    low_rank = matmul_low(flat_rows, down_mats)
    query_low = low_rank[:, :rank_width]
    key_low = low_rank[:, rank_width : 2 * rank_width]
    value_low = low_rank[:, 2 * rank_width :]
    query_flat = matmul_low(flat_rows, query_mat) + matmul_high(
        query_low, query_raise.astype(jnp.float32)
    )
    key_flat = matmul_low(flat_rows, key_mat) + matmul_high(key_low, key_raise.astype(jnp.float32))
    value_flat = matmul_low(flat_rows, value_mat) + matmul_high(
        value_low, value_raise.astype(jnp.float32)
    )
    queries = query_flat.reshape(row_count, local_len, per_device, head_width)
    key_own = key_flat.reshape(row_count, local_len, head_width)
    value_own = value_flat.reshape(row_count, local_len, head_width)
    repeat_shape = (row_count, local_len, per_device, head_width)
    key_heads = jnp.broadcast_to(key_own[:, :, None, :], repeat_shape)
    value_heads = jnp.broadcast_to(value_own[:, :, None, :], repeat_shape)
    edge = jnp.concatenate(
        [key_own[:, local_len - WINDOW :], value_own[:, local_len - WINDOW :]], axis=-1
    )
    arrived = from_behind(edge, "seq", 1)
    halo_shape = (row_count, WINDOW, per_device, head_width)
    prev_keys = jnp.broadcast_to(arrived[:, :, None, :head_width], halo_shape)
    prev_values = jnp.broadcast_to(arrived[:, :, None, head_width:], halo_shape)

    def element_all(keys_prior, values_prior, keys_here, values_here, maps_here):
        return jax.vmap(element_row, in_axes=(0, 0, 0, 0, 0, None))(
            keys_prior, values_prior, keys_here, values_here, key_segment, maps_here
        )

    elements, element_pull = jax.vjp(
        element_all, prev_keys, prev_values, key_heads, value_heads, maps
    )
    vacant = (
        jnp.zeros_like(elements[0]),
        jnp.zeros_like(elements[1]),
        jnp.full_like(elements[2], -1.0),
    )
    starts = entering(elements, "seq", link_states, vacant, False)

    def attend_all(
        query_here,
        keys_here,
        values_here,
        keys_prior,
        values_prior,
        maps_here,
        states_here,
        totals_here,
    ):
        return jax.vmap(attend_row, in_axes=(0, 0, 0, 0, 0, None, 0, 0, 0, 0, 0))(
            query_here,
            keys_here,
            values_here,
            keys_prior,
            values_prior,
            maps_here,
            states_here,
            totals_here,
            starts[2],
            key_segment,
            query_segment,
        )

    mixed, attend_pull = jax.vjp(
        attend_all,
        queries,
        key_heads,
        value_heads,
        prev_keys,
        prev_values,
        maps,
        starts[0],
        starts[1],
    )
    mixed_low = mixed.reshape(token_total, -1).astype(jnp.bfloat16)
    out_rank = matmul_low(mixed_low, output_low)
    branch_part = matmul_low(mixed_low, output_mat) + matmul_high(
        out_rank, output_raise.astype(jnp.float32)
    )
    middle = residual_in + reduce_rows(branch_part.reshape(row_count, local_len, model_width))
    normed_two, scale_two = norm_forward(middle, gain_two)
    ffn_rows = gather_rows(normed_two.astype(jnp.bfloat16)).reshape(token_total, model_width)
    gate_pre = matmul_low(ffn_rows, gate_mat)
    upper_pre = matmul_low(ffn_rows, upper_mat)
    sigmoid_gate = jax.nn.sigmoid(gate_pre)
    swish_gate = gate_pre * sigmoid_gate
    hidden = (swish_gate * upper_pre).astype(jnp.bfloat16)
    ffn_out = reduce_rows(matmul_low(hidden, lower_mat).reshape(row_count, local_len, model_width))
    result = (middle + ffn_out).astype(jnp.bfloat16)
    grad_rows = gather_back(grad_in).reshape(token_total, model_width)
    lower_g = matmul_low(hidden.T, grad_rows)
    grad_hidden = matmul_low(grad_rows, lower_mat.T)
    grad_gate = (
        grad_hidden * upper_pre * sigmoid_gate * (1.0 + gate_pre * (1.0 - sigmoid_gate))
    ).astype(jnp.bfloat16)
    grad_upper = (grad_hidden * swish_gate).astype(jnp.bfloat16)
    gate_g = matmul_low(ffn_rows.T, grad_gate)
    upper_g = matmul_low(ffn_rows.T, grad_upper)
    grad_ffn_rows = matmul_low(grad_gate, gate_mat.T) + matmul_low(grad_upper, upper_mat.T)
    grad_normed_two = reduce_back(grad_ffn_rows.reshape(row_count, local_len, model_width))
    grad_mid_norm, gain_two_g = norm_backward(middle, gain_two, scale_two, grad_normed_two)
    grad_middle = grad_in.astype(jnp.float32) + grad_mid_norm
    grad_branch = gather_back(grad_middle.astype(jnp.bfloat16)).reshape(token_total, model_width)
    output_g = matmul_low(mixed_low.T, grad_branch)
    output_raise_g = matmul_high(out_rank.T, grad_branch.astype(jnp.float32))
    grad_out_rank = matmul_low(grad_branch, output_raise.T)
    output_low_g = matmul_high(mixed_low.astype(jnp.float32).T, grad_out_rank)
    grad_mixed = matmul_low(grad_branch, output_mat.T) + matmul_high(
        grad_out_rank, output_low.astype(jnp.float32).T
    )
    (
        grad_query,
        grad_key_att,
        grad_value_att,
        grad_pkey_att,
        grad_pvalue_att,
        maps_g_att,
        grad_states,
        grad_totals,
    ) = attend_pull(grad_mixed.reshape(row_count, local_len, -1))
    returned = entering((grad_states, grad_totals, starts[2]), "seq", link_states, vacant, True)
    guard = jnp.where(returned[2] == elements[2], 1.0, 0.0)
    grad_pkey_elem, grad_pvalue_elem, grad_key_elem, grad_value_elem, maps_g_elem = element_pull(
        (returned[0] * guard, returned[1] * guard[..., 0], jnp.zeros_like(elements[2]))
    )
    back_edge = jnp.concatenate(
        [grad_pkey_att + grad_pkey_elem, grad_pvalue_att + grad_pvalue_elem], axis=-1
    )
    came_back = from_behind(back_edge.astype(jnp.bfloat16), "seq", -1).astype(back_edge.dtype)
    padding = ((0, 0), (local_len - WINDOW, 0), (0, 0), (0, 0))
    key_grad_low = (
        (grad_key_att + grad_key_elem + jnp.pad(came_back[..., :head_width], padding))
        .reshape(token_total, -1)
        .astype(jnp.bfloat16)
    )
    value_grad_low = (
        (grad_value_att + grad_value_elem + jnp.pad(came_back[..., head_width:], padding))
        .reshape(token_total, -1)
        .astype(jnp.bfloat16)
    )
    query_grad_low = grad_query.reshape(token_total, -1).astype(jnp.bfloat16)
    query_g = matmul_low(flat_rows.T, query_grad_low)
    key_g = (
        matmul_low(flat_rows.T, key_grad_low)
        .reshape(model_width, per_device, head_width)
        .sum(axis=1)
    )
    value_g = (
        matmul_low(flat_rows.T, value_grad_low)
        .reshape(model_width, per_device, head_width)
        .sum(axis=1)
    )
    key_grad_sum = (
        key_grad_low.astype(jnp.float32).reshape(token_total, per_device, head_width).sum(axis=1)
    )
    value_grad_sum = (
        value_grad_low.astype(jnp.float32).reshape(token_total, per_device, head_width).sum(axis=1)
    )
    query_raise_g = matmul_high(query_low.T, query_grad_low.astype(jnp.float32))
    key_raise_g = matmul_high(key_low.T, key_grad_sum)
    value_raise_g = matmul_high(value_low.T, value_grad_sum)
    grad_low_rank = jnp.concatenate(
        [
            matmul_low(query_grad_low, query_raise.T),
            matmul_high(key_grad_sum, key_raise.astype(jnp.float32).T),
            matmul_high(value_grad_sum, value_raise.astype(jnp.float32).T),
        ],
        axis=1,
    )
    down_g = matmul_high(flat_rows.astype(jnp.float32).T, grad_low_rank)
    grad_flat = (
        matmul_low(query_grad_low, query_mat.T)
        + matmul_low(key_grad_low, jnp.tile(key_mat, (1, per_device)).T)
        + matmul_low(value_grad_low, jnp.tile(value_mat, (1, per_device)).T)
        + matmul_high(grad_low_rank, down_mats.astype(jnp.float32).T)
    )
    grad_normed_one = reduce_back(grad_flat.reshape(row_count, local_len, model_width))
    grad_in_norm, gain_one_g = norm_backward(residual_in, gain_one, scale_one, grad_normed_one)
    input_grad = grad_middle + grad_in_norm
    local = (
        gain_one_g,
        gain_two_g,
        query_g,
        key_g,
        value_g,
        output_g,
        down_g[:, :rank_width],
        query_raise_g,
        down_g[:, rank_width : 2 * rank_width],
        key_raise_g,
        down_g[:, 2 * rank_width :],
        value_raise_g,
        output_low_g,
        output_raise_g,
        maps_g_att + maps_g_elem,
        gate_g,
        upper_g,
        lower_g,
    )
    return (result, input_grad, local)


def body(
    inputs,
    segment_ids,
    cotangent,
    attn_gain,
    ffn_gain,
    query_weight,
    key_weight,
    value_weight,
    output_weight,
    query_down,
    query_lift,
    key_down,
    key_lift,
    value_down,
    value_lift,
    output_down,
    output_lift,
    feature_maps,
    gate_weight,
    up_weight,
    down_weight,
):
    head_index = lax.axis_index("heads")
    per_device = HEADS // lax.axis_size("heads")
    group = head_index * per_device // (HEADS // KV)
    gathered = (
        lax.all_gather(query_weight, ("rows", "seq"), axis=0, tiled=True),
        lax.all_gather(key_weight, ("rows", "seq"), axis=0, tiled=True),
        lax.all_gather(value_weight, ("rows", "seq"), axis=0, tiled=True),
        lax.all_gather(query_lift, ("rows", "seq"), axis=0, tiled=True),
        lax.all_gather(key_lift, ("rows", "seq"), axis=0, tiled=True),
        lax.all_gather(value_lift, ("rows", "seq"), axis=0, tiled=True),
        lax.all_gather(gate_weight, ("rows", "seq"), axis=0, tiled=True),
        lax.all_gather(up_weight, ("rows", "seq"), axis=0, tiled=True),
        lax.all_gather(output_weight, ("rows", "seq"), axis=1, tiled=True),
        lax.all_gather(output_down, ("rows", "seq"), axis=1, tiled=True),
        lax.all_gather(down_weight, ("rows", "seq"), axis=1, tiled=True),
        lax.all_gather(feature_maps, ("rows", "seq"), axis=1, tiled=True),
    )
    minor = (
        lax.all_gather(attn_gain, ("rows", "heads", "seq"), axis=0, tiled=True),
        lax.all_gather(ffn_gain, ("rows", "heads", "seq"), axis=0, tiled=True),
        lax.all_gather(query_down, ("rows", "heads", "seq"), axis=0, tiled=True),
        lax.all_gather(key_down, ("rows", "heads", "seq"), axis=0, tiled=True),
        lax.all_gather(value_down, ("rows", "heads", "seq"), axis=0, tiled=True),
        lax.all_gather(output_lift, ("rows", "heads", "seq"), axis=1, tiled=True),
    )

    def select_group(whole):
        return lax.dynamic_slice_in_dim(whole, group * HD, HD, 1)

    weights = (
        minor[0].astype(jnp.float32),
        minor[1].astype(jnp.float32),
        gathered[0],
        select_group(gathered[1]),
        select_group(gathered[2]),
        gathered[8],
        jnp.concatenate([minor[2], minor[3], minor[4]], axis=1),
        gathered[3],
        select_group(gathered[4]),
        select_group(gathered[5]),
        gathered[9],
        minor[5],
        gathered[11].astype(jnp.float32),
        gathered[6],
        gathered[7],
        gathered[10],
    )
    outputs = []
    input_grads = []
    totals = None
    for batch_index in range(inputs.shape[0]):
        result, input_grad, local = micro_batch(
            inputs[batch_index, :, 0],
            cotangent[batch_index, :, 0],
            segment_ids[batch_index],
            weights,
        )
        outputs.append(result)
        input_grads.append(input_grad)
        reduced = reduce_grads(local, group)
        totals = reduced if totals is None else jax.tree.map(jnp.add, totals, reduced)
    return (jnp.stack(outputs)[:, :, None], jnp.stack(input_grads)[:, :, None]) + tuple(totals)


def solution(mesh):
    placed = (
        P(None, "rows", "seq", "heads", None),
        P(None, "rows", None),
        P(None, "rows", "seq", "heads", None),
        P(("rows", "heads", "seq")),
        P(("rows", "heads", "seq")),
        P(("rows", "seq"), "heads"),
        P(("rows", "seq"), None),
        P(("rows", "seq"), None),
        P("heads", ("rows", "seq")),
        P(("rows", "heads", "seq"), None),
        P(("rows", "seq"), "heads"),
        P(("rows", "heads", "seq"), None),
        P(("rows", "seq"), None),
        P(("rows", "heads", "seq"), None),
        P(("rows", "seq"), None),
        P("heads", ("rows", "seq")),
        P(None, ("rows", "heads", "seq")),
        P("heads", ("rows", "seq"), None),
        P(("rows", "seq"), "heads"),
        P(("rows", "seq"), "heads"),
        P("heads", ("rows", "seq")),
    )
    return jax.shard_map(
        body,
        mesh=mesh,
        in_specs=placed,
        out_specs=(
            P(None, "rows", "seq", "heads", None),
            P(None, "rows", "seq", "heads", None),
            P(("rows", "heads", "seq")),
            P(("rows", "heads", "seq")),
            P(("rows", "seq"), "heads"),
            P(("rows", "seq"), None),
            P(("rows", "seq"), None),
            P("heads", ("rows", "seq")),
            P(("rows", "heads", "seq"), None),
            P(("rows", "seq"), "heads"),
            P(("rows", "heads", "seq"), None),
            P(("rows", "seq"), None),
            P(("rows", "heads", "seq"), None),
            P(("rows", "seq"), None),
            P("heads", ("rows", "seq")),
            P(None, ("rows", "heads", "seq")),
            P("heads", ("rows", "seq"), None),
            P(("rows", "seq"), "heads"),
            P(("rows", "seq"), "heads"),
            P("heads", ("rows", "seq")),
        ),
        check_vma=False,
    )
```

profile of v0, /device:TPU:0, one launch (start us, length us, event | category | flops | bytes accessed | tf_op | source)
XLA Modules:
  0.0 7337.9 jit_solution(8239174955470320315)
XLA Ops:
  10.5 42.3 all-reduce.546
  233.1 41.3 all-gather.20
  274.6 37.4 all-gather.21
  312.1 39.3 all-gather.22
  351.5 36.9 all-gather.27
  710.0 16.6 pad.4508
  941.3 16.7 pad.2333
  958.0 17.1 pad.2334
  1103.3 16.6 pad.2237
  1282.8 16.8 pad.2285
  1461.2 16.6 pad.2189
  1540.1 148.9 %reduce-scatter.61.cloned.1.call-done = f32[1,128,2048]{2,1,0:T(8,128)} async-done(((f32[1,1024,2048]{2,1,0:T(8,128)}), f32[1,128,2048]{2,1,0:T(8,128)}) %reduce-scatter.61.cloned.1.call-update) | async-done | bytes 1048592 | tf_op jit(solution)/shard_map/reduce_scatter | solution.py:201
  1699.8 24.3 all-gather.70.cloned.1.call-done
  1724.1 76.0 %all-gather.66.cloned.1.call-done = bf16[1,1024,2048]{2,1,0:T(8,128)(2,1)} async-done(((bf16[1,128,2048]{2,1,0:T(8,128)(2,1)}), bf16[1,1024,2048]{2,1,0:T(8,128)(2,1)}) %all-gather.66.cloned.1.call-update) | async-done | bytes 4194320 | tf_op jit(solution)/shard_map/all_gather | solution.py:197
  1810.2 24.1 all-gather.68.cloned.1.call-done
  1844.3 26.0 all-gather.72.cloned.1.call-done
  1870.2 75.4 %all-gather.94.cloned.1.call-done = bf16[1,1,1,1024,2048]{4,3,2,1,0:T(8,128)(2,1)} async-done(((bf16[1,1,1,128,2048]{4,3,2,1,0:T(8,128)(2,1)}), bf16[1,1,1,1024,2048]{4,3,2,1,0:T(8,128)(2,1)}) %all-gather.94.cloned.1.call-update) | async-done | bytes 4194320 | tf_op jit(solution)/shard_map/all_gather | solution.py:205
  1970.7 49.2 all-gather.80.cloned.1.call-done
  2036.3 57.9 all-gather.98.cloned.1.call-done
  2119.9 125.2 %reduce-scatter.77.cloned.1.call-done = f32[1,128,2048]{2,1,0:T(8,128)} async-done(((f32[1,1024,2048]{2,1,0:T(8,128)}), f32[1,128,2048]{2,1,0:T(8,128)}) %reduce-scatter.77.cloned.1.call-update) | async-done | bytes 1048592 | tf_op jit(solution)/shard_map/reduce_scatter | solution.py:209
  2245.1 152.1 %reduce-scatter.85.cloned.1.call-done = f32[1,128,2048]{2,1,0:T(8,128)} async-done(((f32[1,1024,2048]{2,1,0:T(8,128)}), f32[1,128,2048]{2,1,0:T(8,128)}) %reduce-scatter.85.cloned.1.call-update) | async-done | bytes 1048592 | tf_op jit(solution)/shard_map/reduce_scatter | solution.py:209
  2403.4 70.4 all-gather.76.cloned.1.call-done
  2489.9 57.7 all-gather.96.cloned.1.call-done
  2576.0 45.9 all-gather.84.cloned.1.call-done
  2638.1 57.7 all-gather.100.cloned.1.call-done
  2745.7 100.8 %reduce-scatter.81.cloned.1.call-done = f32[1,128,2048]{2,1,0:T(8,128)} async-done(((f32[1,1024,2048]{2,1,0:T(8,128)}), f32[1,128,2048]{2,1,0:T(8,128)}) %reduce-scatter.81.cloned.1.call-update) | async-done | bytes 1048592 | tf_op jit(solution)/shard_map/reduce_scatter | solution.py:209
  2846.5 151.9 %reduce-scatter.89.cloned.1.call-done = f32[1,128,2048]{2,1,0:T(8,128)} async-done(((f32[1,1024,2048]{2,1,0:T(8,128)}), f32[1,128,2048]{2,1,0:T(8,128)}) %reduce-scatter.89.cloned.1.call-update) | async-done | bytes 1048592 | tf_op jit(solution)/shard_map/reduce_scatter | solution.py:209
  3003.3 146.9 %reduce-scatter.67.cloned.1.call-done = f32[1,128,2048]{2,1,0:T(8,128)} async-done(((f32[1,1024,2048]{2,1,0:T(8,128)}), f32[1,128,2048]{2,1,0:T(8,128)}) %reduce-scatter.67.cloned.1.call-update) | async-done | bytes 1048592 | tf_op jit(solution)/shard_map/reduce_scatter | solution.py:201
  3150.2 152.1 %reduce-scatter.75.cloned.1.call-done = f32[1,128,2048]{2,1,0:T(8,128)} async-done(((f32[1,1024,2048]{2,1,0:T(8,128)}), f32[1,128,2048]{2,1,0:T(8,128)}) %reduce-scatter.75.cloned.1.call-update) | async-done | bytes 1048592 | tf_op jit(solution)/shard_map/reduce_scatter | solution.py:201
  3329.8 47.5 all-gather.86.cloned.1.call-done
  3405.4 46.3 all-gather.88.cloned.1.call-done
  3492.5 33.0 all-gather.90.cloned.1.call-done
  3733.8 16.7 pad.4535
  4567.6 16.6 pad.3200
  4603.9 16.7 pad.4529
  5253.1 21.2 reduce-scatter.125.cloned.1.call-done
  5274.2 47.1 reduce-scatter.131.cloned.1.call-done
  5321.3 47.1 reduce-scatter.127.cloned.1.call-done
  5372.8 17.5 reduce-scatter.109.cloned.1.call-done
  5390.3 22.0 reduce-scatter.113.cloned.1.call-done
  5412.3 21.9 reduce-scatter.111.cloned.1.call-done
  5434.2 22.0 reduce-scatter.115.cloned.1.call-done
  5457.6 35.4 all-reduce.557.cloned.1.call-done
  5498.6 37.1 all-reduce.547
  5539.5 90.5 %reduce-scatter.163.cloned.1.call-done = f32[64,8]{1,0:T(8,128)} async-done(((f32[2048,8]{1,0:T(8,128)}), f32[64,8]{1,0:T(8,128)}) %reduce-scatter.163.cloned.1.call-update) | async-done | bytes 2064
  5631.4 132.0 %reduce-scatter.161.cloned.1.call-done = f32[64,8]{1,0:T(8,128)} async-done(((f32[2048,8]{1,0:T(8,128)}), f32[64,8]{1,0:T(8,128)}) %reduce-scatter.161.cloned.1.call-update) | async-done | bytes 2064
  5764.8 132.0 %reduce-scatter.159.cloned.1.call-done = f32[64,8]{1,0:T(8,128)} async-done(((f32[2048,8]{1,0:T(8,128)}), f32[64,8]{1,0:T(8,128)}) %reduce-scatter.159.cloned.1.call-update) | async-done | bytes 2064
  5898.3 132.0 %reduce-scatter.157.cloned.1.call-done = f32[64,8]{1,0:T(8,128)} async-done(((f32[2048,8]{1,0:T(8,128)}), f32[64,8]{1,0:T(8,128)}) %reduce-scatter.157.cloned.1.call-update) | async-done | bytes 2064
  6031.7 22.4 reduce-scatter.101.cloned.1.call-done
  6054.1 27.3 reduce-scatter.107.cloned.1.call-done
  6081.5 27.6 reduce-scatter.103.cloned.1.call-done
  6109.1 27.3 reduce-scatter.105.cloned.1.call-done
  6138.5 25.4 reduce-scatter.93.cloned.1.call-done
  6163.9 28.1 reduce-scatter.99.cloned.1.call-done
  6191.9 28.2 reduce-scatter.97.cloned.1.call-done
  6220.2 27.9 reduce-scatter.95.cloned.1.call-done
  6250.2 162.3 %all-reduce.555.cloned.1.call-done = (bf16[512,512]{1,0:T(8,128)(2,1)}, bf16[512,512]{1,0:T(8,128)(2,1)}, bf16[512,512]{1,0:T(8,128)(2,1)}, bf16[512,512]{1,0:T(...) async-done(((bf16[512,512]{1,0:T(8,128)(2,1)}, bf16[512,512]{1,0:T(8,128)(2,1)}, ...) | async-done | bytes 4194320 | tf_op jit(solution)/shard_map/psum | solution.py:241
  6416.7 147.5 %reduce-scatter.83.cloned.1.call-done = f32[1,128,2048]{2,1,0:T(8,128)} async-done(((f32[1,1024,2048]{2,1,0:T(8,128)}), f32[1,128,2048]{2,1,0:T(8,128)}) %reduce-scatter.83.cloned.1.call-update) | async-done | bytes 1048592 | tf_op jit(solution)/shard_map/reduce_scatter | solution.py:209
  6564.2 151.5 %reduce-scatter.87.cloned.1.call-done = f32[1,128,2048]{2,1,0:T(8,128)} async-done(((f32[1,1024,2048]{2,1,0:T(8,128)}), f32[1,128,2048]{2,1,0:T(8,128)}) %reduce-scatter.87.cloned.1.call-update) | async-done | bytes 1048592 | tf_op jit(solution)/shard_map/reduce_scatter | solution.py:209
  6715.7 152.0 %reduce-scatter.91.cloned.1.call-done = f32[1,128,2048]{2,1,0:T(8,128)} async-done(((f32[1,1024,2048]{2,1,0:T(8,128)}), f32[1,128,2048]{2,1,0:T(8,128)}) %reduce-scatter.91.cloned.1.call-update) | async-done | bytes 1048592 | tf_op jit(solution)/shard_map/reduce_scatter | solution.py:209
  6867.7 151.7 %reduce-scatter.79.cloned.1.call-done = f32[1,128,2048]{2,1,0:T(8,128)} async-done(((f32[1,1024,2048]{2,1,0:T(8,128)}), f32[1,128,2048]{2,1,0:T(8,128)}) %reduce-scatter.79.cloned.1.call-update) | async-done | bytes 1048592 | tf_op jit(solution)/shard_map/reduce_scatter | solution.py:209
  7022.8 42.0 all-reduce.545
  7072.2 100.0 %reduce-scatter.63.cloned.1.call-done = f32[1,128,2048]{2,1,0:T(8,128)} async-done(((f32[1,1024,2048]{2,1,0:T(8,128)}), f32[1,128,2048]{2,1,0:T(8,128)}) %reduce-scatter.63.cloned.1.call-update) | async-done | bytes 1048592 | tf_op jit(solution)/shard_map/reduce_scatter | solution.py:201
  7176.2 147.8 %reduce-scatter.71.cloned.1.call-done = f32[1,128,2048]{2,1,0:T(8,128)} async-done(((f32[1,1024,2048]{2,1,0:T(8,128)}), f32[1,128,2048]{2,1,0:T(8,128)}) %reduce-scatter.71.cloned.1.call-update) | async-done | bytes 1048592 | tf_op jit(solution)/shard_map/reduce_scatter | solution.py:201
  (5060 shorter events, 3211.0 us)
Async XLA Ops:
  7.2 401.3 %all-gather.58.cloned.1.call-start = ((), (), s32[]{:S(2)}) async-start(), calls=%async_computation.53 | async-start | bytes 2621440 | tf_op jit(solution)/shard_map/all_gather | solution.py:587
  7.9 401.9 %all-gather.60.cloned.1.call-start = ((), (), s32[]{:S(2)}) async-start(), calls=%async_computation.54 | async-start | bytes 2621440 | tf_op jit(solution)/shard_map/all_gather | solution.py:588
  8.7 402.6 %all-gather.56.cloned.1.call-start = ((), (), s32[]{:S(2)}) async-start(), calls=%async_computation.52 | async-start | bytes 4718592 | tf_op jit(solution)/shard_map/all_gather | solution.py:197
  56.7 359.7 %all-gather.78.cloned.1.call-start = ((), (), s32[]{:S(2)}) async-start(), calls=%async_computation.67 | async-start | bytes 4718592 | tf_op jit(solution)/shard_map/all_gather | solution.py:197
  57.3 363.3 %all-gather.74.cloned.1.call-start = ((), (), s32[]{:S(2)}) async-start(), calls=%async_computation.63 | async-start | bytes 4718592 | tf_op jit(solution)/shard_map/all_gather | solution.py:197
  57.9 366.9 %all-gather.82.cloned.1.call-start = ((), (), s32[]{:S(2)}) async-start(), calls=%async_computation.71 | async-start | bytes 4718592 | tf_op jit(solution)/shard_map/all_gather | solution.py:197
  58.5 404.0 %all-gather.62.cloned.1.call-start = ((), (), s32[]{:S(2)}) async-start(), calls=%async_computation.55 | async-start | bytes 1310720 | tf_op jit(solution)/shard_map/all_gather | solution.py:586
  59.2 931.0 %all-gather.64.cloned.1.call-start = ((), (), s32[]{:S(2)}) async-start(), calls=%async_computation.56 | async-start | bytes 1310720 | tf_op jit(solution)/shard_map/all_gather | solution.py:594
  60.0 1480.1 %reduce-scatter.73.cloned.1.call-start = ((), (), s32[]{:S(2)}) async-start(), calls=%async_computation.72 | async-start | bytes 9437184 | tf_op jit(solution)/shard_map/reduce_scatter | solution.py:201
  998.6 541.5 %reduce-scatter.65.cloned.1.call-start = ((), (), s32[]{:S(2)}) async-start(), calls=%async_computation.64 | async-start | bytes 9437184 | tf_op jit(solution)/shard_map/reduce_scatter | solution.py:201
  1181.1 359.0 %reduce-scatter.69.cloned.1.call-start = ((), (), s32[]{:S(2)}) async-start(), calls=%async_computation.68 | async-start | bytes 9437184 | tf_op jit(solution)/shard_map/reduce_scatter | solution.py:201
  1699.0 395.3 %all-gather.98.cloned.1.call-start = ((), (), s32[]{:S(2)}) async-start(), calls=%async_computation.113 | async-start | bytes 4718592 | tf_op jit(solution)/shard_map/all_gather | solution.py:205
  1699.8 545.3 %reduce-scatter.77.cloned.1.call-start = ((), (), s32[]{:S(2)}) async-start(), calls=%async_computation.75 | async-start | bytes 9437184 | tf_op jit(solution)/shard_map/reduce_scatter | solution.py:209
  1970.7 426.5 %reduce-scatter.85.cloned.1.call-start = ((), (), s32[]{:S(2)}) async-start(), calls=%async_computation.81 | async-start | bytes 9437184 | tf_op jit(solution)/shard_map/reduce_scatter | solution.py:209
  2119.8 354.0 %all-gather.76.cloned.1.call-start = ((), (), s32[]{:S(2)}) async-start(), calls=%async_computation.65 | async-start | bytes 4718592 | tf_op jit(solution)/shard_map/all_gather | solution.py:197
  2403.3 443.2 %reduce-scatter.81.cloned.1.call-start = ((), (), s32[]{:S(2)}) async-start(), calls=%async_computation.78 | async-start | bytes 9437184 | tf_op jit(solution)/shard_map/reduce_scatter | solution.py:209
  2576.0 422.5 %reduce-scatter.89.cloned.1.call-start = ((), (), s32[]{:S(2)}) async-start(), calls=%async_computation.84 | async-start | bytes 9437184 | tf_op jit(solution)/shard_map/reduce_scatter | solution.py:209
  2724.0 426.1 %reduce-scatter.67.cloned.1.call-start = ((), (), s32[]{:S(2)}) async-start(), calls=%async_computation.66 | async-start | bytes 9437184 | tf_op jit(solution)/shard_map/reduce_scatter | solution.py:201
  2734.8 567.5 %reduce-scatter.75.cloned.1.call-start = ((), (), s32[]{:S(2)}) async-start(), calls=%async_computation.74 | async-start | bytes 9437184 | tf_op jit(solution)/shard_map/reduce_scatter | solution.py:201
  2745.6 631.7 %all-gather.86.cloned.1.call-start = ((), (), s32[]{:S(2)}) async-start(), calls=%async_computation.76 | async-start | bytes 4718592 | tf_op jit(solution)/shard_map/all_gather | solution.py:205
  3003.0 448.7 %all-gather.88.cloned.1.call-start = ((), (), s32[]{:S(2)}) async-start(), calls=%async_computation.79 | async-start | bytes 4718592 | tf_op jit(solution)/shard_map/all_gather | solution.py:205
  3329.6 1819.1 %reduce-scatter.141.cloned.1.call-start = ((), (), s32[]{:S(2)}) async-start(), calls=%async_computation.115 | async-start | bytes 2621440 | tf_op jit(solution)/shard_map/reduce_scatter | solution.py:250
  4356.5 792.2 %reduce-scatter.149.cloned.1.call-start = ((), (), s32[]{:S(2)}) async-start(), calls=%async_computation.119 | async-start | bytes 2621440 | tf_op jit(solution)/shard_map/reduce_scatter | solution.py:253
  4395.2 753.5 %reduce-scatter.145.cloned.1.call-start = ((), (), s32[]{:S(2)}) async-start(), calls=%async_computation.117 | async-start | bytes 2621440 | tf_op jit(solution)/shard_map/reduce_scatter | solution.py:250
  4443.2 705.5 %reduce-scatter.153.cloned.1.call-start = ((), (), s32[]{:S(2)}) async-start(), calls=%async_computation.121 | async-start | bytes 2621440 | tf_op jit(solution)/shard_map/reduce_scatter | solution.py:253
  4476.7 672.1 %reduce-scatter.143.cloned.1.call-start = ((), (), s32[]{:S(2)}) async-start(), calls=%async_computation.116 | async-start | bytes 2621440 | tf_op jit(solution)/shard_map/reduce_scatter | solution.py:250
  4601.4 547.4 %reduce-scatter.151.cloned.1.call-start = ((), (), s32[]{:S(2)}) async-start(), calls=%async_computation.120 | async-start | bytes 2621440 | tf_op jit(solution)/shard_map/reduce_scatter | solution.py:253
  4695.8 453.0 %reduce-scatter.147.cloned.1.call-start = ((), (), s32[]{:S(2)}) async-start(), calls=%async_computation.118 | async-start | bytes 2621440 | tf_op jit(solution)/shard_map/reduce_scatter | solution.py:250
  4729.3 419.5 %reduce-scatter.155.cloned.1.call-start = ((), (), s32[]{:S(2)}) async-start(), calls=%async_computation.122 | async-start | bytes 2621440 | tf_op jit(solution)/shard_map/reduce_scatter | solution.py:253
  4742.6 501.8 %reduce-scatter.137.cloned.1.call-start = ((), (), s32[]{:S(2)}) async-start(), calls=%async_computation.109 | async-start | bytes 5242880 | tf_op jit(solution)/shard_map/reduce_scatter | solution.py:277
  4752.4 492.0 %reduce-scatter.133.cloned.1.call-start = ((), (), s32[]{:S(2)}) async-start(), calls=%async_computation.107 | async-start | bytes 5242880 | tf_op jit(solution)/shard_map/reduce_scatter | solution.py:277
  4762.6 481.9 %reduce-scatter.139.cloned.1.call-start = ((), (), s32[]{:S(2)}) async-start(), calls=%async_computation.110 | async-start | bytes 5242880 | tf_op jit(solution)/shard_map/reduce_scatter | solution.py:277
  4772.5 472.0 %reduce-scatter.135.cloned.1.call-start = ((), (), s32[]{:S(2)}) async-start(), calls=%async_computation.108 | async-start | bytes 5242880 | tf_op jit(solution)/shard_map/reduce_scatter | solution.py:277
  4782.4 466.2 %reduce-scatter.121.cloned.1.call-start = ((), (), s32[]{:S(2)}) async-start(), calls=%async_computation.101 | async-start | bytes 5242880 | tf_op jit(solution)/shard_map/reduce_scatter | solution.py:265
  4792.4 456.2 %reduce-scatter.117.cloned.1.call-start = ((), (), s32[]{:S(2)}) async-start(), calls=%async_computation.99 | async-start | bytes 5242880 | tf_op jit(solution)/shard_map/reduce_scatter | solution.py:265
  4802.4 446.2 %reduce-scatter.123.cloned.1.call-start = ((), (), s32[]{:S(2)}) async-start(), calls=%async_computation.102 | async-start | bytes 5242880 | tf_op jit(solution)/shard_map/reduce_scatter | solution.py:265
  4812.3 436.3 %reduce-scatter.119.cloned.1.call-start = ((), (), s32[]{:S(2)}) async-start(), calls=%async_computation.100 | async-start | bytes 5242880 | tf_op jit(solution)/shard_map/reduce_scatter | solution.py:265
  4823.0 430.1 %reduce-scatter.129.cloned.1.call-start = ((), (), s32[]{:S(2)}) async-start(), calls=%async_computation.105 | async-start | bytes 5242880 | tf_op jit(solution)/shard_map/reduce_scatter | solution.py:268
  4833.2 441.0 %reduce-scatter.125.cloned.1.call-start = ((), (), s32[]{:S(2)}) async-start(), calls=%async_computation.103 | async-start | bytes 5242880 | tf_op jit(solution)/shard_map/reduce_scatter | solution.py:268
  4843.2 478.1 %reduce-scatter.131.cloned.1.call-start = ((), (), s32[]{:S(2)}) async-start(), calls=%async_computation.106 | async-start | bytes 5242880 | tf_op jit(solution)/shard_map/reduce_scatter | solution.py:268
  4853.3 515.1 %reduce-scatter.127.cloned.1.call-start = ((), (), s32[]{:S(2)}) async-start(), calls=%async_computation.104 | async-start | bytes 5242880 | tf_op jit(solution)/shard_map/reduce_scatter | solution.py:268
  4869.5 520.8 %reduce-scatter.109.cloned.1.call-start = ((), (), s32[]{:S(2)}) async-start(), calls=%async_computation.95 | async-start | bytes 81920 | tf_op jit(solution)/shard_map/reduce_scatter | solution.py:280
  5065.6 368.6 %reduce-scatter.111.cloned.1.call-start = ((), (), s32[]{:S(2)}) async-start(), calls=%async_computation.96 | async-start | bytes 81920 | tf_op jit(solution)/shard_map/reduce_scatter | solution.py:280
  5070.3 385.9 %reduce-scatter.115.cloned.1.call-start = ((), (), s32[]{:S(2)}) async-start(), calls=%async_computation.98 | async-start | bytes 81920 | tf_op jit(solution)/shard_map/reduce_scatter | solution.py:280
  5075.3 417.7 %all-reduce.557.cloned.1.call-start = ((), (), s32[]{:S(2)}) async-start(), calls=%async_computation.128 | async-start | bytes 196608
  5090.8 539.2 %reduce-scatter.163.cloned.1.call-start = ((), (), s32[]{:S(2)}) async-start(), calls=%async_computation.126 | async-start | bytes 1081344
  5093.1 670.3 %reduce-scatter.161.cloned.1.call-start = ((), (), s32[]{:S(2)}) async-start(), calls=%async_computation.125 | async-start | bytes 1081344
  5108.0 788.9 %reduce-scatter.159.cloned.1.call-start = ((), (), s32[]{:S(2)}) async-start(), calls=%async_computation.124 | async-start | bytes 1081344
  5109.4 920.9 %reduce-scatter.157.cloned.1.call-start = ((), (), s32[]{:S(2)}) async-start(), calls=%async_computation.123 | async-start | bytes 1081344
  5110.8 943.3 %reduce-scatter.101.cloned.1.call-start = ((), (), s32[]{:S(2)}) async-start(), calls=%async_computation.91 | async-start | bytes 1310720 | tf_op jit(solution)/shard_map/reduce_scatter | solution.py:271
  5115.4 966.1 %reduce-scatter.107.cloned.1.call-start = ((), (), s32[]{:S(2)}) async-start(), calls=%async_computation.94 | async-start | bytes 1310720 | tf_op jit(solution)/shard_map/reduce_scatter | solution.py:271
  5120.0 989.1 %reduce-scatter.103.cloned.1.call-start = ((), (), s32[]{:S(2)}) async-start(), calls=%async_computation.92 | async-start | bytes 1310720 | tf_op jit(solution)/shard_map/reduce_scatter | solution.py:271
  5124.6 1011.8 %reduce-scatter.105.cloned.1.call-start = ((), (), s32[]{:S(2)}) async-start(), calls=%async_computation.93 | async-start | bytes 1310720 | tf_op jit(solution)/shard_map/reduce_scatter | solution.py:271
  5129.2 1034.7 %reduce-scatter.93.cloned.1.call-start = ((), (), s32[]{:S(2)}) async-start(), calls=%async_computation.87 | async-start | bytes 1310720 | tf_op jit(solution)/shard_map/reduce_scatter | solution.py:247
  5134.0 1057.9 %reduce-scatter.99.cloned.1.call-start = ((), (), s32[]{:S(2)}) async-start(), calls=%async_computation.90 | async-start | bytes 1310720 | tf_op jit(solution)/shard_map/reduce_scatter | solution.py:247
  5138.7 1081.5 %reduce-scatter.97.cloned.1.call-start = ((), (), s32[]{:S(2)}) async-start(), calls=%async_computation.89 | async-start | bytes 1310720 | tf_op jit(solution)/shard_map/reduce_scatter | solution.py:247
  5143.3 1104.7 %reduce-scatter.95.cloned.1.call-start = ((), (), s32[]{:S(2)}) async-start(), calls=%async_computation.88 | async-start | bytes 1310720 | tf_op jit(solution)/shard_map/reduce_scatter | solution.py:247
  5148.6 1263.9 %all-reduce.555.cloned.1.call-start = ((), (), s32[]{:S(2)}) async-start(), calls=%async_computation.127 | async-start | bytes 8388608 | tf_op jit(solution)/shard_map/psum | solution.py:241
  5149.3 1414.9 %reduce-scatter.83.cloned.1.call-start = ((), (), s32[]{:S(2)}) async-start(), calls=%async_computation.80 | async-start | bytes 9437184 | tf_op jit(solution)/shard_map/reduce_scatter | solution.py:209
  5169.6 1546.1 %reduce-scatter.87.cloned.1.call-start = ((), (), s32[]{:S(2)}) async-start(), calls=%async_computation.83 | async-start | bytes 9437184 | tf_op jit(solution)/shard_map/reduce_scatter | solution.py:209
  5187.4 1680.3 %reduce-scatter.91.cloned.1.call-start = ((), (), s32[]{:S(2)}) async-start(), calls=%async_computation.86 | async-start | bytes 9437184 | tf_op jit(solution)/shard_map/reduce_scatter | solution.py:209
  5204.3 1815.1 %reduce-scatter.79.cloned.1.call-start = ((), (), s32[]{:S(2)}) async-start(), calls=%async_computation.77 | async-start | bytes 9437184 | tf_op jit(solution)/shard_map/reduce_scatter | solution.py:209
  5221.2 1951.0 %reduce-scatter.63.cloned.1.call-start = ((), (), s32[]{:S(2)}) async-start(), calls=%async_computation.62 | async-start | bytes 9437184 | tf_op jit(solution)/shard_map/reduce_scatter | solution.py:201
  5231.6 2092.3 %reduce-scatter.71.cloned.1.call-start = ((), (), s32[]{:S(2)}) async-start(), calls=%async_computation.70 | async-start | bytes 9437184 | tf_op jit(solution)/shard_map/reduce_scatter | solution.py:201
  (1425 other events, 43969.2 us)
Sparse Core Ops, SparseCore 0:
  9.6 25.4 all-gather.57
  62.6 73.2 all-gather.55
  138.5 71.7 all-gather.77
  212.8 72.2 all-gather.73
  287.6 72.3 all-gather.81
  998.7 152.5 reduce-scatter.72
  1181.2 149.4 reduce-scatter.64
  1361.7 149.5 reduce-scatter.68
  1539.3 149.6 reduce-scatter.60
  1690.6 33.4 all-gather.69
  1726.7 73.3 all-gather.65
  1801.5 32.7 all-gather.67
  1835.7 34.4 all-gather.71
  1872.2 73.3 all-gather.93
  1948.2 71.6 all-gather.79
  2022.6 71.6 all-gather.97
  2097.7 147.2 reduce-scatter.76
  2249.1 147.9 reduce-scatter.84
  2401.4 72.3 all-gather.75
  2476.0 71.6 all-gather.95
  2550.2 71.6 all-gather.83
  2624.0 71.6 all-gather.99
  2699.2 147.2 reduce-scatter.80
  2850.4 147.9 reduce-scatter.88
  3002.1 148.0 reduce-scatter.66
  3154.2 147.9 reduce-scatter.74
  3304.8 72.3 all-gather.85
  3380.0 71.6 all-gather.87
  3453.8 71.6 all-gather.89
  3527.5 71.6 all-gather.91
  4356.6 32.6 reduce-scatter.140
  4395.3 33.7 reduce-scatter.148
  4443.3 35.5 reduce-scatter.144
  4481.4 32.6 reduce-scatter.152
  4601.5 38.1 reduce-scatter.142
  4695.9 38.9 reduce-scatter.150
  4737.4 31.4 reduce-scatter.146
  4771.6 31.4 reduce-scatter.154
  4805.6 44.4 reduce-scatter.136
  4852.7 44.4 reduce-scatter.132
  4899.7 44.5 reduce-scatter.138
  4946.8 44.5 reduce-scatter.134
  4993.8 44.4 reduce-scatter.120
  5040.9 44.5 reduce-scatter.116
  5088.4 44.5 reduce-scatter.122
  5135.5 44.5 reduce-scatter.118
  5182.6 44.5 reduce-scatter.128
  5229.7 44.4 reduce-scatter.124
  5276.8 44.4 reduce-scatter.130
  5323.8 44.5 reduce-scatter.126
  5459.9 32.9 all-reduce.556
  5495.1 134.7 reduce-scatter.162
  5632.2 131.1 reduce-scatter.160
  5765.8 131.0 reduce-scatter.158
  5899.1 131.1 reduce-scatter.156
  6167.0 24.9 reduce-scatter.98
  6223.1 24.9 reduce-scatter.94
  6253.4 159.0 all-reduce.554
  6416.4 147.7 reduce-scatter.82
  6567.6 148.0 reduce-scatter.86
  6719.6 148.0 reduce-scatter.90
  6871.3 148.0 reduce-scatter.78
  7023.3 148.8 reduce-scatter.62
  7175.9 148.0 reduce-scatter.70
  (13 shorter events, 277.7 us)
where the time goes:
time: 7420 us; the launch traced here: 7340 us
  waiting for transfers between devices  3630 us (49%)
  local copies, waits for them, and re-layouts  1540 us (21%)
  matrix products  1130 us (15%)
  other arithmetic  577 us (8%)
  blocking collectives  349 us (5%)
  between operations  89.6 us (1%)
    reduce_scatter x8, waiting for transfers between devices, reduce_back(): return lax.psum_scatter(values, 'heads', scatter_dimension=1, tiled=True)  1130 us
    reduce_scatter x8, waiting for transfers between devices, reduce_rows(): return lax.psum_scatter(values, 'heads', scatter_dimension=1, tiled=True)  696 us
    unnamed x82, waiting for transfers between devices  533 us
    dot_general x100, matrix products, matmul_low(): return jnp.dot(left, right, preferred_element_type=jnp.float32)  487 us
    unnamed x2873, local copies, waits for them, and re-layouts  391 us
    all_gather x8, waiting for transfers between devices, gather_back(): return lax.all_gather(values, 'heads', axis=1, tiled=True)  376 us
    pad x136, local copies, waits for them, and re-layouts, window_attend(): states = link_states(initial, lax.associative_scan(link_states, ordered))  361 us
    pad x135, local copies, waits for them, and re-layouts, element_row(): prefix = lax.associative_scan(link_states, terms)  259 us

commit v1 on v0

v1 whole, which is shorter than its diff:
```python
import functools

import jax
import jax.numpy as jnp
from jax import lax
from jax.experimental import pallas as pl
from jax.experimental.pallas import tpu as pltpu
from jax.sharding import PartitionSpec as P

HEADS = 32
KV = 8
HD = 64
WINDOW = 64
CHUNK = 2 * WINDOW
FEATS = 2 * HD
AUG = HD + 16
F32 = jnp.float32
BF16 = jnp.bfloat16


def mm(left, right, left_dim=1, right_dim=0):
    return lax.dot_general(
        left, right, (((left_dim,), (right_dim,)), ((), ())), preferred_element_type=F32
    )


def chunk_masks(chunk, seg_row, seg_own, seg_prev):
    place = lax.broadcasted_iota(jnp.int32, (CHUNK, CHUNK), 1)
    key = lax.broadcasted_iota(jnp.int32, (CHUNK, CHUNK), 0)
    same_own = seg_own == seg_row
    same_prev = (seg_prev - jnp.where(chunk == 0, 100, 0)) == seg_row
    far = -1e30
    bias_own = jnp.where(same_own & (key <= place) & (key > place - WINDOW), 0.0, far)
    bias_prev = jnp.where(same_prev & (key > place + WINDOW), 0.0, far)
    linear_prev = jnp.where(same_prev & (key <= place + WINDOW), 1.0, 0.0)
    linear_own = jnp.where(same_own & (key <= place - WINDOW), 1.0, 0.0)
    return bias_prev[WINDOW:], bias_own, linear_prev, linear_own[:WINDOW]


def with_ones(values):
    return jnp.concatenate([values, jnp.ones((AUG - HD, CHUNK), values.dtype)], axis=0)


def features_of(vectors, maps_t):
    logits = mm(maps_t, vectors)
    high = jnp.exp(logits - jnp.max(logits, axis=0, keepdims=True))
    low = jnp.exp(jnp.min(logits, axis=0, keepdims=True) - logits)
    high = high * (1.0 / jnp.sum(high, axis=0, keepdims=True))
    low = low * (1.0 / jnp.sum(low, axis=0, keepdims=True))
    return jnp.concatenate([high, low], axis=0)


def features_back(features, grad):
    product = features * grad
    high = product[:HD] - features[:HD] * jnp.sum(product[:HD], axis=0, keepdims=True)
    low = product[HD:] - features[HD:] * jnp.sum(product[HD:], axis=0, keepdims=True)
    return high - low


def forward_kernel(
    last_ref, order_ref, seg_row_ref, seg_own_ref, seg_prev_ref,
    q_ref, kt_ref, k_ref, kp_ref, vt_ref, vtp_ref, maps_t_ref,
    mixed_ref, peak_ref, den_ref, fq_ref, fkt_ref, fk_ref, state_out_ref,
    state_ref, fk_prev_ref,
):
    chunk = pl.program_id(0)
    head_count = fq_ref.shape[0]
    per_key = head_count // k_ref.shape[0]

    @pl.when(chunk == 0)
    def _():
        state_ref[...] = jnp.zeros_like(state_ref)
        fk_prev_ref[...] = jnp.zeros_like(fk_prev_ref)

    seg_row = seg_row_ref[...]
    bias_prev, bias_own, linear_prev, linear_own = chunk_masks(
        chunk, seg_row, seg_own_ref[...], seg_prev_ref[...]
    )
    tag_state = jnp.where(chunk >= 2, last_ref[jnp.maximum(chunk - 2, 0)], -1)
    tag_prev = jnp.where(chunk >= 1, last_ref[jnp.maximum(chunk - 1, 0)], -2)
    carried = jnp.where(seg_row == tag_state, 1.0, 0.0)
    joined = jnp.where(tag_state == tag_prev, 1.0, 0.0)
    keep_prev = jnp.where(seg_prev_ref[...] == tag_prev, 1.0, 0.0).astype(BF16)
    for head in range(head_count):
        group = head // per_key
        rows = slice(head * HD, (head + 1) * HD)
        key_rows = slice(group * HD, (group + 1) * HD)
        query = q_ref[rows, :]
        maps_t = maps_t_ref[head]
        feat_q = features_of(query, maps_t)
        feat_kt = features_of(kt_ref[key_rows, :], maps_t)
        fq_ref[head] = feat_q.astype(BF16)
        fkt_ref[head] = feat_kt.astype(BF16)
        feat_k = jnp.transpose(feat_kt).astype(BF16)
        fk_ref[head] = feat_k
        scaled = query * jnp.asarray(HD**-0.5, BF16)
        score_prev = mm(kp_ref[group, WINDOW:, :], scaled) + bias_prev
        score_own = mm(k_ref[group], scaled) + bias_own
        peak = jnp.maximum(
            jnp.max(score_prev, axis=0, keepdims=True), jnp.max(score_own, axis=0, keepdims=True)
        )
        weight_prev = jnp.exp(score_prev - peak)
        weight_own = jnp.exp(score_own - peak)
        damped = feat_q * jnp.exp(-peak)
        damped_low = damped.astype(BF16)
        fk_prev = fk_prev_ref[head]
        lin_prev = mm(fk_prev, damped_low) * linear_prev
        lin_own = mm(feat_k[:WINDOW], damped_low) * linear_own
        all_prev = jnp.concatenate([lin_prev[:WINDOW], lin_prev[WINDOW:] + weight_prev], axis=0)
        all_own = jnp.concatenate([lin_own + weight_own[:WINDOW], weight_own[WINDOW:]], axis=0)
        value_prev = with_ones(vtp_ref[key_rows, :])
        state = state_ref[head]
        state_low = state.astype(BF16)
        state_out_ref[0, head] = state_low
        total = (
            mm(value_prev, all_prev.astype(BF16))
            + mm(with_ones(vt_ref[key_rows, :]), all_own.astype(BF16))
            + mm(state_low, (damped * carried).astype(BF16))
        )
        den = total[HD : HD + 1]
        mixed_ref[rows, :] = (total[:HD] * (1.0 / den)).astype(BF16)
        peak_ref[head : head + 1, :] = peak
        den_ref[head : head + 1, :] = den
        state_ref[head] = state * joined + mm(value_prev, fk_prev * keep_prev)
        fk_prev_ref[head] = feat_k


def backward_kernel(
    last_ref, order_ref, seg_row_ref, seg_own_ref, seg_prev_ref,
    q_ref, kt_ref, ktp_ref, k_ref, kp_ref, v_ref, vp_ref, vtp_ref, maps_ref, lift_ref,
    mixed_ref, grad_ref, peak_ref, den_ref, fq_ref, fkt_ref, fktp_ref, fk_ref, fkp_ref, state_ref,
    grows_ref, gmaps_ref,
    gstate_ref, cphi_ref, ck_ref, cv_ref,
):
    step = pl.program_id(0)
    chunk = pl.num_programs(0) - 1 - step
    head_count = fq_ref.shape[0]
    group_count = k_ref.shape[0]
    per_key = head_count // group_count

    @pl.when(step == 0)
    def _():
        gstate_ref[...] = jnp.zeros_like(gstate_ref)
        cphi_ref[...] = jnp.zeros_like(cphi_ref)
        ck_ref[...] = jnp.zeros_like(ck_ref)
        cv_ref[...] = jnp.zeros_like(cv_ref)
        gmaps_ref[...] = jnp.zeros_like(gmaps_ref)

    seg_row = seg_row_ref[...]
    bias_prev, bias_own, linear_prev, linear_own = chunk_masks(
        chunk, seg_row, seg_own_ref[...], seg_prev_ref[...]
    )
    tag_state = jnp.where(chunk >= 2, last_ref[jnp.maximum(chunk - 2, 0)], -1)
    tag_prev = jnp.where(chunk >= 1, last_ref[jnp.maximum(chunk - 1, 0)], -2)
    carried = jnp.where(seg_row == tag_state, 1.0, 0.0)
    joined = jnp.where(tag_state == tag_prev, 1.0, 0.0)
    keep_col = jnp.where(seg_prev_ref[...] == tag_prev, 1.0, 0.0)
    keep_prev = jnp.transpose(jnp.broadcast_to(keep_col, (CHUNK, CHUNK)))[:1]
    scale = HD**-0.5
    none = jnp.zeros((WINDOW, CHUNK), F32)
    for group in range(group_count):
        key_rows = slice(group * HD, (group + 1) * HD)
        key_t = kt_ref[key_rows, :]
        value_prev = with_ones(vtp_ref[key_rows, :])
        own_k = ck_ref[group]
        own_v = cv_ref[group]
        next_k = None
        next_v = None
        for head in range(group * per_key, (group + 1) * per_key):
            rows = slice(head * HD, (head + 1) * HD)
            query = q_ref[rows, :]
            scaled = query * jnp.asarray(scale, BF16)
            peak = peak_ref[head : head + 1, :]
            den = den_ref[head : head + 1, :]
            weight_prev = jnp.exp(mm(kp_ref[group, WINDOW:, :], scaled) + bias_prev - peak)
            weight_own = jnp.exp(mm(k_ref[group], scaled) + bias_own - peak)
            damp = jnp.exp(-peak)
            feat_q = fq_ref[head].astype(F32)
            damped = feat_q * damp
            damped_low = damped.astype(BF16)
            carried_low = (damped * carried).astype(BF16)
            lin_prev = mm(fkp_ref[head], damped_low) * linear_prev
            lin_own = mm(fk_ref[head, :WINDOW, :], damped_low) * linear_own
            all_prev = jnp.concatenate([lin_prev[:WINDOW], lin_prev[WINDOW:] + weight_prev], axis=0)
            all_own = jnp.concatenate([lin_own + weight_own[:WINDOW], weight_own[WINDOW:]], axis=0)
            grad = grad_ref[rows, :].astype(F32)
            dnum = grad * (1.0 / den)
            dden = -jnp.sum(dnum * mixed_ref[rows, :].astype(F32), axis=0, keepdims=True)
            dnum_low = dnum.astype(BF16)
            dtotal = jnp.concatenate(
                [dnum, dden, jnp.zeros((AUG - HD - 1, CHUNK), F32)], axis=0
            ).astype(BF16)
            dall_prev = mm(vp_ref[group], dnum_low) + dden
            dall_own = mm(v_ref[group], dnum_low) + dden
            dscore_prev = jnp.concatenate([none, weight_prev * dall_prev[WINDOW:]], axis=0).astype(BF16)
            dscore_own = (weight_own * dall_own).astype(BF16)
            dlin_prev = (linear_prev * dall_prev).astype(BF16)
            dlin_own = jnp.concatenate([linear_own * dall_own[:WINDOW], none], axis=0).astype(BF16)
            gstate = gstate_ref[head]
            gstate_low = gstate.astype(BF16)
            ddamped = (
                mm(fktp_ref[head], dlin_prev)
                + mm(fkt_ref[head], dlin_own)
                + carried * mm(state_ref[0, head], dtotal, 0, 0)
            )
            dlogit_q = features_back(feat_q, ddamped * damp).astype(BF16)
            maps = maps_ref[head]
            grad_q = (
                mm(ktp_ref[key_rows, :], dscore_prev) + mm(key_t, dscore_own)
            ) * scale + mm(maps, dlogit_q)
            grows_ref[rows, :] = grad_q.astype(BF16)
            dphi_own = cphi_ref[head] + mm(damped_low, dlin_own, 1, 1)
            cphi_ref[head] = (
                mm(damped_low, dlin_prev, 1, 1) + mm(gstate_low, value_prev, 0, 0) * keep_prev
            )
            dlogit_k = features_back(fkt_ref[head].astype(F32), dphi_own).astype(BF16)
            gmaps_ref[head] += mm(dlogit_q, query, 1, 1) + mm(dlogit_k, key_t, 1, 1)
            own_k += mm(scaled, dscore_own, 1, 1) + mm(maps, dlogit_k)
            part_k = mm(scaled, dscore_prev, 1, 1)
            own_v += mm(dnum_low, all_own.astype(BF16), 1, 1)
            part_v = (
                mm(dnum_low, all_prev.astype(BF16), 1, 1)
                + mm(gstate_low[:HD], fktp_ref[head]) * keep_prev
            )
            next_k = part_k if next_k is None else next_k + part_k
            next_v = part_v if next_v is None else next_v + part_v
            gstate_ref[head] = gstate * joined + mm(dtotal, carried_low, 1, 1)
        key_start = (head_count + group) * HD
        value_start = (head_count + group_count + group) * HD
        grows_ref[key_start : key_start + HD, :] = own_k.astype(BF16)
        grows_ref[value_start : value_start + HD, :] = own_v.astype(BF16)
        ck_ref[group] = next_k
        cv_ref[group] = next_v
    width = lift_ref.shape[1]
    grows_ref[width:, :] = mm(lift_ref[...], grows_ref[:width, :]).astype(BF16)


def attend_forward(last, order, seg_row, seg_col, rows, natural, maps_t):
    heads = maps_t.shape[0]
    groups, length = natural.shape[0] // 2, natural.shape[1]
    chunks = length // CHUNK
    first = heads // groups

    def before(c):
        return jnp.maximum(c - 1, 0)

    def spec(count, block, shift):
        return pl.BlockSpec((count * HD, CHUNK), lambda c, last, order: (block, order[shift(c)]))

    def nat(block, shift):
        return pl.BlockSpec((groups, CHUNK, HD), lambda c, last, order: (block, order[shift(c)], 0))

    def here(c):
        return c

    stat = pl.BlockSpec((heads, CHUNK), lambda c, last, order: (0, c))
    feat_t = pl.BlockSpec((heads, FEATS, CHUNK), lambda c, last, order: (0, 0, c))
    return pl.pallas_call(
        forward_kernel,
        grid_spec=pltpu.PrefetchScalarGridSpec(
            num_scalar_prefetch=2,
            grid=(chunks,),
            in_specs=[
                pl.BlockSpec((1, CHUNK), lambda c, last, order: (0, c)),
                pl.BlockSpec((CHUNK, 1), lambda c, last, order: (c, 0)),
                pl.BlockSpec((CHUNK, 1), lambda c, last, order: (before(c), 0)),
                spec(heads, 0, here),
                spec(groups, first, here),
                nat(0, here),
                nat(0, before),
                spec(groups, first + 1, here),
                spec(groups, first + 1, before),
                pl.BlockSpec((heads, HD, HD), lambda c, last, order: (0, 0, 0)),
            ],
            out_specs=[
                spec(heads, 0, here), stat, stat,
                feat_t, feat_t,
                pl.BlockSpec((heads, CHUNK, FEATS), lambda c, last, order: (0, c, 0)),
                pl.BlockSpec((1, heads, AUG, FEATS), lambda c, last, order: (c, 0, 0, 0)),
            ],
            scratch_shapes=[
                pltpu.VMEM((heads, AUG, FEATS), F32),
                pltpu.VMEM((heads, CHUNK, FEATS), BF16),
            ],
        ),
        out_shape=[
            jax.ShapeDtypeStruct((heads * HD, length), BF16),
            jax.ShapeDtypeStruct((heads, length), F32),
            jax.ShapeDtypeStruct((heads, length), F32),
            jax.ShapeDtypeStruct((heads, FEATS, length), BF16),
            jax.ShapeDtypeStruct((heads, FEATS, length), BF16),
            jax.ShapeDtypeStruct((heads, length, FEATS), BF16),
            jax.ShapeDtypeStruct((chunks, heads, AUG, FEATS), BF16),
        ],
        compiler_params=pltpu.CompilerParams(
            dimension_semantics=("arbitrary",), vmem_limit_bytes=32 * 2**20
        ),
        cost_estimate=pl.CostEstimate(
            flops=heads * length * 3600000, bytes_accessed=heads * length * 1600, transcendentals=0
        ),
        name="attend_forward",
    )(last, order, seg_row, seg_col, seg_col, rows, rows, natural, natural, rows, rows, maps_t)


def attend_backward(last, order, seg_row, seg_col, rows, natural, maps, lift, saved, grad):
    mixed, peak, den, fq, fkt, fk, states = saved
    heads = maps.shape[0]
    groups, length = natural.shape[0] // 2, natural.shape[1]
    chunks = length // CHUNK
    first = heads // groups
    height = lift.shape[0] + lift.shape[1]

    def here(s):
        return chunks - 1 - s

    def before(s):
        return jnp.maximum(chunks - 2 - s, 0)

    def spec(count, block, shift):
        return pl.BlockSpec((count * HD, CHUNK), lambda s, last, order: (block, order[shift(s)]))

    def nat(block, shift):
        return pl.BlockSpec((groups, CHUNK, HD), lambda s, last, order: (block, order[shift(s)], 0))

    def feat_t(shift):
        return pl.BlockSpec((heads, FEATS, CHUNK), lambda s, last, order: (0, 0, shift(s)))

    def feat(shift):
        return pl.BlockSpec((heads, CHUNK, FEATS), lambda s, last, order: (0, shift(s), 0))

    stat = pl.BlockSpec((heads, CHUNK), lambda s, last, order: (0, here(s)))
    whole = pl.BlockSpec((heads, HD, HD), lambda s, last, order: (0, 0, 0))
    return pl.pallas_call(
        backward_kernel,
        grid_spec=pltpu.PrefetchScalarGridSpec(
            num_scalar_prefetch=2,
            grid=(chunks,),
            in_specs=[
                pl.BlockSpec((1, CHUNK), lambda s, last, order: (0, here(s))),
                pl.BlockSpec((CHUNK, 1), lambda s, last, order: (here(s), 0)),
                pl.BlockSpec((CHUNK, 1), lambda s, last, order: (before(s), 0)),
                spec(heads, 0, here),
                spec(groups, first, here), spec(groups, first, before),
                nat(0, here), nat(0, before),
                nat(1, here), nat(1, before),
                spec(groups, first + 1, before),
                whole,
                pl.BlockSpec(lift.shape, lambda s, last, order: (0, 0)),
                spec(heads, 0, here), spec(heads, 0, here), stat, stat,
                feat_t(here), feat_t(here), feat_t(before), feat(here), feat(before),
                pl.BlockSpec((1, heads, AUG, FEATS), lambda s, last, order: (here(s), 0, 0, 0)),
            ],
            out_specs=[
                pl.BlockSpec((height, CHUNK), lambda s, last, order: (0, order[here(s)])),
                whole,
            ],
            scratch_shapes=[
                pltpu.VMEM((heads, AUG, FEATS), F32),
                pltpu.VMEM((heads, FEATS, CHUNK), F32),
                pltpu.VMEM((groups, HD, CHUNK), F32),
                pltpu.VMEM((groups, HD, CHUNK), F32),
            ],
        ),
        out_shape=[
            jax.ShapeDtypeStruct((height, length), BF16),
            jax.ShapeDtypeStruct((heads, HD, HD), F32),
        ],
        compiler_params=pltpu.CompilerParams(
            dimension_semantics=("arbitrary",), vmem_limit_bytes=32 * 2**20
        ),
        cost_estimate=pl.CostEstimate(
            flops=heads * length * 7200000, bytes_accessed=heads * length * 2400, transcendentals=0
        ),
        name="attend_backward",
    )(
        last, order, seg_row, seg_col, seg_col, rows, rows, rows, natural, natural, natural, natural,
        rows, maps, lift, mixed, grad, peak, den, fq, fkt, fkt, fk, fk, states,
    )


ALL = ("rows", "heads", "seq")
SWAP = [(0, 1), (1, 0)]
LOWS = 32


def over_x(value):
    return lax.ppermute(value, "rows", SWAP)


def over_c(value):
    return lax.ppermute(value, "seq", SWAP)


def after(value, *others):
    return lax.optimization_barrier((value, others))[0]


def body(
    inputs,
    segment_ids,
    cotangent,
    attn_gain,
    ffn_gain,
    query_weight,
    key_weight,
    value_weight,
    output_weight,
    query_down,
    query_lift,
    key_down,
    key_lift,
    value_down,
    value_lift,
    output_down,
    output_lift,
    feature_maps,
    gate_weight,
    up_weight,
    down_weight,
):
    heads_size = lax.axis_size("heads")
    depth = inputs.shape[0]
    wide = heads_size // depth
    per = HEADS // heads_size
    near = depth // 2
    block_rows = per * HD
    rank = query_down.shape[1]
    width = inputs.shape[-1]
    half = width // 2
    share = inputs.shape[3]
    held = depth * share
    head_index = lax.axis_index("heads")
    x = lax.axis_index("rows")
    c = lax.axis_index("seq")
    z = head_index // wide
    y = head_index % wide
    kv_pick = y * per // (HEADS // KV)
    kv_depth = KV // depth

    def over_y(value, k):
        return lax.ppermute(
            value,
            "heads",
            [(a * wide + b, a * wide + (b ^ k)) for a in range(depth) for b in range(wide)],
        )

    def over_z(value, k=1):
        return lax.ppermute(
            value,
            "heads",
            [(a * wide + b, (a + k) % depth * wide + b) for a in range(depth) for b in range(wide)],
        )

    def trade_z(value):
        groups = [[a * wide + b for a in range(depth)] for b in range(wide)]
        return lax.all_to_all(
            value, "heads", split_axis=0, concat_axis=0, tiled=True, axis_index_groups=groups
        )

    def trade_c(value, split, concat):
        return lax.all_to_all(value, "seq", split_axis=split, concat_axis=concat, tiled=True)

    def turn(value, axis):
        return jnp.stack(
            [lax.dynamic_index_in_dim(value, (z - j) % depth, axis, False) for j in range(depth)],
            axis,
        )

    def in_order(kept, moved, axis):
        return jnp.where(
            c == 0,
            jnp.concatenate([kept, moved], axis=axis),
            jnp.concatenate([moved, kept], axis=axis),
        )

    def rotate(value):
        return jnp.where(
            x == 1, jnp.concatenate([value[..., half:], value[..., :half]], axis=-1), value
        )

    def ring(block):
        blocks = [block]
        for _ in range(depth - 1):
            blocks.append(over_z(blocks[-1]))
        return blocks

    def shift_sum(blocks):
        total = blocks[0].astype(F32)
        for k in range(1, depth):
            total = total + over_z(blocks[depth - k], k).astype(F32)
        return total

    def shifts(block):
        return [block] + [over_z(block, k) for k in range(1, depth)]

    def ring_sum(blocks):
        total = blocks[1]
        for j in list(range(2, depth)) + [0]:
            moved = over_z(total)
            total = (moved.astype(F32) + blocks[j].astype(F32)).astype(
                F32 if j == 0 else blocks[1].dtype
            )
        return total

    def gather_tokens(value):
        chip = jnp.concatenate([value, over_c(value)], axis=0)
        others = []
        for k in range(1, wide):
            moved = over_y(value, k)
            others += [moved, over_c(moved)]
        return chip, jnp.concatenate(others, axis=0)

    def reduce_tokens(make_chip, make_others, waits=()):
        others = make_others()
        sent = []
        arrived = []
        for k in range(1, wide):
            start = (k - 1) * 2 * held
            mine = others[start : start + held]
            moved = over_c(others[start + held : start + 2 * held])
            sent.append((mine.astype(F32) + moved.astype(F32)).astype(BF16))
            arrived.append(over_y(sent[-1], k))
        chip = make_chip()
        total = chip[:held].astype(F32) + over_c(chip[held:]).astype(F32)
        if waits:
            arrived = [after(piece, *waits) for piece in arrived]
        for piece in arrived:
            total = total + piece.astype(F32)
        return total, sent

    def rms(values):
        return lax.rsqrt(jnp.mean(values * values, axis=-1, keepdims=True) + 1e-05)

    def norm_back(values, gain, scale, grad):
        unit = values * scale
        scaled = grad * gain
        return (
            scale * (scaled - unit * jnp.mean(scaled * unit, axis=-1, keepdims=True)),
            jnp.sum(grad * unit, axis=0),
        )

    small = (
        attn_gain, ffn_gain, query_down, key_down, value_down, output_lift,
        query_lift, key_lift, value_lift, output_down, feature_maps,
    )
    packed = jnp.concatenate([piece.reshape(-1) for piece in small])
    near_small = in_order(packed[None], over_c(packed)[None], 0)[None]
    step = 1
    while step < wide:
        moved = over_y(near_small, step)
        near_small = jnp.where(
            (y // step) % 2 == 0,
            jnp.concatenate([near_small, moved], axis=0),
            jnp.concatenate([moved, near_small], axis=0),
        )
        step *= 2
    layer_in = rotate(trade_z(after(inputs[:, 0, 0], near_small)).reshape(held, width)).astype(F32)
    near_small = turn(jnp.stack(shifts(near_small)), 0).reshape(heads_size, 2, -1)
    far_small = over_x(near_small)
    turned_small = jnp.stack([near_small, far_small])
    spread_small = jnp.where(x == 0, turned_small, jnp.stack([far_small, near_small]))
    starts = [0]
    for piece in small:
        starts.append(starts[-1] + piece.size)

    def piece(index, turned):
        source = turned_small if turned else spread_small
        return source[..., starts[index] : starts[index + 1]].reshape(
            (2, heads_size, 2) + small[index].shape
        )

    def pick_heads(value):
        value = value.reshape((depth, wide) + value.shape[1:])
        value = lax.dynamic_index_in_dim(value, y, 1, False)
        return lax.dynamic_slice_in_dim(value, c * near, near, 0)

    gain_one = piece(0, True).reshape(width).astype(F32)
    gain_two = piece(1, True).reshape(width).astype(F32)
    downs = [piece(i, True).reshape(width, rank) for i in (2, 3, 4)]
    downs_t = jnp.concatenate(downs + [jnp.zeros((width, LOWS - 3 * rank), BF16)], axis=1).T
    out_lift = jnp.moveaxis(piece(5, True), 3, 0).reshape(rank, width)
    query_raise = jnp.transpose(
        piece(6, False).reshape(2, heads_size, 2, -1, per, HD), (1, 4, 0, 2, 3, 5)
    ).reshape(heads_size, per, rank, HD)
    query_raise = jnp.moveaxis(pick_heads(query_raise), 2, 0).reshape(rank, -1)

    def pick_keys(value):
        value = value.reshape(value.shape[0], depth, kv_depth, HD)
        value = lax.dynamic_index_in_dim(value, kv_pick, 2, False)
        return lax.dynamic_slice_in_dim(value, c * near, near, 1).reshape(value.shape[0], -1)

    def pick_near(value):
        value = value.reshape(value.shape[0], depth, kv_depth, HD)
        value = lax.dynamic_index_in_dim(value, kv_pick, 2, False).reshape(value.shape[0], -1).T
        rows_near = near * HD
        kept = lax.dynamic_slice_in_dim(value, c * rows_near, rows_near, 0)
        return in_order(kept, over_c(lax.dynamic_slice_in_dim(value, (1 - c) * rows_near, rows_near, 0)), 1)

    key_raise = pick_keys(piece(7, False)[:, 0].reshape(rank, KV * HD))
    value_raise = pick_keys(piece(8, False)[:, 0].reshape(rank, KV * HD))
    out_down = jnp.transpose(
        piece(9, False).reshape(2, heads_size, 2, per, HD, -1), (1, 3, 4, 0, 2, 5)
    ).reshape(heads_size, per, HD, rank)
    out_down = pick_heads(out_down).reshape(-1, rank)
    maps = jnp.transpose(piece(10, False), (1, 3, 0, 2, 4, 5)).reshape(heads_size, per, HD, HD)
    maps = pick_heads(maps).reshape(-1, HD, HD)
    query_rows = near * block_rows
    key_rows = near * HD
    lift = jnp.concatenate(
        [
            jnp.pad(query_raise, ((0, 0), (0, 2 * key_rows))),
            jnp.pad(key_raise, ((0, 0), (query_rows, key_rows))),
            jnp.pad(value_raise, ((0, 0), (query_rows + key_rows, 0))),
            jnp.zeros((LOWS - 3 * rank, query_rows + 2 * key_rows), BF16),
        ],
        axis=0,
    )
    row_count = query_rows + 2 * key_rows

    def spread_heads(block):
        blocks = turn(jnp.stack(shifts(block)), 0)
        kept = lax.dynamic_slice_in_dim(blocks, c * near, near, 0)
        moved = over_c(lax.dynamic_slice_in_dim(blocks, (1 - c) * near, near, 0))
        return in_order(kept, moved, 2).reshape(near * block_rows, half)

    query_own = spread_heads(query_weight.T)
    kv_own = jnp.concatenate([pick_near(key_weight), pick_near(value_weight)], axis=0)
    both_own = jnp.concatenate([query_own, kv_own], axis=0)
    both = jnp.concatenate([both_own, over_x(both_own)], axis=1)
    project = jnp.concatenate([both, downs_t], axis=0)

    pack_one = jnp.stack([after(gate_weight, near_small).T, after(up_weight, near_small).T])
    own_one = [trade_c(pack_one, 1, 2)]
    own_two = [trade_c(after(down_weight, near_small), 0, 1)]
    other_one = [over_x(own_one[0])]
    other_two = [over_x(own_two[0])]
    project = after(project, other_one[0])

    def next_block(*waits):
        one, two = own_one[-1], own_two[-1]
        if waits:
            one, two = after(one, *waits), after(two, *waits)
        own_one.append(over_z(one))
        own_two.append(over_z(two))

    def next_half():
        place = len(other_one)
        other_one.append(over_x(own_one[place]))
        other_two.append(over_x(own_two[place]))

    next_block(layer_in)

    scale_one = rms(layer_in)
    normed = gather_tokens((layer_in * scale_one * gain_one).astype(BF16))

    def project_rows(tokens):
        flat = mm(project, tokens, 1, 1)
        low = flat[row_count:].astype(BF16)
        return (flat[:row_count] + mm(lift, low, 0, 0)).astype(BF16), low

    pieces = [project_rows(tokens) for tokens in normed]
    rows = jnp.concatenate([piece_rows for piece_rows, _ in pieces], axis=1)
    low_rows = jnp.concatenate([low for _, low in pieces], axis=1)

    def flips(value, y_axis, c_axis):
        value = jnp.where(c == 1, jnp.flip(value, c_axis), value)
        step = 1
        while step < wide:
            shape = value.shape
            apart = value.reshape(
                shape[:y_axis] + (wide // (2 * step), 2, step) + shape[y_axis + 1 :]
            )
            value = jnp.where((y // step) % 2 == 1, jnp.flip(apart, y_axis + 1), apart).reshape(shape)
            step *= 2
        return value

    length = wide * 2 * held
    chunks = length // CHUNK
    if share % CHUNK == 0:
        across = share // CHUNK
        numbers = jnp.arange(chunks, dtype=jnp.int32).reshape(2, depth, wide, across)
        order = flips(
            jnp.arange(chunks, dtype=jnp.int32).reshape(wide, 2, depth, across), 0, 1
        )
        order = jnp.transpose(order, (1, 2, 0, 3)).reshape(-1)

        def to_natural(value):
            return value

        from_natural = to_natural
    else:
        order = jnp.arange(chunks, dtype=jnp.int32)

        def to_natural(value):
            apart = flips(value.reshape(-1, wide, 2, depth, share), 1, 2)
            return jnp.transpose(apart, (0, 2, 3, 1, 4)).reshape(value.shape)

        def from_natural(value):
            apart = jnp.transpose(value.reshape(-1, 2, depth, wide, share), (0, 3, 1, 2, 4))
            return flips(apart, 1, 2).reshape(value.shape)

    segment = lax.dynamic_index_in_dim(segment_ids[:, 0], z, 0, False)
    last = segment.reshape(chunks, CHUNK)[:, -1]
    seg_row = segment[None, :]
    seg_col = segment[:, None]
    rows_nat = to_natural(rows)
    key_nat = jnp.transpose(rows_nat[query_rows:].reshape(-1, HD, length), (0, 2, 1))
    key_nat = after(key_nat, own_one[1], own_two[1])
    next_block()
    next_half()
    saved = attend_forward(
        last, order, seg_row, seg_col, rows_nat, key_nat, jnp.transpose(maps, (0, 2, 1))
    )
    mixed = from_natural(saved[0])

    out_own = spread_heads(after(output_weight, rows))
    out_mat = jnp.concatenate([out_own, over_x(out_own)], axis=1)
    rank_rows = mm(out_down, mixed, 0, 0).astype(BF16)
    split = 2 * held

    def branch(part, *waits):
        def make():
            rows_in = after(mixed[:, part], *waits)
            return (mm(rows_in, out_mat, 0, 0) + mm(rank_rows[:, part], out_lift, 0, 0)).astype(BF16)

        return make

    chip_part, other_part = slice(0, split), slice(split, length)
    branch_sum, _ = reduce_tokens(
        branch(chip_part, own_one[2], own_two[2], other_one[1], other_two[1]), branch(other_part)
    )
    middle = layer_in + branch_sum
    next_block()
    next_half()
    next_half()

    scale_two = rms(middle)
    ffn_rows = gather_tokens((middle * scale_two * gain_two).astype(BF16))
    ffn_rows = (ffn_rows[0], after(ffn_rows[1], own_one[3], other_one[2]))
    grad_out = rotate(
        trade_z(after(cotangent[:, 0, 0], own_two[3])).reshape(held, width)
    )
    grads = gather_tokens(grad_out)
    own_gate, own_up = [jnp.concatenate([b[i] for b in own_one], axis=0) for i in range(2)]
    other_gate, other_up = [jnp.concatenate([b[i] for b in other_one], axis=0) for i in range(2)]
    own_down = jnp.concatenate(own_two, axis=0)
    other_down = jnp.concatenate(other_two, axis=0)

    def from_width(tokens, own, other):
        return mm(tokens[:, :half], own, 1, 1) + mm(tokens[:, half:], other, 1, 1)

    gates = [from_width(tokens, own_gate, other_gate).astype(BF16) for tokens in ffn_rows]
    ups = [from_width(tokens, own_up, other_up).astype(BF16) for tokens in ffn_rows]

    def activate(gate, up):
        gate = gate.astype(F32)
        return (gate * jax.nn.sigmoid(gate) * up.astype(F32)).astype(BF16)

    hidden = [activate(gate, up) for gate, up in zip(gates, ups)]

    def ffn_forward(part):
        return lambda: jnp.concatenate(
            [mm(hidden[part], own_down).astype(BF16), mm(hidden[part], other_down).astype(BF16)],
            axis=1,
        )

    ffn_out, ffn_sent = reduce_tokens(ffn_forward(0), ffn_forward(1))
    grads = (grads[0], after(grads[1], *ffn_sent))

    def over_tokens(left, right):
        total = mm(left[0], right[0], 0, 0)
        for a, b in zip(left[1:], right[1:]):
            total = total + mm(a, b, 0, 0)
        return total.astype(BF16)

    def send_other(left, right):
        return over_x(over_tokens(left, [b[:, half:] for b in right]))

    def keep_own(left, right):
        return over_tokens(left, [b[:, :half] for b in right])

    def add_up(kept, moved):
        kept = jnp.split(kept, depth, axis=0)
        moved = jnp.split(moved, depth, axis=0)
        return [(a.astype(F32) + b.astype(F32)).astype(BF16) for a, b in zip(kept, moved)]

    down_moved = send_other(hidden, grads)
    grad_gates, grad_ups = [], []
    for grad, gate, up in zip(grads, gates, ups):
        grad_hidden = from_width(grad, own_down, other_down)
        gate = gate.astype(F32)
        sigmoid = jax.nn.sigmoid(gate)
        grad_gates.append(
            (grad_hidden * up.astype(F32) * sigmoid * (1.0 + gate * (1.0 - sigmoid))).astype(BF16)
        )
        grad_ups.append((grad_hidden * gate * sigmoid).astype(BF16))

    def ffn_back(part):
        return lambda: jnp.concatenate(
            [
                (mm(grad_gates[part], a) + mm(grad_ups[part], b)).astype(BF16)
                for a, b in ((own_gate, own_up), (other_gate, other_up))
            ],
            axis=1,
        )

    grad_ffn, grad_ffn_sent = reduce_tokens(ffn_back(0), ffn_back(1))
    ffn_out = after(ffn_out, *grad_ffn_sent)
    output = trade_z(rotate((middle + ffn_out).astype(BF16)).reshape(depth, share, width))
    gate_moved = send_other(grad_gates, ffn_rows)
    up_moved = send_other(grad_ups, ffn_rows)

    grad_mid_norm, gain_two_grad = norm_back(middle, gain_two, scale_two, grad_ffn)
    grad_middle = grad_out.astype(F32) + grad_mid_norm

    down_kept = keep_own(hidden, grads)
    gate_kept = keep_own(grad_gates, ffn_rows)
    up_kept = keep_own(grad_ups, ffn_rows)

    grad_branch = jnp.concatenate(gather_tokens(grad_middle.astype(BF16)), axis=0)
    grad_olow = mm(out_lift, grad_branch, 1, 1).astype(BF16)
    grad_mixed = (mm(out_mat, grad_branch, 1, 1) + mm(out_down, grad_olow)).astype(BF16)
    down_sums = add_up(down_kept, after(down_moved, grad_middle))
    down_step = after(over_z(down_sums[1]), grad_branch)
    down_step = (down_step.astype(F32) + down_sums[2].astype(F32)).astype(BF16)
    down_step = over_z(down_step)
    gate_sums = add_up(gate_kept, after(gate_moved, grad_branch))
    out_lift_grad = mm(rank_rows, grad_branch)
    out_down_grad = mm(mixed, grad_olow, 1, 1)
    out_weight_grad = mm(mixed, grad_branch).astype(BF16)

    grad_mixed = after(grad_mixed, gate_sums[1:], output)
    gate_shifted = [over_z(gate_sums[depth - k], k) for k in range(1, depth)]
    grad_rows, maps_grad = attend_backward(
        last, order, seg_row, seg_col, rows_nat, key_nat, maps, lift, saved, to_natural(grad_mixed)
    )
    grad_rows = after(from_natural(grad_rows), down_step, gate_shifted)

    def project_back(part):
        return lambda: mm(grad_rows[:, part], project, 0, 0).astype(BF16)

    grad_normed, normed_sent = reduce_tokens(project_back(chip_part), project_back(other_part))

    late_rows = after(grad_rows, *normed_sent)
    project_grad = [
        mm(late_rows[:, chip_part], normed[0][:, cut]) + mm(late_rows[:, other_part], normed[1][:, cut])
        for cut in (slice(0, half), slice(half, width))
    ]
    lift_grad = mm(low_rows, late_rows[:row_count], 1, 1)[: 3 * rank].reshape(3, rank, row_count)
    column = lax.broadcasted_iota(jnp.int32, (3, 1, row_count), 2)
    owner_of = (column >= query_rows).astype(jnp.int32) + (column >= query_rows + key_rows)
    kind = lax.broadcasted_iota(jnp.int32, (3, 1, row_count), 0)
    lift_grad = jnp.sum(jnp.where(owner_of == kind, lift_grad, 0.0), axis=0).T

    def halves(value):
        middle_at = value.shape[-1] // 2
        first, second = value[..., :middle_at], value[..., middle_at:]
        return jnp.where(x == 0, first, second), jnp.where(x == 0, second, first)

    quarter = half // 2
    rank_own = rank // 4
    maps_own = HD // 4

    def part_of(value, place):
        sizes = (quarter, rank_own, maps_own)
        start = 0
        parts = []
        for size in sizes:
            if start < value.shape[1]:
                parts.append(lax.dynamic_slice_in_dim(value, start + place * size, size, 1))
            start += 2 * size
        return jnp.concatenate(parts, axis=1).astype(BF16)

    def by_depth(value, height):
        return value.reshape(near, height, value.shape[-1])

    def collect(own_half, other_half, blocks):
        summed = own_half.astype(F32) + over_x(other_half.astype(BF16)).astype(F32)

        def ready(place):
            return blocks(part_of(summed, place))

        return shift_sum(list(turn(in_order(ready(c), over_c(ready(1 - c)), 0), 0)))

    down_lift = halves(out_down_grad)
    out_sum = collect(
        *[
            jnp.concatenate([out_weight_grad[:, i * half : (i + 1) * half], down_lift[i]], axis=1)
            for i in range(2)
        ],
        lambda value: by_depth(value, block_rows),
    )
    out_grad = out_sum[:, :quarter]
    output_down_grad = out_sum[:, quarter : quarter + rank_own]

    lift_halves = halves(lift_grad)
    maps_halves = halves(
        jnp.concatenate(
            [maps_grad.reshape(query_rows, HD), jnp.zeros((2 * key_rows, HD), F32)], axis=0
        )
    )
    late_sum = collect(
        *[
            jnp.concatenate([project_grad[i][:row_count], lift_halves[i], maps_halves[i]], axis=1)
            for i in range(2)
        ],
        lambda value: jnp.concatenate(
            [
                by_depth(value[:query_rows], block_rows),
                by_depth(value[query_rows : query_rows + key_rows], HD),
                by_depth(value[query_rows + key_rows :], HD),
            ],
            axis=1,
        ),
    )
    query_grad = late_sum[:block_rows, :quarter].T
    query_lift_grad = late_sum[:block_rows, quarter : quarter + rank_own].T
    feature_maps_grad = jnp.transpose(
        late_sum[:block_rows, quarter + rank_own :].reshape(per, HD, maps_own), (0, 2, 1)
    )
    kv_sum = late_sum[block_rows:, : quarter + rank_own].reshape(2, HD, quarter + rank_own)
    kv_sum = jnp.where(
        lax.broadcasted_iota(jnp.int32, (kv_depth, 1, 1, 1), 0) == kv_pick, kv_sum[None], 0.0
    ).astype(BF16)
    step = 1
    while step < wide:
        kv_sum = (kv_sum.astype(F32) + over_y(kv_sum, step).astype(F32)).astype(BF16)
        step *= 2
    kv_sum = turn(jnp.stack(shifts(kv_sum)), 0)
    kv_sum = jnp.transpose(kv_sum, (2, 4, 0, 1, 3)).reshape(2, quarter + rank_own, KV * HD)
    kv_sum = kv_sum.astype(F32)

    gate_total = gate_sums[0].astype(F32)
    for block in gate_shifted:
        gate_total = gate_total + block.astype(F32)
    down_step = (down_step.astype(F32) + down_sums[3].astype(F32)).astype(BF16)
    down_total = over_z(down_step).astype(F32) + down_sums[0].astype(F32)
    up_total = ring_sum(add_up(up_kept, after(up_moved, *normed_sent)))

    def to_owner(total):
        return trade_c(total.astype(BF16), 1, 0)

    down_grad = to_owner(down_total).astype(F32)
    gate_grad = to_owner(gate_total).T.astype(F32)
    up_grad = to_owner(up_total).T.astype(F32)

    grad_in_norm, gain_one_grad = norm_back(layer_in, gain_one, scale_one, grad_normed)
    input_grad = trade_z(
        rotate((grad_middle + grad_in_norm).astype(BF16)).reshape(depth, share, width)
    ).astype(F32)

    minor = jnp.concatenate(
        [
            gain_one_grad[None],
            gain_two_grad[None],
            jnp.concatenate([part[row_count : row_count + 3 * rank] for part in project_grad], axis=1),
            out_lift_grad,
        ],
        axis=0,
    )
    minor = minor[:, :half] + over_x(minor[:, half:])
    minor = jnp.moveaxis(minor.reshape(-1, depth, wide, 2, half // (2 * heads_size)), 0, 3)
    minor = shift_sum(list(turn(minor, 0)))
    total = lax.dynamic_index_in_dim(minor, y, 0, False)
    for k in range(1, wide):
        total = total + over_y(lax.dynamic_index_in_dim(minor, y ^ k, 0, False), k)
    minor = lax.dynamic_index_in_dim(total, c, 0, False) + over_c(
        lax.dynamic_index_in_dim(total, 1 - c, 0, False)
    )
    minor = minor.T
    return (
        output[:, None, None],
        input_grad[:, None, None],
        minor[:, 0],
        minor[:, 1],
        query_grad,
        kv_sum[0, :quarter],
        kv_sum[1, :quarter],
        out_grad,
        minor[:, 2 : 2 + rank],
        query_lift_grad,
        minor[:, 2 + rank : 2 + 2 * rank],
        kv_sum[0, quarter:],
        minor[:, 2 + 2 * rank : 2 + 3 * rank],
        kv_sum[1, quarter:],
        output_down_grad,
        minor[:, 2 + 3 * rank :].T,
        feature_maps_grad,
        gate_grad,
        up_grad,
        down_grad,
    )


def solution(mesh):
    placed = (
        P(None, "rows", "seq", "heads", None),
        P(None, "rows", None),
        P(None, "rows", "seq", "heads", None),
        P(("rows", "heads", "seq")),
        P(("rows", "heads", "seq")),
        P(("rows", "seq"), "heads"),
        P(("rows", "seq"), None),
        P(("rows", "seq"), None),
        P("heads", ("rows", "seq")),
        P(("rows", "heads", "seq"), None),
        P(("rows", "seq"), "heads"),
        P(("rows", "heads", "seq"), None),
        P(("rows", "seq"), None),
        P(("rows", "heads", "seq"), None),
        P(("rows", "seq"), None),
        P("heads", ("rows", "seq")),
        P(None, ("rows", "heads", "seq")),
        P("heads", ("rows", "seq"), None),
        P(("rows", "seq"), "heads"),
        P(("rows", "seq"), "heads"),
        P("heads", ("rows", "seq")),
    )
    return jax.shard_map(
        body,
        mesh=mesh,
        in_specs=placed,
        out_specs=(
            P(None, "rows", "seq", "heads", None),
            P(None, "rows", "seq", "heads", None),
            P(("rows", "heads", "seq")),
            P(("rows", "heads", "seq")),
            P(("rows", "seq"), "heads"),
            P(("rows", "seq"), None),
            P(("rows", "seq"), None),
            P("heads", ("rows", "seq")),
            P(("rows", "heads", "seq"), None),
            P(("rows", "seq"), "heads"),
            P(("rows", "heads", "seq"), None),
            P(("rows", "seq"), None),
            P(("rows", "heads", "seq"), None),
            P(("rows", "seq"), None),
            P("heads", ("rows", "seq")),
            P(None, ("rows", "heads", "seq")),
            P("heads", ("rows", "seq"), None),
            P(("rows", "seq"), "heads"),
            P(("rows", "seq"), "heads"),
            P("heads", ("rows", "seq")),
        ),
        check_vma=False,
    )
```

time: 7420 us -> 1490 us (0.20); the launches traced: 7340 us -> 1480 us
  waiting for transfers between devices: 3630 us -> 465 us
  local copies, waits for them, and re-layouts: 1540 us -> 199 us
  matrix products: 1130 us -> 380 us
  other arithmetic: 577 us -> 156 us
  blocking collectives: 349 us -> 14.5 us
  Pallas kernels: 0 us -> 145 us
  starting transfers between devices: 19.5 us -> 120 us
  between operations: 89.6 us -> 4.11 us
    reduce_scatter x48 -> x0, waiting for transfers between devices: 2240 us -> none  [the longest x8 1130 us: reduce_back(): return lax.psum_scatter(values, 'heads', scatter_dimension=1, tiled=True)]
    dot_general x284 -> x58, matrix products: 1130 us -> 380 us  [mm(): lax.dot_general(left, right, (((left_dim,), (right_dim,)), ((), ())), pre...]
    all_gather x23 -> x0, waiting for transfers between devices: 692 us -> none  [the longest x8 376 us: gather_back(): return lax.all_gather(values, 'heads', axis=1, tiled=True)]
    pad x279 -> x0, local copies, waits for them, and re-layouts: 622 us -> none  [the longest x136 361 us: window_attend(): states = link_states(initial, lax.associative_scan(link_states, ordered))]
    unnamed x82 -> x0, waiting for transfers between devices: 533 us -> none
    ppermute x8 -> x88, waiting for transfers between devices: 3.62 us -> 462 us  [the longest x36 256 us: over_z(): lax.ppermute(value, 'heads', [(a * wide + b, (a + k) % depth * wide + b)...]
    unnamed x2873 -> x395, local copies, waits for them, and re-layouts: 391 us -> 67.4 us
    all_gather x25 -> x0, blocking collectives: 222 us -> none  [the longest x1 41.3 us: body(): lax.all_gather(query_down, ('rows', 'heads', 'seq'), axis=0, tiled=True)]
where the time goes in v1:
time: 1490 us; the launch traced here: 1480 us
  waiting for transfers between devices  465 us (31%)
  matrix products  380 us (26%)
  local copies, waits for them, and re-layouts  199 us (13%)
  other arithmetic  156 us (10%)
  Pallas kernels  145 us (10%)
  starting transfers between devices  120 us (8%)
    dot_general x58, matrix products, mm(): lax.dot_general(left, right, (((left_dim,), (right_dim,)), ((), ())), pre...  380 us
    ppermute x36, waiting for transfers between devices, over_z(): lax.ppermute(value, 'heads', [(a * wide + b, (a + k) % depth * wide + b)...  256 us
    ppermute x17, waiting for transfers between devices, over_x(): return lax.ppermute(value, 'rows', SWAP)  113 us
    pallas_call x1, Pallas kernels, attend_backward(): pl.pallas_call(backward_kernel, grid_spec=pltpu.PrefetchScalarGridSpec(nu...  94.5 us
    ppermute x11, waiting for transfers between devices, over_y(): lax.ppermute(value, 'heads', [(a * wide + b, a * wide + (b ^ k)) for a in...  92.7 us
    unnamed x395, local copies, waits for them, and re-layouts  67.4 us
    pallas_call x1, Pallas kernels, attend_forward(): pl.pallas_call(forward_kernel, grid_spec=pltpu.PrefetchScalarGridSpec(num...  50.7 us
    ppermute x36, starting transfers between devices, over_z(): lax.ppermute(value, 'heads', [(a * wide + b, (a + k) % depth * wide + b)...  37.7 us
  transfers between devices with their start and end apart: 94, of which 33 were waited for; matrix products, arithmetic and copies ran while one was open for 46% of the time, Pallas kernels for 10%

profile of v1, /device:TPU:0, one launch (start us, length us, event | category | flops | bytes accessed | tf_op | source)
XLA Modules:
  0.0 1483.2 jit_solution(11039345605603445002)
XLA Ops:
  75.1 15.0 %collective-permute-done.4 = bf16[256,512]{1,0:T(8,128)(2,1)} collective-permute-done((bf16[256,512]{1,0:T(8,128)(2,1)}, bf16[256,512]{1,0:T(8,128)(2,1)}, u32[]{:S(2)}, u32[]{:S(2)}) %collective-permute-start.4) | collective-permute-done | bytes 262176 | tf_op jit(solution)/shard_map/ppermute | solution.py:448
  90.2 30.6 %collective-permute-done.3 = bf16[256,512]{1,0:T(8,128)(2,1)} collective-permute-done((bf16[256,512]{1,0:T(8,128)(2,1)}, bf16[256,512]{1,0:T(8,128)(2,1)}, u32[]{:S(2)}, u32[]{:S(2)}) %collective-permute-start.3) | collective-permute-done | bytes 262176 | tf_op jit(solution)/shard_map/ppermute | solution.py:448
  136.3 24.4 %collective-permute-done.18 = bf16[512,1024]{0,1:T(8,128)(2,1)} collective-permute-done((bf16[512,1024]{0,1:T(8,128)(2,1)}, bf16[512,1024]{0,1:T(8,128)(2,1)}, u32[]{:S(2)}, u32[]{:S(2)}) %collective-permute-start.18) | collective-permute-done | bytes 1048608 | tf_op jit(solution)/shard_map/ppermute | solution.py:448
  164.3 12.9 collective-permute-done.15
  177.3 10.1 pad_maximum_fusion.11
  223.5 42.2 %collective-permute-done.25 = bf16[256,512]{1,0:T(8,128)(2,1)} collective-permute-done((bf16[256,512]{1,0:T(8,128)(2,1)}, bf16[256,512]{1,0:T(8,128)(2,1)}, u32[]{:S(2)}, u32[]{:S(2)}) %collective-permute-start.25) | collective-permute-done | bytes 262176 | tf_op jit(solution)/shard_map/ppermute | solution.py:448
  267.2 15.4 %collective-permute-done.24 = bf16[256,512]{1,0:T(8,128)(2,1)} collective-permute-done((bf16[256,512]{1,0:T(8,128)(2,1)}, bf16[256,512]{1,0:T(8,128)(2,1)}, u32[]{:S(2)}, u32[]{:S(2)}) %collective-permute-start.24) | collective-permute-done | bytes 262176 | tf_op jit(solution)/shard_map/ppermute | solution.py:448
  306.8 50.7 %attend_forward.1 = (bf16[512,2048]{1,0:T(8,128)(2,1)S(1)}, f32[8,2048]{1,0:T(8,128)S(1)}, f32[8,2048]{1,0:T(8,128)S(1)}, bf16[8,128,2048]{2,1,0:T(8,128)(2,1)S(...) custom-call(s32[16]{0:T(128)S(1)} %slice_reduce_fusion.last_ref, ...), custom_call_target="tpu_custom_call" | custom-call | flops 58982400000 | bytes 26214400 | tf_op jit(solution)/shard_map/attend_forward/pallas_call | solution.py:258
  363.4 17.8 %collective-permute-done.27 = bf16[512,1024]{1,0:T(8,128)(2,1)} collective-permute-done((bf16[512,1024]{1,0:T(8,128)(2,1)S(1)}, bf16[512,1024]{1,0:T(8,128)(2,1)}, u32[]{:S(2)}, u32[]{:S(2)}) %collective-permute-start.27) | collective-permute-done | bytes 1048608 | tf_op jit(solution)/shard_map/ppermute | solution.py:387
  408.2 7.4 collective-permute-done.37
  417.1 20.9 %collective-permute-done.38 = bf16[512,1024]{0,1:T(8,128)(2,1)} collective-permute-done((bf16[512,1024]{0,1:T(8,128)(2,1)}, bf16[512,1024]{0,1:T(8,128)(2,1)}, u32[]{:S(2)}, u32[]{:S(2)}) %collective-permute-start.38) | collective-permute-done | bytes 1048608 | tf_op jit(solution)/shard_map/ppermute | solution.py:387
  463.8 18.3 %collective-permute-done.33 = bf16[2,512,1024]{1,2,0:T(8,128)(2,1)} collective-permute-done((bf16[2,512,1024]{1,2,0:T(8,128)(2,1)}, bf16[2,512,1024]{1,2,0:T(8,128)(2,1)}, u32[]{:S(2)}, u32[]{:S(2)}) %collective-permute-start.33) | collective-permute-done | bytes 2097184 | tf_op jit(solution)/shard_map/ppermute | solution.py:387
  486.7 19.8 %collective-permute-done.30 = bf16[512,2048]{1,0:T(8,128)(2,1)S(1)} collective-permute-done((bf16[512,2048]{1,0:T(8,128)(2,1)S(1)}, bf16[512,2048]{1,0:T(8,128)(2,1)S(1)}, u32[]{:S(2)}, u32[]{:S(2)}) %collective-permute-start.30) | collective-permute-done | bytes 2097184 | tf_op jit(solution)/shard_map/ppermute | solution.py:441
  511.9 10.7 fusion.122
  522.5 6.6 collective-permute-done.34
  529.3 11.8 convolution_add_fusion
  547.4 7.1 fusion.129
  554.5 7.2 fusion.126
  561.8 8.7 add_convert_fusion.9
  570.5 17.2 %fusion.3 = (bf16[1024,2048]{1,0:T(8,128)(2,1)}, bf16[1024,2048]{1,0:T(8,128)(2,1)}, bf16[1024,2048]{1,0:T(8,128)(2,1)}) fusion(f32[1024,2048]{1,0:T(8,128)} %convolution_add_fusion, bf16[1024,2048]{1,0:T(8,128)(2,1)} %add_convert_fusion.9, f32[1024,2048]{1,0:T(8,128)} %fusion.126, bf16[1024,1024]{1,0:T(8,128)(2,1)} %copy-done.78, ...), kind=kOutput, calls=%fused_computation.15 | convolution fusion | flops 4353687552 | bytes 39845888 | tf_op jit(solution)/shard_map/dot_general | solution.py:22
  587.7 10.2 fusion.124
  598.0 6.2 fusion.127
  604.2 6.6 add_convert_fusion.15
  610.8 7.2 add_convert_fusion.16
  622.4 7.1 fusion.144
  629.5 6.9 convolution_convert_fusion.7
  636.5 7.3 fusion.145
  643.8 6.7 convolution_convert_fusion.8
  653.5 7.1 fusion.68
  660.6 7.2 fusion.66
  667.8 8.9 add_convert_fusion.7
  676.7 11.9 fusion.4
  688.6 8.1 convolution_convert_fusion.5
  696.7 6.7 convolution_convert_fusion.6
  707.2 7.2 fusion.148
  714.4 7.1 fusion.149
  723.7 10.1 fusion.46
  733.8 14.1 fusion.7
  748.0 8.7 fusion.125
  763.5 7.8 add_convert_fusion.19
  771.3 6.4 add_convert_fusion.20
  779.9 9.8 add_convert_fusion.4
  791.2 9.5 fusion.41
  803.1 9.8 add_convert_fusion.2
  812.9 9.9 add_convert_fusion.5
  827.1 28.8 %collective-permute-done.49 = bf16[512,2048]{1,0:T(8,128)(2,1)S(1)} collective-permute-done((bf16[512,2048]{1,0:T(8,128)(2,1)S(1)}, bf16[512,2048]{1,0:T(8,128)(2,1)S(1)}, u32[]{:S(2)}, u32[]{:S(2)}) %collective-permute-start.49) | collective-permute-done | bytes 2097184 | tf_op jit(solution)/shard_map/ppermute | solution.py:441
  861.4 6.4 fusion.130
  868.3 8.7 add_convert_fusion.1
  882.9 10.8 fusion.44
  893.7 21.7 %collective-permute-done.51 = bf16[512,2048]{1,0:T(8,128)(2,1)} collective-permute-done((bf16[512,2048]{1,0:T(8,128)(2,1)}, bf16[512,2048]{1,0:T(8,128)(2,1)}, u32[]{:S(2)}, u32[]{:S(2)}) %collective-permute-start.51) | collective-permute-done | bytes 2097184 | tf_op jit(solution)/shard_map/ppermute | solution.py:441
  915.4 7.3 add_convert_fusion.3
  922.8 11.3 add_convert_fusion
  934.1 38.5 %collective-permute-done.54 = bf16[2048,1024]{0,1:T(8,128)(2,1)} collective-permute-done((bf16[2048,1024]{0,1:T(8,128)(2,1)}, bf16[2048,1024]{0,1:T(8,128)(2,1)}, u32[]{:S(2)}, u32[]{:S(2)}) %collective-permute-start.54) | collective-permute-done | bytes 4194336 | tf_op jit(solution)/shard_map/ppermute | solution.py:387
  994.9 7.3 add_convert_fusion.14.grad_ref
  1028.5 94.5 %attend_backward.1 = (bf16[800,2048]{1,0:T(8,128)(2,1)S(1)}, f32[8,64,64]{2,1,0:T(8,128)S(1)}) custom-call(s32[16]{0:T(128)S(1)} %slice_reduce_fusion.last_ref, s32[16]{0:T(128)S(1)} %reshape.552.order_ref, s32[1,2048]{1,0:T(1,128)S(1)} %fusion.210.seg_row_ref, s32[2048,1]{1,0:T(8,128)S(1)} %copy-done.9, s32[2048,1]{1,0:T(8,128)S(1)} %copy-done.9, ...), custom_call_target="tpu_custom_call" | custom-call | flops 117964800000 | bytes 39321600 | tf_op jit(solution)/shard_map/attend_backward/pallas_call | solution.py:333
  1127.6 6.3 convolution_convert_fusion
  1147.1 7.1 convolution_convert_fusion.1
  1180.0 14.2 collective-permute-done.82
  1198.5 12.9 collective-permute-done.81
  1268.9 14.7 collective-permute-done.84
  1344.9 11.9 collective-permute-done.86
  1363.7 21.8 %all-to-all-start.5 = ((bf16[4,128,2048]{2,1,0:T(8,128)(2,1)}), bf16[4,128,2048]{2,1,0:T(8,128)(2,1)}, u32[]{:S(2)}, u32[]{:S(2)}) async-start(bf16[4,128,2048]{2,1,0:T(8,128)(2,1)} %bitcast.84), calls=%async_computation.5 | async-start | bytes 4194304 | tf_op jit(solution)/shard_map/all_to_all | solution.py:456
  1386.7 20.2 %collective-permute-done.72 = bf16[384,530]{1,0:T(8,128)(2,1)} collective-permute-done((bf16[384,530]{1,0:T(8,128)(2,1)}, bf16[384,530]{1,0:T(8,128)(2,1)}, u32[]{:S(2)}, u32[]{:S(2)}) %collective-permute-start.72) | collective-permute-done | bytes 407072 | tf_op jit(solution)/shard_map/ppermute | solution.py:448
  1427.6 40.9 %collective-permute-done.76 = bf16[2,2,64,514]{3,2,0,1:T(8,128)(2,1)S(1)} collective-permute-done((bf16[2,2,64,514]{3,2,0,1:T(8,128)(2,1)S(1)}, bf16[2,2,64,514]{3,2,0,1:T(8,128)(2,1)S(1)}, u32[]{:S(2)}, u32[]{:S(2)}) %collective-permute-start.76) | collective-permute-done | bytes 263200 | tf_op jit(solution)/shard_map/ppermute | solution.py:448
  (829 shorter events, 530.8 us)
Async XLA Ops:
  45.7 78.5 %all-to-all-start = ((bf16[4,128,2048]{2,1,0:T(8,128)(2,1)}), bf16[4,128,2048]{2,1,0:T(8,128)(2,1)S(1)}, u32[]{:S(2)}, u32[]{:S(2)}) async-start(bf16[4,128,2048]{2,1,0:T(8,128)(2,1)} %bitcast.375), calls=%async_computation | async-start | bytes 4194304 | tf_op jit(solution)/shard_map/all_to_all | solution.py:456
  50.3 39.8 %collective-permute-start.4 = (bf16[256,512]{1,0:T(8,128)(2,1)}, bf16[256,512]{1,0:T(8,128)(2,1)}, u32[]{:S(2)}, u32[]{:S(2)}) collective-permute-start(bf16[256,512]{1,0:T(8,128)(2,1)} %bitcast.6), channel_id=1, source_target_pairs={{0,12},{2,14},{4,0},{6,2},{8,4},{10,6},{12,8},{14,10},{1,13},{3,15... | collective-permute-start | bytes 786440 | tf_op jit(solution)/shard_map/ppermute | solution.py:448
  54.1 66.7 %collective-permute-start.3 = (bf16[256,512]{1,0:T(8,128)(2,1)}, bf16[256,512]{1,0:T(8,128)(2,1)}, u32[]{:S(2)}, u32[]{:S(2)}) collective-permute-start(bf16[256,512]{1,0:T(8,128)(2,1)} %bitcast.6), channel_id=1, source_target_pairs={{0,8},{2,10},{4,12},{6,14},{8,0},{10,2},{12,4},{14,6},{1,9},{3,11}... | collective-permute-start | bytes 786440 | tf_op jit(solution)/shard_map/ppermute | solution.py:448
  54.1 66.7 %collective-permute-start.2 = (bf16[256,512]{1,0:T(8,128)(2,1)}, bf16[256,512]{1,0:T(8,128)(2,1)}, u32[]{:S(2)}, u32[]{:S(2)}) collective-permute-start(bf16[256,512]{1,0:T(8,128)(2,1)} %bitcast.6), channel_id=1, source_target_pairs={{0,4},{2,6},{4,8},{6,10},{8,12},{10,14},{12,0},{14,2},{1,5},{3,7},... | collective-permute-start | bytes 786440 | tf_op jit(solution)/shard_map/ppermute | solution.py:448
  71.2 52.2 %collective-permute-start.12 = (bf16[8,2,9344]{2,1,0:T(2,128)(2,1)S(1)}, bf16[8,2,9344]{2,1,0:T(2,128)(2,1)S(1)}, u32[]{:S(2)}, u32[]{:S(2)}) collective-permute-start(bf16[8,2,9344]{2,1,0:T(2,128)(2,1)S(1)} %bitcast.356), channel_id=1, source_target_pairs={{0,16},{16,0},{1,17},{17,1},{2,18},{18,2},{3,19},{19,3},{4,20},{20... | collective-permute-start | bytes 897032 | tf_op jit(solution)/shard_map/ppermute | solution.py:387
  73.7 113.7 %collective-permute-start.13 = (bf16[2,512,1024]{1,2,0:T(8,128)(2,1)}, bf16[2,512,1024]{1,2,0:T(8,128)(2,1)}, u32[]{:S(2)}, u32[]{:S(2)}) collective-permute-start(bf16[2,512,1024]{1,2,0:T(8,128)(2,1)} %bitcast.36), channel_id=1, source_target_pairs={{0,16},{16,0},{1,17},{17,1},{2,18},{18,2},{3,19},{19,3},{4,20},{20... | collective-permute-start | bytes 6291464 | tf_op jit(solution)/shard_map/ppermute | solution.py:387
  128.8 48.3 %collective-permute-start.15 = (bf16[512,2048]{1,0:T(8,128)(2,1)}, bf16[512,2048]{1,0:T(8,128)(2,1)}, u32[]{:S(2)}, u32[]{:S(2)}) collective-permute-start(bf16[512,2048]{1,0:T(8,128)(2,1)} %get-tuple-element.188), channel_id=1, source_target_pairs={{0,2},{2,0},{4,6},{6,4},{8,10},{10,8},{12,14},{14,12},{1,3},{3,1},... | collective-permute-start | bytes 6291464 | tf_op jit(solution)/shard_map/ppermute | solution.py:441
  133.0 55.8 %collective-permute-start.14 = (bf16[512,2048]{1,0:T(8,128)(2,1)}, bf16[512,2048]{1,0:T(8,128)(2,1)}, u32[]{:S(2)}, u32[]{:S(2)}) collective-permute-start(bf16[512,2048]{1,0:T(8,128)(2,1)} %get-tuple-element.188), channel_id=1, source_target_pairs={{0,1},{1,0},{2,3},{3,2},{4,5},{5,4},{6,7},{7,6},{8,9},{9,8},{10,11... | collective-permute-start | bytes 6291464 | tf_op jit(solution)/shard_map/ppermute | solution.py:391
  133.3 27.5 %collective-permute-start.18 = (bf16[512,1024]{0,1:T(8,128)(2,1)}, bf16[512,1024]{0,1:T(8,128)(2,1)}, u32[]{:S(2)}, u32[]{:S(2)}) collective-permute-start(bf16[512,1024]{0,1:T(8,128)(2,1)} %bitcast.48), channel_id=1, source_target_pairs={{0,4},{2,6},{4,8},{6,10},{8,12},{10,14},{12,0},{14,2},{1,5},{3,7},... | collective-permute-start | bytes 3145736 | tf_op jit(solution)/shard_map/ppermute | solution.py:448
  134.5 42.7 %collective-permute-start.8 = (bf16[768,1024]{1,0:T(8,128)(2,1)}, bf16[768,1024]{1,0:T(8,128)(2,1)}, u32[]{:S(2)}, u32[]{:S(2)}) collective-permute-start(bf16[768,1024]{1,0:T(8,128)(2,1)} %pad_maximum_fusion.20), channel_id=1, source_target_pairs={{0,16},{16,0},{1,17},{17,1},{2,18},{18,2},{3,19},{19,3},{4,20},{20... | collective-permute-start | bytes 4718600 | tf_op jit(solution)/shard_map/ppermute | solution.py:387
  187.4 102.1 %collective-permute-start.17 = (bf16[2,512,1024]{1,2,0:T(8,128)(2,1)}, bf16[2,512,1024]{1,2,0:T(8,128)(2,1)}, u32[]{:S(2)}, u32[]{:S(2)}) collective-permute-start(bf16[2,512,1024]{1,2,0:T(8,128)(2,1)} %bitcast.36), channel_id=1, source_target_pairs={{0,4},{2,6},{4,8},{6,10},{8,12},{10,14},{12,0},{14,2},{1,5},{3,7},... | collective-permute-start | bytes 6291464 | tf_op jit(solution)/shard_map/ppermute | solution.py:448
  187.6 101.9 %collective-permute-start.35 = (bf16[512,1024]{0,1:T(8,128)(2,1)}, bf16[512,1024]{0,1:T(8,128)(2,1)}, u32[]{:S(2)}, u32[]{:S(2)}) collective-permute-start(bf16[512,1024]{0,1:T(8,128)(2,1)} %collective-permute-done.20), channel_id=1, source_target_pairs={{0,4},{2,6},{4,8},{6,10},{8,12},{10,14},{12,0},{14,2},{1,5},{3,7},... | collective-permute-start | bytes 3145736 | tf_op jit(solution)/shard_map/ppermute | solution.py:448
  204.9 60.8 %collective-permute-start.25 = (bf16[256,512]{1,0:T(8,128)(2,1)}, bf16[256,512]{1,0:T(8,128)(2,1)}, u32[]{:S(2)}, u32[]{:S(2)}) collective-permute-start(bf16[256,512]{1,0:T(8,128)(2,1)} %param.29), channel_id=1, source_target_pairs={{0,12},{2,14},{4,0},{6,2},{8,4},{10,6},{12,8},{14,10},{1,13},{3,15... | collective-permute-start | bytes 786440 | tf_op jit(solution)/shard_map/ppermute | solution.py:448
  207.7 74.8 %collective-permute-start.24 = (bf16[256,512]{1,0:T(8,128)(2,1)}, bf16[256,512]{1,0:T(8,128)(2,1)}, u32[]{:S(2)}, u32[]{:S(2)}) collective-permute-start(bf16[256,512]{1,0:T(8,128)(2,1)} %param.29), channel_id=1, source_target_pairs={{0,8},{2,10},{4,12},{6,14},{8,0},{10,2},{12,4},{14,6},{1,9},{3,11}... | collective-permute-start | bytes 786440 | tf_op jit(solution)/shard_map/ppermute | solution.py:448
  208.2 74.3 %collective-permute-start.23 = (bf16[256,512]{1,0:T(8,128)(2,1)}, bf16[256,512]{1,0:T(8,128)(2,1)}, u32[]{:S(2)}, u32[]{:S(2)}) collective-permute-start(bf16[256,512]{1,0:T(8,128)(2,1)} %param.29), channel_id=1, source_target_pairs={{0,4},{2,6},{4,8},{6,10},{8,12},{10,14},{12,0},{14,2},{1,5},{3,7},... | collective-permute-start | bytes 786440 | tf_op jit(solution)/shard_map/ppermute | solution.py:448
  265.7 120.8 %collective-permute-start.36 = (bf16[512,1024]{0,1:T(8,128)(2,1)}, bf16[512,1024]{0,1:T(8,128)(2,1)}, u32[]{:S(2)}, u32[]{:S(2)}) collective-permute-start(bf16[512,1024]{0,1:T(8,128)(2,1)} %bitcast.48), channel_id=1, source_target_pairs={{0,16},{16,0},{1,17},{17,1},{2,18},{18,2},{3,19},{19,3},{4,20},{20... | collective-permute-start | bytes 3145736 | tf_op jit(solution)/shard_map/ppermute | solution.py:387
  288.0 102.8 %collective-permute-start.22 = (bf16[512,1024]{0,1:T(8,128)(2,1)}, bf16[512,1024]{0,1:T(8,128)(2,1)}, u32[]{:S(2)}, u32[]{:S(2)}) collective-permute-start(bf16[512,1024]{0,1:T(8,128)(2,1)} %collective-permute-done.18), channel_id=1, source_target_pairs={{0,16},{16,0},{1,17},{17,1},{2,18},{18,2},{3,19},{19,3},{4,20},{20... | collective-permute-start | bytes 3145736 | tf_op jit(solution)/shard_map/ppermute | solution.py:387
  289.5 101.8 %collective-permute-start.19 = (bf16[2,512,1024]{1,2,0:T(8,128)(2,1)}, bf16[2,512,1024]{1,2,0:T(8,128)(2,1)}, u32[]{:S(2)}, u32[]{:S(2)}) collective-permute-start(bf16[2,512,1024]{1,2,0:T(8,128)(2,1)} %collective-permute-done.17), channel_id=1, source_target_pairs={{0,4},{2,6},{4,8},{6,10},{8,12},{10,14},{12,0},{14,2},{1,5},{3,7},... | collective-permute-start | bytes 6291464 | tf_op jit(solution)/shard_map/ppermute | solution.py:448
  289.5 101.8 %collective-permute-start.21 = (bf16[2,512,1024]{1,2,0:T(8,128)(2,1)}, bf16[2,512,1024]{1,2,0:T(8,128)(2,1)}, u32[]{:S(2)}, u32[]{:S(2)}) collective-permute-start(bf16[2,512,1024]{1,2,0:T(8,128)(2,1)} %collective-permute-done.17), channel_id=1, source_target_pairs={{0,16},{16,0},{1,17},{17,1},{2,18},{18,2},{3,19},{19,3},{4,20},{20... | collective-permute-start | bytes 6291464 | tf_op jit(solution)/shard_map/ppermute | solution.py:387
  290.1 112.1 %all-to-all-start.3 = ((bf16[4,128,2048]{2,1,0:T(8,128)(2,1)}), bf16[4,128,2048]{2,1,0:T(8,128)(2,1)}, u32[]{:S(2)}, u32[]{:S(2)}) async-start(bf16[4,128,2048]{2,1,0:T(8,128)(2,1)} %bitcast.376), calls=%async_computation.3 | async-start | bytes 4194304 | tf_op jit(solution)/shard_map/all_to_all | solution.py:456
  302.4 78.8 %collective-permute-start.27 = (bf16[512,1024]{1,0:T(8,128)(2,1)S(1)}, bf16[512,1024]{1,0:T(8,128)(2,1)}, u32[]{:S(2)}, u32[]{:S(2)}) collective-permute-start(bf16[512,1024]{1,0:T(8,128)(2,1)S(1)} %maximum_select_fusion.8), channel_id=1, source_target_pairs={{0,16},{16,0},{1,17},{17,1},{2,18},{18,2},{3,19},{19,3},{4,20},{20... | collective-permute-start | bytes 3145736 | tf_op jit(solution)/shard_map/ppermute | solution.py:387
  390.8 47.3 %collective-permute-start.38 = (bf16[512,1024]{0,1:T(8,128)(2,1)}, bf16[512,1024]{0,1:T(8,128)(2,1)}, u32[]{:S(2)}, u32[]{:S(2)}) collective-permute-start(bf16[512,1024]{0,1:T(8,128)(2,1)} %collective-permute-done.35), channel_id=1, source_target_pairs={{0,16},{16,0},{1,17},{17,1},{2,18},{18,2},{3,19},{19,3},{4,20},{20... | collective-permute-start | bytes 3145736 | tf_op jit(solution)/shard_map/ppermute | solution.py:387
  391.3 67.0 %collective-permute-start.32 = (bf16[2,512,1024]{1,2,0:T(8,128)(2,1)}, bf16[2,512,1024]{1,2,0:T(8,128)(2,1)}, u32[]{:S(2)}, u32[]{:S(2)}) collective-permute-start(bf16[2,512,1024]{1,2,0:T(8,128)(2,1)} %collective-permute-done.19), channel_id=1, source_target_pairs={{0,4},{2,6},{4,8},{6,10},{8,12},{10,14},{12,0},{14,2},{1,5},{3,7},... | collective-permute-start | bytes 6291464 | tf_op jit(solution)/shard_map/ppermute | solution.py:448
  392.1 90.0 %collective-permute-start.33 = (bf16[2,512,1024]{1,2,0:T(8,128)(2,1)}, bf16[2,512,1024]{1,2,0:T(8,128)(2,1)}, u32[]{:S(2)}, u32[]{:S(2)}) collective-permute-start(bf16[2,512,1024]{1,2,0:T(8,128)(2,1)} %collective-permute-done.19), channel_id=1, source_target_pairs={{0,16},{16,0},{1,17},{17,1},{2,18},{18,2},{3,19},{19,3},{4,20},{20... | collective-permute-start | bytes 6291464 | tf_op jit(solution)/shard_map/ppermute | solution.py:387
  406.6 80.1 %collective-permute-start.28 = (bf16[512,2048]{1,0:T(8,128)(2,1)S(1)}, bf16[512,2048]{1,0:T(8,128)(2,1)S(1)}, u32[]{:S(2)}, u32[]{:S(2)}) collective-permute-start(bf16[512,2048]{1,0:T(8,128)(2,1)S(1)} %copy-done.76), channel_id=1, source_target_pairs={{0,1},{1,0},{2,3},{3,2},{4,5},{5,4},{6,7},{7,6},{8,9},{9,8},{10,11... | collective-permute-start | bytes 6291464 | tf_op jit(solution)/shard_map/ppermute | solution.py:391
  415.6 71.0 %collective-permute-start.44 = (bf16[512,2048]{1,0:T(8,128)(2,1)S(1)}, bf16[512,2048]{1,0:T(8,128)(2,1)S(1)}, u32[]{:S(2)}, u32[]{:S(2)}) collective-permute-start(bf16[512,2048]{1,0:T(8,128)(2,1)S(1)} %maximum_select_fusion.2), channel_id=1, source_target_pairs={{0,2},{2,0},{4,6},{6,4},{8,10},{10,8},{12,14},{14,12},{1,3},{3,1},... | collective-permute-start | bytes 6291464 | tf_op jit(solution)/shard_map/ppermute | solution.py:441
  438.1 68.4 %collective-permute-start.30 = (bf16[512,2048]{1,0:T(8,128)(2,1)S(1)}, bf16[512,2048]{1,0:T(8,128)(2,1)S(1)}, u32[]{:S(2)}, u32[]{:S(2)}) collective-permute-start(bf16[512,2048]{1,0:T(8,128)(2,1)S(1)} %add_convert_fusion.22), channel_id=1, source_target_pairs={{0,2},{2,0},{4,6},{6,4},{8,10},{10,8},{12,14},{14,12},{1,3},{3,1},... | collective-permute-start | bytes 6291464 | tf_op jit(solution)/shard_map/ppermute | solution.py:441
  458.3 53.6 %collective-permute-start.47 = (bf16[512,2048]{1,0:T(8,128)(2,1)S(1)}, bf16[512,2048]{1,0:T(8,128)(2,1)S(1)}, u32[]{:S(2)}, u32[]{:S(2)}) collective-permute-start(bf16[512,2048]{1,0:T(8,128)(2,1)S(1)} %maximum_select_fusion.2), channel_id=1, source_target_pairs={{0,1},{1,0},{2,3},{3,2},{4,5},{5,4},{6,7},{7,6},{8,9},{9,8},{10,11... | collective-permute-start | bytes 6291464 | tf_op jit(solution)/shard_map/ppermute | solution.py:391
  482.1 47.0 %collective-permute-start.34 = (bf16[2,512,1024]{1,2,0:T(8,128)(2,1)}, bf16[2,512,1024]{1,2,0:T(8,128)(2,1)S(1)}, u32[]{:S(2)}, u32[]{:S(2)}) collective-permute-start(bf16[2,512,1024]{1,2,0:T(8,128)(2,1)} %collective-permute-done.32), channel_id=1, source_target_pairs={{0,16},{16,0},{1,17},{17,1},{2,18},{18,2},{3,19},{19,3},{4,20},{20... | collective-permute-start | bytes 6291464 | tf_op jit(solution)/shard_map/ppermute | solution.py:387
  486.6 56.0 %collective-permute-start.45 = (bf16[512,2048]{1,0:T(8,128)(2,1)S(1)}, bf16[512,2048]{1,0:T(8,128)(2,1)S(1)}, u32[]{:S(2)}, u32[]{:S(2)}) collective-permute-start(bf16[512,2048]{1,0:T(8,128)(2,1)S(1)} %collective-permute-done.44), channel_id=1, source_target_pairs={{0,1},{1,0},{2,3},{3,2},{4,5},{5,4},{6,7},{7,6},{8,9},{9,8},{10,11... | collective-permute-start | bytes 6291464 | tf_op jit(solution)/shard_map/ppermute | solution.py:391
  511.9 33.3 %collective-permute-start.31 = (bf16[512,2048]{1,0:T(8,128)(2,1)}, bf16[512,2048]{1,0:T(8,128)(2,1)S(1)}, u32[]{:S(2)}, u32[]{:S(2)}) collective-permute-start(bf16[512,2048]{1,0:T(8,128)(2,1)} %multiply_convert_fusion), channel_id=1, source_target_pairs={{0,1},{1,0},{2,3},{3,2},{4,5},{5,4},{6,7},{7,6},{8,9},{9,8},{10,11... | collective-permute-start | bytes 6291464 | tf_op jit(solution)/shard_map/ppermute | solution.py:391
  541.1 95.3 %collective-permute-start.40 = (bf16[512,2048]{1,0:T(8,128)(2,1)}, bf16[512,2048]{1,0:T(8,128)(2,1)}, u32[]{:S(2)}, u32[]{:S(2)}) collective-permute-start(bf16[512,2048]{1,0:T(8,128)(2,1)} %multiply_convert_fusion), channel_id=1, source_target_pairs={{0,2},{2,0},{4,6},{6,4},{8,10},{10,8},{12,14},{14,12},{1,3},{3,1},... | collective-permute-start | bytes 6291464 | tf_op jit(solution)/shard_map/ppermute | solution.py:441
  619.6 207.5 %collective-permute-start.48 = (bf16[512,2048]{1,0:T(8,128)(2,1)}, bf16[512,2048]{1,0:T(8,128)(2,1)}, u32[]{:S(2)}, u32[]{:S(2)}) collective-permute-start(bf16[512,2048]{1,0:T(8,128)(2,1)} %pad_maximum_fusion.12), channel_id=1, source_target_pairs={{0,1},{1,0},{2,3},{3,2},{4,5},{5,4},{6,7},{7,6},{8,9},{9,8},{10,11... | collective-permute-start | bytes 6291464 | tf_op jit(solution)/shard_map/ppermute | solution.py:391
  705.7 117.1 %collective-permute-start.39 = (bf16[512,2048]{1,0:T(8,128)(2,1)}, bf16[512,2048]{1,0:T(8,128)(2,1)}, u32[]{:S(2)}, u32[]{:S(2)}) collective-permute-start(bf16[512,2048]{1,0:T(8,128)(2,1)} %pad_maximum_fusion.16), channel_id=1, source_target_pairs={{0,1},{1,0},{2,3},{3,2},{4,5},{5,4},{6,7},{7,6},{8,9},{9,8},{10,11... | collective-permute-start | bytes 6291464 | tf_op jit(solution)/shard_map/ppermute | solution.py:391
  762.9 60.4 %collective-permute-start.43 = (bf16[512,2048]{1,0:T(8,128)(2,1)S(1)}, bf16[512,2048]{1,0:T(8,128)(2,1)}, u32[]{:S(2)}, u32[]{:S(2)}) collective-permute-start(bf16[512,2048]{1,0:T(8,128)(2,1)S(1)} %add_convert_fusion.21), channel_id=1, source_target_pairs={{0,2},{2,0},{4,6},{6,4},{8,10},{10,8},{12,14},{14,12},{1,3},{3,1},... | collective-permute-start | bytes 6291464 | tf_op jit(solution)/shard_map/ppermute | solution.py:441
  789.7 196.4 %collective-permute-start.53 = (bf16[2048,1024]{0,1:T(8,128)(2,1)}, bf16[2048,1024]{0,1:T(8,128)(2,1)}, u32[]{:S(2)}, u32[]{:S(2)}) collective-permute-start(bf16[2048,1024]{0,1:T(8,128)(2,1)} %add_convert_fusion.4), channel_id=1, source_target_pairs={{0,16},{16,0},{1,17},{17,1},{2,18},{18,2},{3,19},{19,3},{4,20},{20... | collective-permute-start | bytes 12582920 | tf_op jit(solution)/shard_map/ppermute | solution.py:387
  801.5 54.4 %collective-permute-start.49 = (bf16[512,2048]{1,0:T(8,128)(2,1)S(1)}, bf16[512,2048]{1,0:T(8,128)(2,1)S(1)}, u32[]{:S(2)}, u32[]{:S(2)}) collective-permute-start(bf16[512,2048]{1,0:T(8,128)(2,1)S(1)} %add_convert_fusion.18), channel_id=1, source_target_pairs={{0,2},{2,0},{4,6},{6,4},{8,10},{10,8},{12,14},{14,12},{1,3},{3,1},... | collective-permute-start | bytes 6291464 | tf_op jit(solution)/shard_map/ppermute | solution.py:441
  822.8 149.8 %collective-permute-start.54 = (bf16[2048,1024]{0,1:T(8,128)(2,1)}, bf16[2048,1024]{0,1:T(8,128)(2,1)}, u32[]{:S(2)}, u32[]{:S(2)}) collective-permute-start(bf16[2048,1024]{0,1:T(8,128)(2,1)} %add_convert_fusion.2), channel_id=1, source_target_pairs={{0,16},{16,0},{1,17},{17,1},{2,18},{18,2},{3,19},{19,3},{4,20},{20... | collective-permute-start | bytes 12582920 | tf_op jit(solution)/shard_map/ppermute | solution.py:387
  867.8 47.6 %collective-permute-start.51 = (bf16[512,2048]{1,0:T(8,128)(2,1)}, bf16[512,2048]{1,0:T(8,128)(2,1)}, u32[]{:S(2)}, u32[]{:S(2)}) collective-permute-start(bf16[512,2048]{1,0:T(8,128)(2,1)} %get-tuple-element.184), channel_id=1, source_target_pairs={{0,2},{2,0},{4,6},{6,4},{8,10},{10,8},{12,14},{14,12},{1,3},{3,1},... | collective-permute-start | bytes 6291464 | tf_op jit(solution)/shard_map/ppermute | solution.py:441
  879.3 95.5 %all-to-all-start.4 = ((bf16[4,128,2048]{2,1,0:T(8,128)(2,1)}), bf16[4,128,2048]{2,1,0:T(8,128)(2,1)S(1)}, u32[]{:S(2)}, u32[]{:S(2)}) async-start(bf16[4,128,2048]{2,1,0:T(8,128)(2,1)} %bitcast.82), calls=%async_computation.4 | async-start | bytes 4194304 | tf_op jit(solution)/shard_map/all_to_all | solution.py:456
  893.7 81.1 %collective-permute-start.50 = (bf16[512,2048]{1,0:T(8,128)(2,1)}, bf16[512,2048]{1,0:T(8,128)(2,1)}, u32[]{:S(2)}, u32[]{:S(2)}) collective-permute-start(bf16[512,2048]{1,0:T(8,128)(2,1)} %get-tuple-element.184), channel_id=1, source_target_pairs={{0,1},{1,0},{2,3},{3,2},{4,5},{5,4},{6,7},{7,6},{8,9},{9,8},{10,11... | collective-permute-start | bytes 6291464 | tf_op jit(solution)/shard_map/ppermute | solution.py:391
  915.4 59.4 %collective-permute-start.52 = (bf16[512,2048]{1,0:T(8,128)(2,1)}, bf16[512,2048]{1,0:T(8,128)(2,1)}, u32[]{:S(2)}, u32[]{:S(2)}) collective-permute-start(bf16[512,2048]{1,0:T(8,128)(2,1)} %collective-permute-done.51), channel_id=1, source_target_pairs={{0,1},{1,0},{2,3},{3,2},{4,5},{5,4},{6,7},{7,6},{8,9},{9,8},{10,11... | collective-permute-start | bytes 6291464 | tf_op jit(solution)/shard_map/ppermute | solution.py:391
  974.2 32.8 %collective-permute-start.55 = (bf16[512,1024]{0,1:T(8,128)(2,1)S(1)}, bf16[512,1024]{0,1:T(8,128)(2,1)}, u32[]{:S(2)}, u32[]{:S(2)}) collective-permute-start(bf16[512,1024]{0,1:T(8,128)(2,1)S(1)} %add_convert_fusion.38), channel_id=1, source_target_pairs={{0,4},{2,6},{4,8},{6,10},{8,12},{10,14},{12,0},{14,2},{1,5},{3,7},... | collective-permute-start | bytes 3145736 | tf_op jit(solution)/shard_map/ppermute | solution.py:448
  991.0 136.5 %collective-permute-start.57 = (bf16[512,1024]{0,1:T(8,128)(2,1)}, bf16[512,1024]{0,1:T(8,128)(2,1)}, u32[]{:S(2)}, u32[]{:S(2)}) collective-permute-start(bf16[512,1024]{0,1:T(8,128)(2,1)} %get-tuple-element.194), channel_id=1, source_target_pairs={{0,4},{2,6},{4,8},{6,10},{8,12},{10,14},{12,0},{14,2},{1,5},{3,7},... | collective-permute-start | bytes 3145736 | tf_op jit(solution)/shard_map/ppermute | solution.py:448
  991.1 136.5 %collective-permute-start.58 = (bf16[512,1024]{0,1:T(8,128)(2,1)}, bf16[512,1024]{0,1:T(8,128)(2,1)}, u32[]{:S(2)}, u32[]{:S(2)}) collective-permute-start(bf16[512,1024]{0,1:T(8,128)(2,1)} %get-tuple-element.195), channel_id=1, source_target_pairs={{0,8},{2,10},{4,12},{6,14},{8,0},{10,2},{12,4},{14,6},{1,9},{3,11}... | collective-permute-start | bytes 3145736 | tf_op jit(solution)/shard_map/ppermute | solution.py:448
  994.9 132.7 %collective-permute-start.59 = (bf16[512,1024]{0,1:T(8,128)(2,1)}, bf16[512,1024]{0,1:T(8,128)(2,1)}, u32[]{:S(2)}, u32[]{:S(2)}) collective-permute-start(bf16[512,1024]{0,1:T(8,128)(2,1)} %get-tuple-element.196), channel_id=1, source_target_pairs={{0,12},{2,14},{4,0},{6,2},{8,4},{10,6},{12,8},{14,10},{1,13},{3,15... | collective-permute-start | bytes 3145736 | tf_op jit(solution)/shard_map/ppermute | solution.py:448
  1010.3 116.6 %collective-permute-start.56 = (bf16[512,1024]{0,1:T(8,128)(2,1)}, bf16[512,1024]{0,1:T(8,128)(2,1)}, u32[]{:S(2)}, u32[]{:S(2)}) collective-permute-start(bf16[512,1024]{0,1:T(8,128)(2,1)} %add_convert_fusion.36), channel_id=1, source_target_pairs={{0,4},{2,6},{4,8},{6,10},{8,12},{10,14},{12,0},{14,2},{1,5},{3,7},... | collective-permute-start | bytes 3145736 | tf_op jit(solution)/shard_map/ppermute | solution.py:448
  1018.0 115.9 %collective-permute-start.78 = (bf16[512,1028]{0,1:T(8,128)(2,1)}, bf16[512,1028]{0,1:T(8,128)(2,1)}, u32[]{:S(2)}, u32[]{:S(2)}) collective-permute-start(bf16[512,1028]{0,1:T(8,128)(2,1)} %copy.390), channel_id=1, source_target_pairs={{0,16},{16,0},{1,17},{17,1},{2,18},{18,2},{3,19},{19,3},{4,20},{20... | collective-permute-start | bytes 3158024 | tf_op jit(solution)/shard_map/ppermute | solution.py:387
  1126.9 126.9 %collective-permute-start.83 = (bf16[2048,1024]{0,1:T(8,128)(2,1)}, bf16[2048,1024]{0,1:T(8,128)(2,1)}, u32[]{:S(2)}, u32[]{:S(2)}) collective-permute-start(bf16[2048,1024]{0,1:T(8,128)(2,1)} %add_convert_fusion), channel_id=1, source_target_pairs={{0,16},{16,0},{1,17},{17,1},{2,18},{18,2},{3,19},{19,3},{4,20},{20... | collective-permute-start | bytes 12582920 | tf_op jit(solution)/shard_map/ppermute | solution.py:387
  1155.8 71.8 %collective-permute-start.61 = (bf16[512,2048]{1,0:T(8,128)(2,1)}, bf16[512,2048]{1,0:T(8,128)(2,1)}, u32[]{:S(2)}, u32[]{:S(2)}) collective-permute-start(bf16[512,2048]{1,0:T(8,128)(2,1)} %slice.561), channel_id=1, source_target_pairs={{0,1},{1,0},{2,3},{3,2},{4,5},{5,4},{6,7},{7,6},{8,9},{9,8},{10,11... | collective-permute-start | bytes 6291464 | tf_op jit(solution)/shard_map/ppermute | solution.py:391
  1161.0 55.2 %collective-permute-start.87 = (bf16[512,1024]{0,1:T(8,128)(2,1)}, bf16[512,1024]{0,1:T(8,128)(2,1)}, u32[]{:S(2)}, u32[]{:S(2)}) collective-permute-start(bf16[512,1024]{0,1:T(8,128)(2,1)} %add_convert_fusion.25), channel_id=1, source_target_pairs={{0,4},{2,6},{4,8},{6,10},{8,12},{10,14},{12,0},{14,2},{1,5},{3,7},... | collective-permute-start | bytes 3145736 | tf_op jit(solution)/shard_map/ppermute | solution.py:448
  1180.0 31.4 %collective-permute-start.81 = (bf16[256,514]{0,1:T(8,128)(2,1)}, bf16[256,514]{0,1:T(8,128)(2,1)}, u32[]{:S(2)}, u32[]{:S(2)}) collective-permute-start(bf16[256,514]{0,1:T(8,128)(2,1)} %get-tuple-element.262), channel_id=1, source_target_pairs={{0,8},{2,10},{4,12},{6,14},{8,0},{10,2},{12,4},{14,6},{1,9},{3,11}... | collective-permute-start | bytes 789512 | tf_op jit(solution)/shard_map/ppermute | solution.py:448
  1211.3 96.8 %collective-permute-start.60 = (bf16[512,2048]{1,0:T(8,128)(2,1)}, bf16[512,2048]{1,0:T(8,128)(2,1)}, u32[]{:S(2)}, u32[]{:S(2)}) collective-permute-start(bf16[512,2048]{1,0:T(8,128)(2,1)} %slice.559), channel_id=1, source_target_pairs={{0,1},{1,0},{2,3},{3,2},{4,5},{5,4},{6,7},{7,6},{8,9},{9,8},{10,11... | collective-permute-start | bytes 6291464 | tf_op jit(solution)/shard_map/ppermute | solution.py:391
  1232.0 76.1 %collective-permute-start.62 = (bf16[512,2048]{1,0:T(8,128)(2,1)}, bf16[512,2048]{1,0:T(8,128)(2,1)}, u32[]{:S(2)}, u32[]{:S(2)}) collective-permute-start(bf16[512,2048]{1,0:T(8,128)(2,1)} %add_convert_fusion.13), channel_id=1, source_target_pairs={{0,2},{2,0},{4,6},{6,4},{8,10},{10,8},{12,14},{14,12},{1,3},{3,1},... | collective-permute-start | bytes 6291464 | tf_op jit(solution)/shard_map/ppermute | solution.py:441
  1252.4 37.8 %collective-permute-start.69 = (bf16[768,1060]{0,1:T(8,128)(2,1)}, bf16[768,1060]{0,1:T(8,128)(2,1)}, u32[]{:S(2)}, u32[]{:S(2)}) collective-permute-start(bf16[768,1060]{0,1:T(8,128)(2,1)} %copy.378), channel_id=1, source_target_pairs={{0,16},{16,0},{1,17},{17,1},{2,18},{18,2},{3,19},{19,3},{4,20},{20... | collective-permute-start | bytes 4884488 | tf_op jit(solution)/shard_map/ppermute | solution.py:387
  1286.9 34.8 %collective-permute-start.85 = (bf16[512,1024]{0,1:T(8,128)(2,1)}, bf16[512,1024]{0,1:T(8,128)(2,1)}, u32[]{:S(2)}, u32[]{:S(2)}) collective-permute-start(bf16[512,1024]{0,1:T(8,128)(2,1)} %add_convert_fusion.31), channel_id=1, source_target_pairs={{0,4},{2,6},{4,8},{6,10},{8,12},{10,14},{12,0},{14,2},{1,5},{3,7},... | collective-permute-start | bytes 3145736 | tf_op jit(solution)/shard_map/ppermute | solution.py:448
  1305.1 28.9 %collective-permute-start.70 = (bf16[2,384,530]{1,0,2:T(2,128)(2,1)}, bf16[2,384,530]{1,0,2:T(2,128)(2,1)}, u32[]{:S(2)}, u32[]{:S(2)}) collective-permute-start(bf16[2,384,530]{1,0,2:T(2,128)(2,1)} %pad_maximum_fusion.29), channel_id=1, source_target_pairs={{0,1},{1,0},{2,3},{3,2},{4,5},{5,4},{6,7},{7,6},{8,9},{9,8},{10,11... | collective-permute-start | bytes 2442248 | tf_op jit(solution)/shard_map/ppermute | solution.py:391
  1328.5 28.3 %collective-permute-start.86 = (bf16[512,1024]{0,1:T(8,128)(2,1)}, bf16[512,1024]{0,1:T(8,128)(2,1)}, u32[]{:S(2)}, u32[]{:S(2)}) collective-permute-start(bf16[512,1024]{0,1:T(8,128)(2,1)} %add_convert_fusion.29), channel_id=1, source_target_pairs={{0,4},{2,6},{4,8},{6,10},{8,12},{10,14},{12,0},{14,2},{1,5},{3,7},... | collective-permute-start | bytes 3145736 | tf_op jit(solution)/shard_map/ppermute | solution.py:448
  1341.7 45.0 %collective-permute-start.73 = (bf16[384,530]{1,0:T(8,128)(2,1)}, bf16[384,530]{1,0:T(8,128)(2,1)S(1)}, u32[]{:S(2)}, u32[]{:S(2)}) collective-permute-start(bf16[384,530]{1,0:T(8,128)(2,1)} %get-tuple-element.234), channel_id=1, source_target_pairs={{0,12},{2,14},{4,0},{6,2},{8,4},{10,6},{12,8},{14,10},{1,13},{3,15... | collective-permute-start | bytes 1221128 | tf_op jit(solution)/shard_map/ppermute | solution.py:448
  1343.0 63.8 %collective-permute-start.72 = (bf16[384,530]{1,0:T(8,128)(2,1)}, bf16[384,530]{1,0:T(8,128)(2,1)}, u32[]{:S(2)}, u32[]{:S(2)}) collective-permute-start(bf16[384,530]{1,0:T(8,128)(2,1)} %get-tuple-element.235), channel_id=1, source_target_pairs={{0,8},{2,10},{4,12},{6,14},{8,0},{10,2},{12,4},{14,6},{1,9},{3,11}... | collective-permute-start | bytes 1221128 | tf_op jit(solution)/shard_map/ppermute | solution.py:448
  1343.1 63.8 %collective-permute-start.71 = (bf16[384,530]{1,0:T(8,128)(2,1)}, bf16[384,530]{1,0:T(8,128)(2,1)}, u32[]{:S(2)}, u32[]{:S(2)}) collective-permute-start(bf16[384,530]{1,0:T(8,128)(2,1)} %get-tuple-element.233), channel_id=1, source_target_pairs={{0,4},{2,6},{4,8},{6,10},{8,12},{10,14},{12,0},{14,2},{1,5},{3,7},... | collective-permute-start | bytes 1221128 | tf_op jit(solution)/shard_map/ppermute | solution.py:448
  1363.7 113.6 %all-to-all-start.5 = ((bf16[4,128,2048]{2,1,0:T(8,128)(2,1)}), bf16[4,128,2048]{2,1,0:T(8,128)(2,1)}, u32[]{:S(2)}, u32[]{:S(2)}) async-start(bf16[4,128,2048]{2,1,0:T(8,128)(2,1)} %bitcast.84), calls=%async_computation.5 | async-start | bytes 4194304 | tf_op jit(solution)/shard_map/all_to_all | solution.py:456
  1418.4 50.0 %collective-permute-start.76 = (bf16[2,2,64,514]{3,2,0,1:T(8,128)(2,1)S(1)}, bf16[2,2,64,514]{3,2,0,1:T(8,128)(2,1)S(1)}, u32[]{:S(2)}, u32[]{:S(2)}) collective-permute-start(bf16[2,2,64,514]{3,2,0,1:T(8,128)(2,1)S(1)} %add_convert_fusion.42), channel_id=1, source_target_pairs={{0,8},{2,10},{4,12},{6,14},{8,0},{10,2},{12,4},{14,6},{1,9},{3,11}... | collective-permute-start | bytes 789512 | tf_op jit(solution)/shard_map/ppermute | solution.py:448
  1418.5 50.0 %collective-permute-start.75 = (bf16[2,2,64,514]{3,2,0,1:T(8,128)(2,1)S(1)}, bf16[2,2,64,514]{3,2,0,1:T(8,128)(2,1)S(1)}, u32[]{:S(2)}, u32[]{:S(2)}) collective-permute-start(bf16[2,2,64,514]{3,2,0,1:T(8,128)(2,1)S(1)} %add_convert_fusion.42), channel_id=1, source_target_pairs={{0,4},{2,6},{4,8},{6,10},{8,12},{10,14},{12,0},{14,2},{1,5},{3,7},... | collective-permute-start | bytes 789512 | tf_op jit(solution)/shard_map/ppermute | solution.py:448
  (216 other events, 3855.3 us)

commit v2 on v1

--- a/solution.py
+++ b/solution.py
@@ -1,4 +1,4 @@
-import functools
+import math
 
 import jax
 import jax.numpy as jnp
@@ -15,6 +15,7 @@
 FEATS = 2 * HD
 AUG = HD + 16
 F32 = jnp.float32
+PART = 512
 BF16 = jnp.bfloat16
 
 
@@ -37,6 +38,10 @@
     return bias_prev[WINDOW:], bias_own, linear_prev, linear_own[:WINDOW]
 
 
+def turned(values):
+    return jnp.transpose(values.astype(F32)).astype(BF16)
+
+
 def with_ones(values):
     return jnp.concatenate([values, jnp.ones((AUG - HD, CHUNK), values.dtype)], axis=0)
 
@@ -59,13 +64,13 @@
 
 def forward_kernel(
     last_ref, order_ref, seg_row_ref, seg_own_ref, seg_prev_ref,
-    q_ref, kt_ref, k_ref, kp_ref, vt_ref, vtp_ref, maps_t_ref,
+    q_ref, kt_ref, ktp_ref, vt_ref, vtp_ref, maps_t_ref,
     mixed_ref, peak_ref, den_ref, fq_ref, fkt_ref, fk_ref, state_out_ref,
     state_ref, fk_prev_ref,
 ):
     chunk = pl.program_id(0)
     head_count = fq_ref.shape[0]
-    per_key = head_count // k_ref.shape[0]
+    per_key = head_count * HD // kt_ref.shape[0]
 
     @pl.when(chunk == 0)
     def _():
@@ -81,6 +86,8 @@
     carried = jnp.where(seg_row == tag_state, 1.0, 0.0)
     joined = jnp.where(tag_state == tag_prev, 1.0, 0.0)
     keep_prev = jnp.where(seg_prev_ref[...] == tag_prev, 1.0, 0.0).astype(BF16)
+    k_own = turned(kt_ref[...])
+    k_prev = turned(ktp_ref[...])
     for head in range(head_count):
         group = head // per_key
         rows = slice(head * HD, (head + 1) * HD)
@@ -94,8 +101,8 @@
         feat_k = jnp.transpose(feat_kt).astype(BF16)
         fk_ref[head] = feat_k
         scaled = query * jnp.asarray(HD**-0.5, BF16)
-        score_prev = mm(kp_ref[group, WINDOW:, :], scaled) + bias_prev
-        score_own = mm(k_ref[group], scaled) + bias_own
+        score_prev = mm(k_prev[WINDOW:, key_rows], scaled) + bias_prev
+        score_own = mm(k_own[:, key_rows], scaled) + bias_own
         peak = jnp.maximum(
             jnp.max(score_prev, axis=0, keepdims=True), jnp.max(score_own, axis=0, keepdims=True)
         )
@@ -127,7 +134,7 @@
 
 def backward_kernel(
     last_ref, order_ref, seg_row_ref, seg_own_ref, seg_prev_ref,
-    q_ref, kt_ref, ktp_ref, k_ref, kp_ref, v_ref, vp_ref, vtp_ref, maps_ref, lift_ref,
+    q_ref, kt_ref, ktp_ref, vt_ref, vtp_ref, maps_ref, lift_ref,
     mixed_ref, grad_ref, peak_ref, den_ref, fq_ref, fkt_ref, fktp_ref, fk_ref, fkp_ref, state_ref,
     grows_ref, gmaps_ref,
     gstate_ref, cphi_ref, ck_ref, cv_ref,
@@ -135,7 +142,7 @@
     step = pl.program_id(0)
     chunk = pl.num_programs(0) - 1 - step
     head_count = fq_ref.shape[0]
-    group_count = k_ref.shape[0]
+    group_count = kt_ref.shape[0] // HD
     per_key = head_count // group_count
 
     @pl.when(step == 0)
@@ -158,6 +165,10 @@
     keep_prev = jnp.transpose(jnp.broadcast_to(keep_col, (CHUNK, CHUNK)))[:1]
     scale = HD**-0.5
     none = jnp.zeros((WINDOW, CHUNK), F32)
+    k_own = turned(kt_ref[...])
+    k_prev = turned(ktp_ref[...])
+    v_own = turned(vt_ref[...])
+    v_prev = turned(vtp_ref[...])
     for group in range(group_count):
         key_rows = slice(group * HD, (group + 1) * HD)
         key_t = kt_ref[key_rows, :]
@@ -172,8 +183,8 @@
             scaled = query * jnp.asarray(scale, BF16)
             peak = peak_ref[head : head + 1, :]
             den = den_ref[head : head + 1, :]
-            weight_prev = jnp.exp(mm(kp_ref[group, WINDOW:, :], scaled) + bias_prev - peak)
-            weight_own = jnp.exp(mm(k_ref[group], scaled) + bias_own - peak)
+            weight_prev = jnp.exp(mm(k_prev[WINDOW:, key_rows], scaled) + bias_prev - peak)
+            weight_own = jnp.exp(mm(k_own[:, key_rows], scaled) + bias_own - peak)
             damp = jnp.exp(-peak)
             feat_q = fq_ref[head].astype(F32)
             damped = feat_q * damp
@@ -190,8 +201,8 @@
             dtotal = jnp.concatenate(
                 [dnum, dden, jnp.zeros((AUG - HD - 1, CHUNK), F32)], axis=0
             ).astype(BF16)
-            dall_prev = mm(vp_ref[group], dnum_low) + dden
-            dall_own = mm(v_ref[group], dnum_low) + dden
+            dall_prev = mm(v_prev[:, key_rows], dnum_low) + dden
+            dall_own = mm(v_own[:, key_rows], dnum_low) + dden
             dscore_prev = jnp.concatenate([none, weight_prev * dall_prev[WINDOW:]], axis=0).astype(BF16)
             dscore_own = (weight_own * dall_own).astype(BF16)
             dlin_prev = (linear_prev * dall_prev).astype(BF16)
@@ -235,9 +246,9 @@
     grows_ref[width:, :] = mm(lift_ref[...], grows_ref[:width, :]).astype(BF16)
 
 
-def attend_forward(last, order, seg_row, seg_col, rows, natural, maps_t):
+def attend_forward(last, order, seg_row, seg_col, rows, maps_t, waits=()):
     heads = maps_t.shape[0]
-    groups, length = natural.shape[0] // 2, natural.shape[1]
+    groups, length = (rows.shape[0] // HD - heads) // 2, rows.shape[1]
     chunks = length // CHUNK
     first = heads // groups
 
@@ -246,9 +257,6 @@
 
     def spec(count, block, shift):
         return pl.BlockSpec((count * HD, CHUNK), lambda c, last, order: (block, order[shift(c)]))
-
-    def nat(block, shift):
-        return pl.BlockSpec((groups, CHUNK, HD), lambda c, last, order: (block, order[shift(c)], 0))
 
     def here(c):
         return c
@@ -256,7 +264,7 @@
     stat = pl.BlockSpec((heads, CHUNK), lambda c, last, order: (0, c))
     feat_t = pl.BlockSpec((heads, FEATS, CHUNK), lambda c, last, order: (0, 0, c))
     return pl.pallas_call(
-        forward_kernel,
+        ignoring(forward_kernel, 11, len(waits)),
         grid_spec=pltpu.PrefetchScalarGridSpec(
             num_scalar_prefetch=2,
             grid=(chunks,),
@@ -266,12 +274,12 @@
                 pl.BlockSpec((CHUNK, 1), lambda c, last, order: (before(c), 0)),
                 spec(heads, 0, here),
                 spec(groups, first, here),
-                nat(0, here),
-                nat(0, before),
+                spec(groups, first, before),
                 spec(groups, first + 1, here),
                 spec(groups, first + 1, before),
                 pl.BlockSpec((heads, HD, HD), lambda c, last, order: (0, 0, 0)),
-            ],
+            ]
+            + [pl.BlockSpec(memory_space=pl.ANY)] * len(waits),
             out_specs=[
                 spec(heads, 0, here), stat, stat,
                 feat_t, feat_t,
@@ -296,16 +304,20 @@
             dimension_semantics=("arbitrary",), vmem_limit_bytes=32 * 2**20
         ),
         cost_estimate=pl.CostEstimate(
-            flops=heads * length * 3600000, bytes_accessed=heads * length * 1600, transcendentals=0
+            flops=heads * length * 1060000, bytes_accessed=heads * length * 400, transcendentals=0
         ),
         name="attend_forward",
-    )(last, order, seg_row, seg_col, seg_col, rows, rows, natural, natural, rows, rows, maps_t)
-
-
-def attend_backward(last, order, seg_row, seg_col, rows, natural, maps, lift, saved, grad):
+    )(
+        last, order, seg_row, seg_col, seg_col, rows, rows, rows, rows, rows, maps_t, *waits
+    )
+
+
+def attend_backward(
+    last, order, seg_row, seg_col, rows, maps, lift, saved, grad, waits=()
+):
     mixed, peak, den, fq, fkt, fk, states = saved
     heads = maps.shape[0]
-    groups, length = natural.shape[0] // 2, natural.shape[1]
+    groups, length = (rows.shape[0] // HD - heads) // 2, rows.shape[1]
     chunks = length // CHUNK
     first = heads // groups
     height = lift.shape[0] + lift.shape[1]
@@ -319,9 +331,6 @@
     def spec(count, block, shift):
         return pl.BlockSpec((count * HD, CHUNK), lambda s, last, order: (block, order[shift(s)]))
 
-    def nat(block, shift):
-        return pl.BlockSpec((groups, CHUNK, HD), lambda s, last, order: (block, order[shift(s)], 0))
-
     def feat_t(shift):
         return pl.BlockSpec((heads, FEATS, CHUNK), lambda s, last, order: (0, 0, shift(s)))
 
@@ -331,7 +340,7 @@
     stat = pl.BlockSpec((heads, CHUNK), lambda s, last, order: (0, here(s)))
     whole = pl.BlockSpec((heads, HD, HD), lambda s, last, order: (0, 0, 0))
     return pl.pallas_call(
-        backward_kernel,
+        ignoring(backward_kernel, 22, len(waits)),
         grid_spec=pltpu.PrefetchScalarGridSpec(
             num_scalar_prefetch=2,
             grid=(chunks,),
@@ -341,15 +350,14 @@
                 pl.BlockSpec((CHUNK, 1), lambda s, last, order: (before(s), 0)),
                 spec(heads, 0, here),
                 spec(groups, first, here), spec(groups, first, before),
-                nat(0, here), nat(0, before),
-                nat(1, here), nat(1, before),
-                spec(groups, first + 1, before),
+                spec(groups, first + 1, here), spec(groups, first + 1, before),
                 whole,
                 pl.BlockSpec(lift.shape, lambda s, last, order: (0, 0)),
                 spec(heads, 0, here), spec(heads, 0, here), stat, stat,
                 feat_t(here), feat_t(here), feat_t(before), feat(here), feat(before),
                 pl.BlockSpec((1, heads, AUG, FEATS), lambda s, last, order: (here(s), 0, 0, 0)),
-            ],
+            ]
+            + [pl.BlockSpec(memory_space=pl.ANY)] * len(waits),
             out_specs=[
                 pl.BlockSpec((height, CHUNK), lambda s, last, order: (0, order[here(s)])),
                 whole,
@@ -369,13 +377,260 @@
             dimension_semantics=("arbitrary",), vmem_limit_bytes=32 * 2**20
         ),
         cost_estimate=pl.CostEstimate(
-            flops=heads * length * 7200000, bytes_accessed=heads * length * 2400, transcendentals=0
+            flops=heads * length * 2100000, bytes_accessed=heads * length * 600, transcendentals=0
         ),
         name="attend_backward",
     )(
-        last, order, seg_row, seg_col, seg_col, rows, rows, rows, natural, natural, natural, natural,
-        rows, maps, lift, mixed, grad, peak, den, fq, fkt, fkt, fk, fk, states,
-    )
+        last, order, seg_row, seg_col, seg_col, rows, rows, rows, rows, rows, maps, lift, mixed, grad, peak, den, fq, fkt, fkt, fk, fk, states, *waits,
+    )
+
+
+def ignoring(kernel, inputs, waits):
+    def body(*refs):
+        kernel(*refs[:inputs], *refs[inputs + waits :])
+
+    return body
+
+
+def after(value, *others):
+    values = jax.tree.leaves(value)
+    tokens = jax.tree.leaves(others)
+    anywhere = pl.BlockSpec(memory_space=pl.ANY)
+    out = pl.pallas_call(
+        lambda *refs: None,
+        in_specs=[anywhere] * (len(values) + len(tokens)),
+        out_specs=[anywhere] * len(values),
+        out_shape=[jax.ShapeDtypeStruct(v.shape, v.dtype) for v in values],
+        input_output_aliases={i: i for i in range(len(values))},
+        cost_estimate=pl.CostEstimate(flops=0, bytes_accessed=0, transcendentals=0),
+        name="after",
+    )(*values, *tokens)
+    return jax.tree.unflatten(jax.tree.structure(value), out)
+
+
+def stack_rows(pieces):
+    rows, columns = pieces[0].shape
+    tall = min(256, rows)
+    steps = rows // tall
+    count = len(pieces)
+
+    def kernel(*refs):
+        for place in range(count):
+
+            @pl.when(pl.program_id(0) == place)
+            def _(place=place):
+                refs[-1][...] = refs[place][...]
+
+    def spec(place):
+        def at(i, j):
+            return (jnp.where(i < place, 0, jnp.where(i > place, steps - 1, j)), 0)
+
+        return pl.BlockSpec((tall, columns), at)
+
+    return pl.pallas_call(
+        kernel,
+        grid=(count, steps),
+        in_specs=[spec(place) for place in range(count)],
+        out_specs=pl.BlockSpec((tall, columns), lambda i, j: (i * steps + j, 0)),
+        out_shape=jax.ShapeDtypeStruct((count * rows, columns), pieces[0].dtype),
+        cost_estimate=pl.CostEstimate(
+            flops=0, bytes_accessed=count * rows * columns, transcendentals=0
+        ),
+        name="stack_rows",
+    )(*pieces)
+
+
+def weight_grad_kernel(left_ref, right_ref, out_ref):
+    out_ref[...] = mm(left_ref[...], right_ref[...], 0, 0).astype(BF16)
+
+
+def weight_grad(left, right, part, waits=()):
+    tokens, rows = left.shape
+    half = right.shape[1] // 2
+    tall = min(512, rows)
+    return dense_call(
+        weight_grad_kernel,
+        (rows // tall,),
+        [
+            pl.BlockSpec((tokens, tall), lambda i: (0, i)),
+            pl.BlockSpec((tokens, half), lambda i: (0, part)),
+        ],
+        pl.BlockSpec((tall, half), lambda i: (i, 0)),
+        jax.ShapeDtypeStruct((rows, half), BF16),
+        2 * tokens * rows * half,
+        "weight_grad",
+        waits,
+    )(left, right, *waits)
+
+
+def weight_grad_halves(left, right, swap, waits=()):
+    tokens, rows = left.shape
+    half = right.shape[1] // 2
+    tall = min(512, rows)
+
+    def kernel(swap_ref, left_ref, right_ref, *refs):
+        refs[-1][0] = mm(left_ref[...], right_ref[...], 0, 0).astype(BF16)
+
+    return pl.pallas_call(
+        kernel,
+        grid_spec=pltpu.PrefetchScalarGridSpec(
+            num_scalar_prefetch=1,
+            grid=(2, rows // tall),
+            in_specs=[
+                pl.BlockSpec((tokens, tall), lambda p, i, swap: (0, i)),
+                pl.BlockSpec((tokens, half), lambda p, i, swap: (0, p + swap[0] - 2 * p * swap[0])),
+            ]
+            + [pl.BlockSpec(memory_space=pl.ANY)] * len(waits),
+            out_specs=pl.BlockSpec((1, tall, half), lambda p, i, swap: (p, i, 0)),
+        ),
+        out_shape=jax.ShapeDtypeStruct((2, rows, half), BF16),
+        compiler_params=pltpu.CompilerParams(
+            dimension_semantics=("arbitrary", "arbitrary"), vmem_limit_bytes=48 * 2**20
+        ),
+        cost_estimate=pl.CostEstimate(
+            flops=tokens * rows * half, bytes_accessed=rows * half, transcendentals=0
+        ),
+        name="weight_grad_halves",
+    )(swap, left, right, *waits)
+
+
+def dense_call(kernel, grid, in_specs, out_specs, out_shape, flops, name, waits=()):
+    in_specs = in_specs + [pl.BlockSpec(memory_space=pl.ANY)] * len(waits)
+    return pl.pallas_call(
+        ignoring(kernel, len(in_specs) - len(waits), len(waits)),
+        grid=grid,
+        in_specs=in_specs,
+        out_specs=out_specs,
+        out_shape=out_shape,
+        compiler_params=pltpu.CompilerParams(
+            dimension_semantics=("arbitrary",) * len(grid), vmem_limit_bytes=48 * 2**20
+        ),
+        cost_estimate=pl.CostEstimate(
+            flops=flops // 3, bytes_accessed=flops // 8000, transcendentals=0
+        ),
+        name=name,
+    )
+
+
+def sigmoid_of(values):
+    return 0.5 * jnp.tanh(0.5 * values) + 0.5
+
+
+def row_parts(count):
+    size = min(PART, count)
+    return [slice(at, at + size) for at in range(0, count, size)]
+
+
+def gate_kernel(rows_ref, own_gate, other_gate, own_up, other_up, gate_ref, up_ref, hidden_ref):
+    half = own_gate.shape[1]
+    for part in row_parts(rows_ref.shape[0]):
+        left = rows_ref[part, :half]
+        right = rows_ref[part, half:]
+        gate = mm(left, own_gate[...], 1, 1) + mm(right, other_gate[...], 1, 1)
+        up = mm(left, own_up[...], 1, 1) + mm(right, other_up[...], 1, 1)
+        gate_ref[part, :] = gate.astype(BF16)
+        up_ref[part, :] = up.astype(BF16)
+        hidden_ref[part, :] = (gate * sigmoid_of(gate) * up).astype(BF16)
+
+
+def gate_back_kernel(grad_ref, own_down, other_down, gate_ref, up_ref, dgate_ref, dup_ref):
+    half = own_down.shape[1]
+    for part in row_parts(grad_ref.shape[0]):
+        grad = mm(grad_ref[part, :half], own_down[...], 1, 1) + mm(
+            grad_ref[part, half:], other_down[...], 1, 1
+        )
+        gate = gate_ref[part, :].astype(F32)
+        sigmoid = sigmoid_of(gate)
+        grad_swish = grad * sigmoid
+        dup_ref[part, :] = (grad_swish * gate).astype(BF16)
+        dgate_ref[part, :] = (
+            grad_swish * up_ref[part, :].astype(F32) * (1.0 + gate * (1.0 - sigmoid))
+        ).astype(BF16)
+
+
+def sum_kernel(count, lefts_and_weights, out_ref):
+    lefts = lefts_and_weights[:count]
+    owns = lefts_and_weights[count : 2 * count]
+    others = lefts_and_weights[2 * count :]
+    column = pl.program_id(0)
+
+    def write(weights):
+        total = mm(lefts[0][...], weights[0][...])
+        for left, weight in zip(lefts[1:], weights[1:]):
+            total = total + mm(left[...], weight[...])
+        out_ref[...] = total.astype(BF16)
+
+    across = pl.num_programs(0) // 2
+
+    @pl.when(column < across)
+    def _():
+        write(owns)
+
+    @pl.when(column >= across)
+    def _():
+        write(others)
+
+
+def gate_forward(rows, own_gate, other_gate, own_up, other_up, waits=()):
+    tokens, width = rows.shape
+    hidden, half = own_gate.shape
+    tall, wide = min(512, tokens), min(1024, hidden)
+    weight = pl.BlockSpec((wide, half), lambda j, i: (j, 0))
+    out = pl.BlockSpec((tall, wide), lambda j, i: (i, j))
+    return dense_call(
+        gate_kernel,
+        (hidden // wide, tokens // tall),
+        [pl.BlockSpec((tall, width), lambda j, i: (i, 0))] + [weight] * 4,
+        [out] * 3,
+        [jax.ShapeDtypeStruct((tokens, hidden), BF16)] * 3,
+        4 * tokens * width * hidden,
+        "gate_forward",
+        waits,
+    )(rows, own_gate, other_gate, own_up, other_up, *waits)
+
+
+def gate_backward(grad, own_down, other_down, gate, up, waits=()):
+    tokens, width = grad.shape
+    hidden, half = own_down.shape
+    tall, wide = min(512, tokens), min(1024, hidden)
+    weight = pl.BlockSpec((wide, half), lambda j, i: (j, 0))
+    out = pl.BlockSpec((tall, wide), lambda j, i: (i, j))
+    return dense_call(
+        gate_back_kernel,
+        (hidden // wide, tokens // tall),
+        [pl.BlockSpec((tall, width), lambda j, i: (i, 0)), weight, weight, out, out],
+        [out] * 2,
+        [jax.ShapeDtypeStruct((tokens, hidden), BF16)] * 2,
+        2 * tokens * width * hidden,
+        "gate_backward",
+        waits,
+    )(grad, own_down, other_down, gate, up, *waits)
+
+
+def sum_products(lefts, owns, others, start, tokens, waits=()):
+    count = len(lefts)
+    depth = lefts[0].shape[1]
+    half = owns[0].shape[1]
+    tall, wide = math.gcd(math.gcd(start, tokens), 1024), min(512, half)
+    across = half // wide
+    first = start // tall
+
+    def kernel(*refs):
+        sum_kernel(count, refs[:-1], refs[-1])
+
+    left = pl.BlockSpec((tall, depth), lambda j, i: (first + i, 0))
+    own = pl.BlockSpec((depth, wide), lambda j, i: (0, jnp.minimum(j, across - 1)))
+    other = pl.BlockSpec((depth, wide), lambda j, i: (0, jnp.maximum(j - across, 0)))
+    return dense_call(
+        kernel,
+        (2 * across, tokens // tall),
+        [left] * count + [own] * count + [other] * count,
+        pl.BlockSpec((tall, wide), lambda j, i: (i, j)),
+        jax.ShapeDtypeStruct((tokens, 2 * half), BF16),
+        4 * count * tokens * depth * half,
+        "sum_products",
+        waits,
+    )(*lefts, *owns, *others, *waits)
 
 
 ALL = ("rows", "heads", "seq")
@@ -389,10 +644,6 @@
 
 def over_c(value):
     return lax.ppermute(value, "seq", SWAP)
-
-
-def after(value, *others):
-    return lax.optimization_barrier((value, others))[0]
 
 
 def body(
@@ -457,6 +708,12 @@
             value, "heads", split_axis=0, concat_axis=0, tiled=True, axis_index_groups=groups
         )
 
+    def gather_z(block):
+        return trade_z(jnp.broadcast_to(block[None], (depth,) + block.shape))
+
+    def scatter_z(blocks):
+        return jnp.sum(trade_z(blocks).astype(F32), axis=0)
+
     def trade_c(value, split, concat):
         return lax.all_to_all(value, "seq", split_axis=split, concat_axis=concat, tiled=True)
 
@@ -478,37 +735,24 @@
             x == 1, jnp.concatenate([value[..., half:], value[..., :half]], axis=-1), value
         )
 
-    def ring(block):
-        blocks = [block]
-        for _ in range(depth - 1):
-            blocks.append(over_z(blocks[-1]))
-        return blocks
-
-    def shift_sum(blocks):
-        total = blocks[0].astype(F32)
-        for k in range(1, depth):
-            total = total + over_z(blocks[depth - k], k).astype(F32)
+    def shift_sum(blocks, *waits):
+        total = lax.dynamic_index_in_dim(blocks, z, 0, False).astype(F32)
+        moved = [
+            over_z(lax.dynamic_index_in_dim(blocks, (z + k) % depth, 0, False), k)
+            for k in range(1, depth)
+        ]
+        for block in after(moved, *waits) if waits else moved:
+            total = total + block.astype(F32)
         return total
 
-    def shifts(block):
-        return [block] + [over_z(block, k) for k in range(1, depth)]
-
-    def ring_sum(blocks):
-        total = blocks[1]
-        for j in list(range(2, depth)) + [0]:
-            moved = over_z(total)
-            total = (moved.astype(F32) + blocks[j].astype(F32)).astype(
-                F32 if j == 0 else blocks[1].dtype
-            )
-        return total
-
-    def gather_tokens(value):
-        chip = jnp.concatenate([value, over_c(value)], axis=0)
-        others = []
+    def gather_tokens(value, *waits):
+        pieces = [value, over_c(value)]
         for k in range(1, wide):
             moved = over_y(value, k)
-            others += [moved, over_c(moved)]
-        return chip, jnp.concatenate(others, axis=0)
+            if waits:
+                moved = after(moved, *waits)
+            pieces += [moved, over_c(moved)]
+        return pieces
 
     def reduce_tokens(make_chip, make_others, waits=()):
         others = make_others()
@@ -520,13 +764,13 @@
             moved = over_c(others[start + held : start + 2 * held])
             sent.append((mine.astype(F32) + moved.astype(F32)).astype(BF16))
             arrived.append(over_y(sent[-1], k))
-        chip = make_chip()
+        chip = make_chip(sent)
         total = chip[:held].astype(F32) + over_c(chip[held:]).astype(F32)
         if waits:
             arrived = [after(piece, *waits) for piece in arrived]
         for piece in arrived:
             total = total + piece.astype(F32)
-        return total, sent
+        return total, sent, (chip, *arrived)
 
     def rms(values):
         return lax.rsqrt(jnp.mean(values * values, axis=-1, keepdims=True) + 1e-05)
@@ -554,8 +798,10 @@
             jnp.concatenate([moved, near_small], axis=0),
         )
         step *= 2
-    layer_in = rotate(trade_z(after(inputs[:, 0, 0], near_small)).reshape(held, width)).astype(F32)
-    near_small = turn(jnp.stack(shifts(near_small)), 0).reshape(heads_size, 2, -1)
+    layer_in = rotate(trade_z(inputs[:, 0, 0]).reshape(held, width)).astype(F32)
+    near_small = turn(
+        jnp.stack([near_small] + [over_z(near_small, k) for k in range(1, depth)]), 0
+    ).reshape(heads_size, 2, -1)
     far_small = over_x(near_small)
     turned_small = jnp.stack([near_small, far_small])
     spread_small = jnp.where(x == 0, turned_small, jnp.stack([far_small, near_small]))
@@ -617,44 +863,50 @@
     )
     row_count = query_rows + 2 * key_rows
 
-    def spread_heads(block):
-        blocks = turn(jnp.stack(shifts(block)), 0)
+    def hidden_rows(place):
+        parts = [gate_weight, up_weight, down_weight]
+        size = down_weight.shape[0] // 2
+        return jnp.stack(
+            [lax.dynamic_slice_in_dim(p, place * size, size, 1).T for p in parts[:2]]
+            + [lax.dynamic_slice_in_dim(parts[2], place * size, size, 0)]
+        )
+
+    kept_pack = hidden_rows(c)
+    moved_pack = after(over_c(hidden_rows(1 - c)), far_small)
+    ffn_own = [in_order(kept_pack, moved_pack, 2)]
+    ffn_other = [over_x(ffn_own[0])]
+    ring_pack = jnp.where(
+        c != 1,
+        jnp.concatenate([kept_pack, moved_pack], axis=2),
+        jnp.concatenate([moved_pack, kept_pack], axis=2),
+    )
+    query_blocks = gather_z(after(query_weight.T, layer_in))
+    out_blocks = gather_z(after(output_weight, query_blocks))
+    ffn_own.append(over_z(after(ring_pack, out_blocks)))
+
+    def join_heads(blocks):
         kept = lax.dynamic_slice_in_dim(blocks, c * near, near, 0)
         moved = over_c(lax.dynamic_slice_in_dim(blocks, (1 - c) * near, near, 0))
         return in_order(kept, moved, 2).reshape(near * block_rows, half)
 
-    query_own = spread_heads(query_weight.T)
+    query_own = join_heads(query_blocks)
     kv_own = jnp.concatenate([pick_near(key_weight), pick_near(value_weight)], axis=0)
     both_own = jnp.concatenate([query_own, kv_own], axis=0)
-    both = jnp.concatenate([both_own, over_x(both_own)], axis=1)
-    project = jnp.concatenate([both, downs_t], axis=0)
-
-    pack_one = jnp.stack([after(gate_weight, near_small).T, after(up_weight, near_small).T])
-    own_one = [trade_c(pack_one, 1, 2)]
-    own_two = [trade_c(after(down_weight, near_small), 0, 1)]
-    other_one = [over_x(own_one[0])]
-    other_two = [over_x(own_two[0])]
-    project = after(project, other_one[0])
-
-    def next_block(*waits):
-        one, two = own_one[-1], own_two[-1]
-        if waits:
-            one, two = after(one, *waits), after(two, *waits)
-        own_one.append(over_z(one))
-        own_two.append(over_z(two))
+    project_own = jnp.concatenate([both_own, downs_t[:, :half]], axis=0)
+    project_other = jnp.concatenate([over_x(both_own), downs_t[:, half:]], axis=0)
+
+    def next_block():
+        ffn_own.append(over_z(ffn_own[-1]))
 
     def next_half():
-        place = len(other_one)
-        other_one.append(over_x(own_one[place]))
-        other_two.append(over_x(own_two[place]))
-
-    next_block(layer_in)
+        ffn_other.append(over_x(ffn_own[len(ffn_other)]))
 
     scale_one = rms(layer_in)
     normed = gather_tokens((layer_in * scale_one * gain_one).astype(BF16))
+    normed = (jnp.concatenate(normed[:2], axis=0), jnp.concatenate(normed[2:], axis=0))
 
     def project_rows(tokens):
-        flat = mm(project, tokens, 1, 1)
+        flat = mm(project_own, tokens[:, :half], 1, 1) + mm(project_other, tokens[:, half:], 1, 1)
         low = flat[row_count:].astype(BF16)
         return (flat[:row_count] + mm(lift, low, 0, 0)).astype(BF16), low
 
@@ -704,142 +956,165 @@
     seg_row = segment[None, :]
     seg_col = segment[:, None]
     rows_nat = to_natural(rows)
-    key_nat = jnp.transpose(rows_nat[query_rows:].reshape(-1, HD, length), (0, 2, 1))
-    key_nat = after(key_nat, own_one[1], own_two[1])
     next_block()
     next_half()
     saved = attend_forward(
-        last, order, seg_row, seg_col, rows_nat, key_nat, jnp.transpose(maps, (0, 2, 1))
+        last, order, seg_row, seg_col, rows_nat, jnp.transpose(maps, (0, 2, 1)),
+        (ffn_own[1],),
     )
     mixed = from_natural(saved[0])
 
-    out_own = spread_heads(after(output_weight, rows))
+    out_own = join_heads(after(out_blocks, ffn_other[0]))
     out_mat = jnp.concatenate([out_own, over_x(out_own)], axis=1)
     rank_rows = mm(out_down, mixed, 0, 0).astype(BF16)
     split = 2 * held
 
     def branch(part, *waits):
-        def make():
-            rows_in = after(mixed[:, part], *waits)
+        def make(*sent):
+            rows_in = after(mixed[:, part], *waits) if waits else mixed[:, part]
             return (mm(rows_in, out_mat, 0, 0) + mm(rank_rows[:, part], out_lift, 0, 0)).astype(BF16)
 
         return make
 
     chip_part, other_part = slice(0, split), slice(split, length)
-    branch_sum, _ = reduce_tokens(
-        branch(chip_part, own_one[2], own_two[2], other_one[1], other_two[1]), branch(other_part)
+    last_own = [over_z(ffn_own[2][:2])]
+    last_own.append(over_z(after(ffn_own[2][2:], last_own[0])))
+    next_half()
+    branch_sum, _, _ = reduce_tokens(
+        branch(chip_part), branch(other_part, ffn_own[2], ffn_other[1]), (ffn_other[2],)
     )
     middle = layer_in + branch_sum
-    next_block()
-    next_half()
-    next_half()
+    last_other = [over_x(part) for part in last_own]
 
     scale_two = rms(middle)
-    ffn_rows = gather_tokens((middle * scale_two * gain_two).astype(BF16))
-    ffn_rows = (ffn_rows[0], after(ffn_rows[1], own_one[3], other_one[2]))
-    grad_out = rotate(
-        trade_z(after(cotangent[:, 0, 0], own_two[3])).reshape(held, width)
-    )
-    grads = gather_tokens(grad_out)
-    own_gate, own_up = [jnp.concatenate([b[i] for b in own_one], axis=0) for i in range(2)]
-    other_gate, other_up = [jnp.concatenate([b[i] for b in other_one], axis=0) for i in range(2)]
-    own_down = jnp.concatenate(own_two, axis=0)
-    other_down = jnp.concatenate(other_two, axis=0)
-
-    def from_width(tokens, own, other):
-        return mm(tokens[:, :half], own, 1, 1) + mm(tokens[:, half:], other, 1, 1)
-
-    gates = [from_width(tokens, own_gate, other_gate).astype(BF16) for tokens in ffn_rows]
-    ups = [from_width(tokens, own_up, other_up).astype(BF16) for tokens in ffn_rows]
-
-    def activate(gate, up):
-        gate = gate.astype(F32)
-        return (gate * jax.nn.sigmoid(gate) * up.astype(F32)).astype(BF16)
-
-    hidden = [activate(gate, up) for gate, up in zip(gates, ups)]
-
-    def ffn_forward(part):
-        return lambda: jnp.concatenate(
-            [mm(hidden[part], own_down).astype(BF16), mm(hidden[part], other_down).astype(BF16)],
-            axis=1,
-        )
-
-    ffn_out, ffn_sent = reduce_tokens(ffn_forward(0), ffn_forward(1))
-    grads = (grads[0], after(grads[1], *ffn_sent))
-
-    def over_tokens(left, right):
-        total = mm(left[0], right[0], 0, 0)
-        for a, b in zip(left[1:], right[1:]):
-            total = total + mm(a, b, 0, 0)
-        return total.astype(BF16)
-
-    def send_other(left, right):
-        return over_x(over_tokens(left, [b[:, half:] for b in right]))
-
-    def keep_own(left, right):
-        return over_tokens(left, [b[:, :half] for b in right])
-
-    def add_up(kept, moved):
-        kept = jnp.split(kept, depth, axis=0)
-        moved = jnp.split(moved, depth, axis=0)
-        return [(a.astype(F32) + b.astype(F32)).astype(BF16) for a, b in zip(kept, moved)]
-
-    down_moved = send_other(hidden, grads)
-    grad_gates, grad_ups = [], []
-    for grad, gate, up in zip(grads, gates, ups):
-        grad_hidden = from_width(grad, own_down, other_down)
-        gate = gate.astype(F32)
-        sigmoid = jax.nn.sigmoid(gate)
-        grad_gates.append(
-            (grad_hidden * up.astype(F32) * sigmoid * (1.0 + gate * (1.0 - sigmoid))).astype(BF16)
-        )
-        grad_ups.append((grad_hidden * gate * sigmoid).astype(BF16))
-
-    def ffn_back(part):
-        return lambda: jnp.concatenate(
-            [
-                (mm(grad_gates[part], a) + mm(grad_ups[part], b)).astype(BF16)
-                for a, b in ((own_gate, own_up), (other_gate, other_up))
-            ],
-            axis=1,
-        )
-
-    grad_ffn, grad_ffn_sent = reduce_tokens(ffn_back(0), ffn_back(1))
-    ffn_out = after(ffn_out, *grad_ffn_sent)
+    ffn_pieces = gather_tokens((middle * scale_two * gain_two).astype(BF16))
+    ffn_pieces = ffn_pieces[:2] + after(ffn_pieces[2:], last_own[0])
+    ffn_rows = stack_rows(ffn_pieces)
+    grad_out = trade_z(after(cotangent[:, 0, 0], last_own[1]))
+    grad_out = rotate(after(grad_out, middle).reshape(held, width))
+    grads = stack_rows(gather_tokens(grad_out))
+    last_other[0] = after(last_other[0], ffn_rows)
+    own_gate, own_up, own_down = [
+        jnp.concatenate([block[i] for block in ffn_own] + [last_own[i // 2][i % 2]], axis=0)
+        for i in range(3)
+    ]
+    other_gate, other_up, other_down = [
+        jnp.concatenate([block[i] for block in ffn_other] + [last_other[i // 2][i % 2]], axis=0)
+        for i in range(3)
+    ]
+    chip_place = (0, split)
+    other_place = (split, length - split)
+    gates, ups, hidden = gate_forward(
+        ffn_rows, own_gate, other_gate, own_up, other_up, (last_other[1],)
+    )
+
+    def ffn_forward(place):
+        return lambda *sent: sum_products([hidden], [own_down], [other_down], *place)
+
+    swap = x.reshape(1).astype(jnp.int32)
+
+    def sum_x(value):
+        return lax.psum_scatter(value, "rows", scatter_dimension=0, tiled=False)
+
+    down_full = weight_grad_halves(hidden, grads, swap)
+    down_sums = sum_x(down_full).reshape(depth, -1, half)
+    ffn_out, ffn_sent, ffn_parts = reduce_tokens(ffn_forward(chip_place), ffn_forward(other_place))
+
+    grad_gates, grad_ups = gate_backward(
+        grads, own_down, other_down, gates, ups, (down_full, ffn_parts[0], *ffn_sent)
+    )
+
+    def ffn_back(place, wait):
+        return lambda sent=(): sum_products(
+            [grad_gates, grad_ups],
+            [own_gate, own_up],
+            [other_gate, other_up],
+            *place,
+            (*wait, *sent),
+        )
+
     output = trade_z(rotate((middle + ffn_out).astype(BF16)).reshape(depth, share, width))
-    gate_moved = send_other(grad_gates, ffn_rows)
-    up_moved = send_other(grad_ups, ffn_rows)
+    gate_full = weight_grad_halves(grad_gates, ffn_rows, swap, tuple(ffn_parts[1:]))
+    gate_sums = sum_x(gate_full).reshape(depth, -1, half)
+    up_full = weight_grad_halves(grad_ups, ffn_rows, swap, (gate_full,))
+    up_sums = sum_x(up_full).reshape(depth, -1, half)
+    down_traded = trade_z(turn(down_sums, 0))
+    grad_ffn, grad_ffn_sent, _ = reduce_tokens(
+        ffn_back(chip_place, ()),
+        ffn_back(other_place, ()),
+        (gate_full, up_full, down_traded),
+    )
 
     grad_mid_norm, gain_two_grad = norm_back(middle, gain_two, scale_two, grad_ffn)
     grad_middle = grad_out.astype(F32) + grad_mid_norm
 
-    down_kept = keep_own(hidden, grads)
-    gate_kept = keep_own(grad_gates, ffn_rows)
-    up_kept = keep_own(grad_ups, ffn_rows)
-
-    grad_branch = jnp.concatenate(gather_tokens(grad_middle.astype(BF16)), axis=0)
+    def halves(value):
+        middle_at = value.shape[-1] // 2
+        first, second = value[..., :middle_at], value[..., middle_at:]
+        return jnp.where(x == 0, first, second), jnp.where(x == 0, second, first)
+
+    grad_branch = stack_rows(gather_tokens(grad_middle.astype(BF16)))
     grad_olow = mm(out_lift, grad_branch, 1, 1).astype(BF16)
     grad_mixed = (mm(out_mat, grad_branch, 1, 1) + mm(out_down, grad_olow)).astype(BF16)
-    down_sums = add_up(down_kept, after(down_moved, grad_middle))
-    down_step = after(over_z(down_sums[1]), grad_branch)
-    down_step = (down_step.astype(F32) + down_sums[2].astype(F32)).astype(BF16)
-    down_step = over_z(down_step)
-    gate_sums = add_up(gate_kept, after(gate_moved, grad_branch))
+    gate_sums = after(gate_sums, grad_middle)
+    up_sums = after(up_sums, grad_branch)
+    gate_traded = trade_z(after(turn(gate_sums, 0), output))
+    up_shifted = [over_z(up_sums[depth - k], k) for k in range(1, depth)]
     out_lift_grad = mm(rank_rows, grad_branch)
     out_down_grad = mm(mixed, grad_olow, 1, 1)
-    out_weight_grad = mm(mixed, grad_branch).astype(BF16)
-
-    grad_mixed = after(grad_mixed, gate_sums[1:], output)
-    gate_shifted = [over_z(gate_sums[depth - k], k) for k in range(1, depth)]
+    out_grads = [mm(mixed, grad_branch[:, cut]) for cut in (slice(0, half), slice(half, width))]
+    down_lift = halves(out_down_grad)
+    out_halves = [
+        jnp.concatenate([a, b], axis=1).astype(BF16) for a, b in zip(out_grads, down_lift)
+    ]
+    out_moved = over_x(out_halves[1])
+
     grad_rows, maps_grad = attend_backward(
-        last, order, seg_row, seg_col, rows_nat, key_nat, maps, lift, saved, to_natural(grad_mixed)
-    )
-    grad_rows = after(from_natural(grad_rows), down_step, gate_shifted)
+        last, order, seg_row, seg_col, rows_nat, maps, lift, saved, to_natural(grad_mixed),
+        (out_moved, output),
+    )
+    grad_rows = after(from_natural(grad_rows), gate_traded, up_shifted)
+
+    quarter = half // 2
+    rank_own = rank // 4
+    maps_own = HD // 4
+
+    def part_of(value, place):
+        sizes = (quarter, rank_own, maps_own)
+        start = 0
+        parts = []
+        for size in sizes:
+            if start < value.shape[1]:
+                parts.append(lax.dynamic_slice_in_dim(value, start + place * size, size, 1))
+            start += 2 * size
+        return jnp.concatenate(parts, axis=1).astype(BF16)
+
+    def by_depth(value, height):
+        return value.reshape(near, height, value.shape[-1])
+
+    def collect(own_half, moved, blocks, *waits):
+        summed = own_half.astype(F32) + moved.astype(F32)
+
+        def ready(place):
+            return blocks(part_of(summed, place))
+
+        return shift_sum(in_order(ready(c), over_c(ready(1 - c)), 0), *waits)
 
     def project_back(part):
-        return lambda: mm(grad_rows[:, part], project, 0, 0).astype(BF16)
-
-    grad_normed, normed_sent = reduce_tokens(project_back(chip_part), project_back(other_part))
+        def make(*sent):
+            return jnp.concatenate(
+                [mm(grad_rows[:, part], weight, 0, 0).astype(BF16) for weight in (project_own, project_other)],
+                axis=1,
+            )
+
+        return make
+
+    grad_normed, normed_sent, _ = reduce_tokens(
+        project_back(chip_part), project_back(other_part)
+    )
+    grad_in_norm, gain_one_grad = norm_back(layer_in, gain_one, scale_one, grad_normed)
+    grad_in = rotate((grad_middle + grad_in_norm).astype(BF16)).reshape(depth, share, width)
+    input_grad = trade_z(grad_in)
 
     late_rows = after(grad_rows, *normed_sent)
     project_grad = [
@@ -852,44 +1127,13 @@
     kind = lax.broadcasted_iota(jnp.int32, (3, 1, row_count), 0)
     lift_grad = jnp.sum(jnp.where(owner_of == kind, lift_grad, 0.0), axis=0).T
 
-    def halves(value):
-        middle_at = value.shape[-1] // 2
-        first, second = value[..., :middle_at], value[..., middle_at:]
-        return jnp.where(x == 0, first, second), jnp.where(x == 0, second, first)
-
-    quarter = half // 2
-    rank_own = rank // 4
-    maps_own = HD // 4
-
-    def part_of(value, place):
-        sizes = (quarter, rank_own, maps_own)
-        start = 0
-        parts = []
-        for size in sizes:
-            if start < value.shape[1]:
-                parts.append(lax.dynamic_slice_in_dim(value, start + place * size, size, 1))
-            start += 2 * size
-        return jnp.concatenate(parts, axis=1).astype(BF16)
-
-    def by_depth(value, height):
-        return value.reshape(near, height, value.shape[-1])
-
-    def collect(own_half, other_half, blocks):
-        summed = own_half.astype(F32) + over_x(other_half.astype(BF16)).astype(F32)
-
-        def ready(place):
-            return blocks(part_of(summed, place))
-
-        return shift_sum(list(turn(in_order(ready(c), over_c(ready(1 - c)), 0), 0)))
-
-    down_lift = halves(out_down_grad)
     out_sum = collect(
-        *[
-            jnp.concatenate([out_weight_grad[:, i * half : (i + 1) * half], down_lift[i]], axis=1)
-            for i in range(2)
-        ],
+        out_halves[0],
+        after(out_moved, *normed_sent),
         lambda value: by_depth(value, block_rows),
-    )
+        grad_in,
+    )
+
     out_grad = out_sum[:, :quarter]
     output_down_grad = out_sum[:, quarter : quarter + rank_own]
 
@@ -899,11 +1143,15 @@
             [maps_grad.reshape(query_rows, HD), jnp.zeros((2 * key_rows, HD), F32)], axis=0
         )
     )
+    late_halves = [
+        jnp.concatenate(
+            [project_grad[i][:row_count], lift_halves[i], maps_halves[i]], axis=1
+        ).astype(BF16)
+        for i in range(2)
+    ]
     late_sum = collect(
-        *[
-            jnp.concatenate([project_grad[i][:row_count], lift_halves[i], maps_halves[i]], axis=1)
-            for i in range(2)
-        ],
+        late_halves[0],
+        after(over_x(late_halves[1]), grad_in),
         lambda value: jnp.concatenate(
             [
                 by_depth(value[:query_rows], block_rows),
@@ -926,28 +1174,24 @@
     while step < wide:
         kv_sum = (kv_sum.astype(F32) + over_y(kv_sum, step).astype(F32)).astype(BF16)
         step *= 2
-    kv_sum = turn(jnp.stack(shifts(kv_sum)), 0)
+    kv_sum = gather_z(after(kv_sum, input_grad))
     kv_sum = jnp.transpose(kv_sum, (2, 4, 0, 1, 3)).reshape(2, quarter + rank_own, KV * HD)
     kv_sum = kv_sum.astype(F32)
 
-    gate_total = gate_sums[0].astype(F32)
-    for block in gate_shifted:
-        gate_total = gate_total + block.astype(F32)
-    down_step = (down_step.astype(F32) + down_sums[3].astype(F32)).astype(BF16)
-    down_total = over_z(down_step).astype(F32) + down_sums[0].astype(F32)
-    up_total = ring_sum(add_up(up_kept, after(up_moved, *normed_sent)))
+    down_total = jnp.sum(after(down_traded, grad_in).astype(F32), axis=0)
+    gate_total = jnp.sum(after(gate_traded, grad_in).astype(F32), axis=0)
+    up_total = up_sums[0].astype(F32)
+    for block in after(up_shifted, grad_in):
+        up_total = up_total + block.astype(F32)
 
     def to_owner(total):
-        return trade_c(total.astype(BF16), 1, 0)
+        total = total.astype(BF16)
+        kept = lax.dynamic_slice_in_dim(total, c * quarter, quarter, 1)
+        return in_order(kept, over_c(lax.dynamic_slice_in_dim(total, (1 - c) * quarter, quarter, 1)), 0)
 
     down_grad = to_owner(down_total).astype(F32)
     gate_grad = to_owner(gate_total).T.astype(F32)
     up_grad = to_owner(up_total).T.astype(F32)
-
-    grad_in_norm, gain_one_grad = norm_back(layer_in, gain_one, scale_one, grad_normed)
-    input_grad = trade_z(
-        rotate((grad_middle + grad_in_norm).astype(BF16)).reshape(depth, share, width)
-    ).astype(F32)
 
     minor = jnp.concatenate(
         [
@@ -958,9 +1202,9 @@
         ],
         axis=0,
     )
-    minor = minor[:, :half] + over_x(minor[:, half:])
+    minor = minor[:, :half] + over_x(after(minor[:, half:], late_sum))
     minor = jnp.moveaxis(minor.reshape(-1, depth, wide, 2, half // (2 * heads_size)), 0, 3)
-    minor = shift_sum(list(turn(minor, 0)))
+    minor = shift_sum(minor)
     total = lax.dynamic_index_in_dim(minor, y, 0, False)
     for k in range(1, wide):
         total = total + over_y(lax.dynamic_index_in_dim(minor, y ^ k, 0, False), k)
@@ -970,7 +1214,7 @@
     minor = minor.T
     return (
         output[:, None, None],
-        input_grad[:, None, None],
+        input_grad[:, None, None].astype(F32),
         minor[:, 0],
         minor[:, 1],
         query_grad,

time: 1490 us -> 1380 us (0.926)
  matrix products: 380 us -> 85.8 us
  Pallas kernels: 145 us -> 397 us
  waiting for transfers between devices: 465 us -> 414 us
  starting transfers between devices: 120 us -> 91.4 us
    dot_general x58 -> x27, matrix products: 380 us -> 85.8 us  [mm(): lax.dot_general(left, right, (((left_dim,), (right_dim,)), ((), ())), pre...]
    pallas_call x2 -> x40, Pallas kernels: 145 us -> 397 us  [the longest x1 94.4 us: attend_backward(): pl.pallas_call(ignoring(backward_kernel, 22, len(waits)), grid_spec=pltpu...]
    ppermute x36 -> x19, waiting for transfers between devices: 256 us -> 176 us  [over_z(): lax.ppermute(value, 'heads', [(a * wide + b, (a + k) % depth * wide + b)...]
    ppermute x17 -> x11, waiting for transfers between devices: 113 us -> 52.2 us  [over_x(): return lax.ppermute(value, 'rows', SWAP)]
    all_to_all x4 -> x9, waiting for transfers between devices: 0.01 us -> 60 us  [trade_z(): lax.all_to_all(value, 'heads', split_axis=0, concat_axis=0, tiled=True, a...]
    ppermute x11, waiting for transfers between devices: 92.7 us -> 118 us  [over_y(): lax.ppermute(value, 'heads', [(a * wide + b, a * wide + (b ^ k)) for a in...]
    ppermute x36 -> x19, starting transfers between devices: 37.7 us -> 18.5 us  [over_z(): lax.ppermute(value, 'heads', [(a * wide + b, (a + k) % depth * wide + b)...]
    convert_element_type x12 -> x6, other arithmetic: 38.8 us -> 23.6 us  [the longest x1 8.18 us: body(): grad_branch = stack_rows(gather_tokens(grad_middle.astype(BF16)))]
  transfers between devices with their start and end apart: 94 -> 81, of which waited for: 33 -> 31; matrix products, arithmetic and copies ran while one was open for 46% -> 28% of each run, Pallas kernels for 10% -> 27%
where the time goes in v2:
time: 1380 us; the launch traced here: 1360 us
  waiting for transfers between devices  414 us (30%)
  Pallas kernels  397 us (29%)
  local copies, waits for them, and re-layouts  205 us (15%)
  other arithmetic  156 us (11%)
  starting transfers between devices  91.4 us (7%)
  matrix products  85.8 us (6%)
  between operations  17 us (1%)
    ppermute x19, waiting for transfers between devices, over_z(): lax.ppermute(value, 'heads', [(a * wide + b, (a + k) % depth * wide + b)...  176 us
    ppermute x11, waiting for transfers between devices, over_y(): lax.ppermute(value, 'heads', [(a * wide + b, a * wide + (b ^ k)) for a in...  118 us
    pallas_call x1, Pallas kernels, attend_backward(): pl.pallas_call(ignoring(backward_kernel, 22, len(waits)), grid_spec=pltpu...  94.4 us
    dot_general x27, matrix products, mm(): lax.dot_general(left, right, (((left_dim,), (right_dim,)), ((), ())), pre...  85.8 us
    pallas_call x4, Pallas kernels, sum_products(): dense_call(kernel, (2 * across, tokens // tall), [left] * count + [own] *...  77.6 us
    pallas_call x3, Pallas kernels, weight_grad_halves(): pl.pallas_call(kernel, grid_spec=pltpu.PrefetchScalarGridSpec(num_scalar_...  71.4 us
    unnamed x333, local copies, waits for them, and re-layouts  69.7 us
    all_to_all x9, waiting for transfers between devices, trade_z(): lax.all_to_all(value, 'heads', split_axis=0, concat_axis=0, tiled=True, a...  60 us
  transfers between devices with their start and end apart: 81, of which 31 were waited for; matrix products, arithmetic and copies ran while one was open for 28% of the time, Pallas kernels for 27%

profile of v2, /device:TPU:0, one launch (start us, length us, event | category | flops | bytes accessed | tf_op | source)
XLA Modules:
  0.0 1364.9 jit_solution(18334571237888476785)
XLA Ops:
  12.3 6.5 all-to-all-start
  42.0 13.4 collective-permute-done.7
  55.4 17.9 %collective-permute-done.6 = bf16[2,2,9344]{2,1,0:T(2,128)(2,1)S(1)} collective-permute-done((bf16[2,2,9344]{2,1,0:T(2,128)(2,1)S(1)}, bf16[2,2,9344]{2,1,0:T(2,128)(2,1)S(1)}, u32[]{:S(2)}, u32[]{:S(2)}) %collective-permute-start.6) | collective-permute-done | bytes 74784 | tf_op jit(solution)/shard_map/ppermute | solution.py:699
  88.6 6.2 broadcast_select_fusion
  96.7 4.5 fusion.97
  103.4 4.2 all-to-all-start.1
  114.1 18.0 %all-to-all-done.1.refs_1_ = bf16[4,256,512]{2,1,0:T(8,128)(2,1)} async-done(((bf16[4,256,512]{2,1,0:T(8,128)(2,1)}), bf16[4,256,512]{2,1,0:T(8,128)(2,1)}, u32[]{:S(2)}, u32[]{:S(2)}) %all-to-all-start.1) | async-done | bytes 1048608 | tf_op jit(solution)/shard_map/all_to_all | solution.py:707
  156.0 7.0 all-to-all-done.2.refs_1_.refs_0_
  175.6 24.3 %collective-permute-done.10 = bf16[768,1024]{1,0:T(8,128)(2,1)} collective-permute-done((bf16[768,1024]{1,0:T(8,128)(2,1)}, bf16[768,1024]{1,0:T(8,128)(2,1)}, u32[]{:S(2)}, u32[]{:S(2)}) %collective-permute-start.10) | collective-permute-done | bytes 1572896 | tf_op jit(solution)/shard_map/ppermute | solution.py:642
  210.3 4.5 fusion.16
  214.8 20.3 %collective-permute-done.14.refs_11_ = bf16[3,512,1024]{2,1,0:T(8,128)(2,1)} collective-permute-done((bf16[3,512,1024]{2,1,0:T(8,128)(2,1)}, bf16[3,512,1024]{2,1,0:T(8,128)(2,1)}, u32[]{:S(2)}, u32[]{:S(2)}) %collective-permute-start.14) | collective-permute-done | bytes 3145760 | tf_op jit(solution)/shard_map/ppermute | solution.py:699
  240.7 50.8 %attend_forward.1 = (bf16[512,2048]{1,0:T(8,128)(2,1)S(1)}, f32[8,2048]{1,0:T(8,128)S(1)}, f32[8,2048]{1,0:T(8,128)S(1)}, bf16[8,128,2048]{2,1,0:T(8,128)(2,1)S(...) custom-call(s32[16]{0:T(128)S(1)} %slice_reduce_fusion.refs_0_, ...), custom_call_target="tpu_custom_call" | custom-call | flops 17367040000 | bytes 6553600 | tf_op jit(solution)/shard_map/attend_forward/pallas_call | solution.py:266
  293.0 4.6 fusion.77
  298.4 5.0 collective-permute-done.20.refs_2_
  307.0 6.7 add_convert_fusion
  318.0 4.2 add_convert_fusion.1
  327.7 4.2 slice_bitcast_fusion.36
  331.9 35.4 %collective-permute-done.27.refs_2_.refs_1_ = bf16[2,512,1024]{2,1,0:T(8,128)(2,1)} collective-permute-done((bf16[2,512,1024]{2,1,0:T(8,128)(2,1)S(1)}, bf16[2,512,1024]{2,1,0:T(8,128)(2,1)}, u32[]{:S(2)}, u32[]{:S(2)}) %collective-permute-start.27) | collective-permute-done | bytes 2097184 | tf_op jit(solution)/shard_map/ppermute | solution.py:699
  367.4 26.8 %collective-permute-done.29.refs_1_ = bf16[1,512,1024]{2,1,0:T(8,128)(2,1)} collective-permute-done((bf16[1,512,1024]{2,1,0:T(8,128)(2,1)}, bf16[1,512,1024]{2,1,0:T(8,128)(2,1)}, u32[]{:S(2)}, u32[]{:S(2)}) %collective-permute-start.29) | collective-permute-done | bytes 1048608 | tf_op jit(solution)/shard_map/ppermute | solution.py:699
  394.2 4.5 all-to-all-start.4
  400.2 4.1 multiply_reduce_fusion.4
  412.7 41.0 %collective-permute-done.25.refs_0_ = bf16[512,2048]{1,0:T(8,128)(2,1)} collective-permute-done((bf16[512,2048]{1,0:T(8,128)(2,1)}, bf16[512,2048]{1,0:T(8,128)(2,1)}, u32[]{:S(2)}, u32[]{:S(2)}) %collective-permute-start.25) | collective-permute-done | bytes 2097184 | tf_op jit(solution)/shard_map/ppermute | solution.py:692
  479.2 10.2 stack_rows.3.refs_1_.refs_0_.right_ref
  489.4 16.5 %collective-permute-done.35.refs_2_ = bf16[512,2048]{1,0:T(8,128)(2,1)} collective-permute-done((bf16[512,2048]{1,0:T(8,128)(2,1)S(1)}, bf16[512,2048]{1,0:T(8,128)(2,1)}, u32[]{:S(2)}, u32[]{:S(2)}) %collective-permute-start.35) | collective-permute-done | bytes 2097184 | tf_op jit(solution)/shard_map/ppermute | solution.py:692
  514.8 41.5 %gate_forward.1 = (bf16[2048,2048]{1,0:T(8,128)(2,1)}, bf16[2048,2048]{1,0:T(8,128)(2,1)}, bf16[2048,2048]{1,0:T(8,128)(2,1)}) custom-call(bf16[2048,2048]{1,0:T(8,128)(2,1)} %stack_rows.3.refs_1_.refs_0_.right_ref, bf16[2048,1024]{1,0:T(8,128)(2,1)S(1)} %copy-done.2, bf16[2048,1024]{1,0:T(8,128)(2,1)} %pad_maximum_fusion.1.refs_2_.refs_4_, ...), custom_call_target="tpu_custom_call" | custom-call | flops 11453246464 | bytes 4294967 | tf_op jit(solution)/shard_map/gate_forward/pallas_call | solution.py:580
  556.3 10.1 stack_rows.4.right_ref.refs_0_
  566.4 23.8 %weight_grad_halves.3.refs_5_ = bf16[2,2048,1024]{2,1,0:T(8,128)(2,1)} custom-call(s32[1]{0:T(128)} %bitcast.82.swap_ref, bf16[2048,2048]{1,0:T(8,128)(2,1)} %get-tuple-element.45.refs_0_.left_ref, bf16[2048,2048]{1,0:T(8,128)(2,1)} %stack_rows.4.right_ref.refs_0_), custom_call_target="tpu_custom_call" | custom-call | flops 4294967296 | bytes 2097152 | tf_op jit(solution)/shard_map/weight_grad_halves/pallas_call | solution.py:474
  591.8 4.1 pad_maximum_fusion.4.refs_1_
  598.2 13.2 sum_products.5
  618.5 13.2 sum_products.4.refs_6_
  633.8 30.4 %gate_backward.1 = (bf16[2048,2048]{1,0:T(8,128)(2,1)}, bf16[2048,2048]{1,0:T(8,128)(2,1)}) custom-call(bf16[2048,2048]{1,0:T(8,128)(2,1)} %stack_rows.4.right_ref.refs_0_, bf16[2048,1024]{1,0:T(8,128)(2,1)} %pad_maximum_fusion.4.refs_1_, bf16[2048,1024]{1,0:T(8,128)(2,1)} %pad_maximum_fusion.5.refs_2_, bf16[2048,2048]{1,0:T(8,128)(2,1)} %get-tuple-element.46.refs_3_, ...), custom_call_target="tpu_custom_call" | custom-call | flops 5726623232 | bytes 2147483 | tf_op jit(solution)/shard_map/gate_backward/pallas_call | solution.py:598
  664.9 23.8 %weight_grad_halves.4.refs_0_.refs_1_ = bf16[2,2048,1024]{2,1,0:T(8,128)(2,1)} custom-call(s32[1]{0:T(128)} %bitcast.82.swap_ref, bf16[2048,2048]{1,0:T(8,128)(2,1)} %get-tuple-element.48.refs_0_.left_ref, bf16[2048,2048]{1,0:T(8,128)(2,1)} %stack_rows.3.refs_1_.refs_0_.right_ref, bf16[512,2048]{1,0:T(8,128)(2,1)S(1)} %collective-permute-done.33.refs_0_), custom_call_target="tpu_custom_call" | custom-call | flops 4294967296 | bytes 2097152 | tf_op jit(solution)/shard_map/weight_grad_halves/pallas_call | solution.py:474
  688.8 23.9 %weight_grad_halves.5.refs_2_ = bf16[2,2048,1024]{2,1,0:T(8,128)(2,1)} custom-call(s32[1]{0:T(128)} %bitcast.82.swap_ref, bf16[2048,2048]{1,0:T(8,128)(2,1)} %get-tuple-element.49.refs_1_.left_ref, bf16[2048,2048]{1,0:T(8,128)(2,1)} %stack_rows.3.refs_1_.refs_0_.right_ref, bf16[2,2048,1024]{2,1,0:T(8,128)(2,1)} %weight_grad_halves.4.refs_0_.refs_1_), custom_call_target="tpu_custom_call" | custom-call | flops 4294967296 | bytes 2097152 | tf_op jit(solution)/shard_map/weight_grad_halves/pallas_call | solution.py:474
  717.7 5.1 all-to-all-start.5
  722.8 25.2 %sum_products.6 = bf16[1024,2048]{1,0:T(8,128)(2,1)S(1)} custom-call(bf16[2048,2048]{1,0:T(8,128)(2,1)} %get-tuple-element.48.refs_0_.left_ref, bf16[2048,2048]{1,0:T(8,128)(2,1)} %get-tuple-element.49.refs_1_.left_ref, bf16[2048,1024]{1,0:T(8,128)(2,1)} %pad_maximum_fusion.refs_1_.refs_2_, bf16[2048,1024]{1,0:T(8,128)(2,1)} %pad_maximum_fusion.2.refs_3_, ...), custom_call_target="tpu_custom_call" | custom-call | flops 5726623232 | bytes 2147483 | tf_op jit(solution)/shard_map/sum_products/pallas_call | solution.py:624
  748.4 4.1 collective-permute-done.37
  755.0 25.9 %sum_products.7 = bf16[1024,2048]{1,0:T(8,128)(2,1)} custom-call(bf16[2048,2048]{1,0:T(8,128)(2,1)} %get-tuple-element.48.refs_0_.left_ref, bf16[2048,2048]{1,0:T(8,128)(2,1)} %get-tuple-element.49.refs_1_.left_ref, bf16[2048,1024]{1,0:T(8,128)(2,1)} %pad_maximum_fusion.refs_1_.refs_2_, bf16[2048,1024]{1,0:T(8,128)(2,1)} %pad_maximum_fusion.2.refs_3_, ...), custom_call_target="tpu_custom_call" | custom-call | flops 5726623232 | bytes 2147483 | tf_op jit(solution)/shard_map/sum_products/pallas_call | solution.py:624
  786.3 14.9 %collective-permute-done.39.refs_0_ = bf16[512,2048]{1,0:T(8,128)(2,1)} collective-permute-done((bf16[512,2048]{1,0:T(8,128)(2,1)S(1)}, bf16[512,2048]{1,0:T(8,128)(2,1)}, u32[]{:S(2)}, u32[]{:S(2)}) %collective-permute-start.39) | collective-permute-done | bytes 2097184 | tf_op jit(solution)/shard_map/ppermute | solution.py:692
  801.3 14.9 %all-to-all-done.5.refs_3_.refs_0_ = bf16[4,512,1024]{2,1,0:T(8,128)(2,1)} async-done(((bf16[4,512,1024]{2,1,0:T(8,128)(2,1)}), bf16[4,512,1024]{2,1,0:T(8,128)(2,1)}, u32[]{:S(2)}, u32[]{:S(2)}) %all-to-all-start.5) | async-done | bytes 4194336 | tf_op jit(solution)/shard_map/all_to_all | solution.py:707
  816.2 5.6 multiply_reduce_fusion
  823.6 8.2 fusion.96
  839.5 39.2 %collective-permute-done.41.refs_2_ = bf16[512,2048]{1,0:T(8,128)(2,1)} collective-permute-done((bf16[512,2048]{1,0:T(8,128)(2,1)}, bf16[512,2048]{1,0:T(8,128)(2,1)}, u32[]{:S(2)}, u32[]{:S(2)}) %collective-permute-start.41) | collective-permute-done | bytes 2097184 | tf_op jit(solution)/shard_map/ppermute | solution.py:692
  889.2 4.8 all-to-all-start.6
  894.1 10.2 stack_rows.5.refs_1_
  904.3 5.6 convolution_convert_fusion
  913.0 4.5 fusion.31
  929.4 10.0 add_convert_fusion.4.refs_13_
  939.5 4.6 collective-permute-done.43
  957.3 94.4 %attend_backward.1 = (bf16[800,2048]{1,0:T(8,128)(2,1)S(1)}, f32[8,64,64]{2,1,0:T(8,128)S(1)}) custom-call(s32[16]{0:T(128)S(1)} %copy-done.29, s32[16]{0:T(128)S(1)} %copy-done.31, s32[1,2048]{1,0:T(1,128)S(1)} %copy-done.27, s32[2048,1]{1,0:T(8,128)S(1)} %copy-done.21, s32[2048,1]{1,0:T(8,128)S(1)} %copy-done.21, bf16[768,2048]{1,0:T(8,128)(2,1)S(1)} %copy-done.19, ...), custom_call_target="tpu_custom_call" | custom-call | flops 34406400000 | bytes 9830400 | tf_op jit(solution)/shard_map/attend_backward/pallas_call | solution.py:342
  1054.1 24.0 %collective-permute-done.45.refs_3_.refs_1_ = bf16[512,1024]{1,0:T(8,128)(2,1)} collective-permute-done((bf16[512,1024]{1,0:T(8,128)(2,1)}, bf16[512,1024]{1,0:T(8,128)(2,1)}, u32[]{:S(2)}, u32[]{:S(2)}) %collective-permute-start.45) | collective-permute-done | bytes 1048608 | tf_op jit(solution)/shard_map/ppermute | solution.py:699
  1079.4 4.0 convolution_convert_fusion.3
  1105.6 4.5 fusion.39
  1133.4 4.0 fusion.41
  1151.1 16.3 %collective-permute-done.50 = bf16[768,1060]{0,1:T(8,128)(2,1)} collective-permute-done((bf16[768,1060]{0,1:T(8,128)(2,1)}, bf16[768,1060]{0,1:T(8,128)(2,1)}, u32[]{:S(2)}, u32[]{:S(2)}) %collective-permute-start.50) | collective-permute-done | bytes 1628192 | tf_op jit(solution)/shard_map/ppermute | solution.py:642
  1171.2 7.4 multiply_reduce_fusion.1
  1185.0 5.3 all-to-all-start.7
  1199.3 4.4 reduce_sum.95
  1203.7 4.4 reduce_sum.94
  1231.3 4.1 maximum_select_fusion.5
  1255.6 8.5 collective-permute-done.54
  1264.1 21.4 %collective-permute-done.53 = bf16[384,530]{1,0:T(8,128)(2,1)} collective-permute-done((bf16[384,530]{1,0:T(8,128)(2,1)}, bf16[384,530]{1,0:T(8,128)(2,1)}, u32[]{:S(2)}, u32[]{:S(2)}) %collective-permute-start.53) | collective-permute-done | bytes 407072 | tf_op jit(solution)/shard_map/ppermute | solution.py:699
  1313.5 4.3 all-to-all-start.8
  1322.6 4.1 bitcast_convert_fusion
  1326.7 20.0 %all-to-all-done.8 = bf16[4,2,2,64,514]{4,3,1,2,0:T(8,128)(2,1)} async-done(((bf16[4,2,2,64,514]{4,3,1,2,0:T(8,128)(2,1)}), bf16[4,2,2,64,514]{4,3,1,2,0:T(8,128)(2,1)}, u32[]{:S(2)}, u32[]{:S(2)}) %all-to-all-start.8) | async-done | bytes 1052704 | tf_op jit(solution)/shard_map/all_to_all | solution.py:707
  (728 shorter events, 409.1 us)
Async XLA Ops:
  12.3 83.0 %all-to-all-start = ((bf16[4,128,2048]{2,1,0:T(8,128)(2,1)}), bf16[4,128,2048]{2,1,0:T(8,128)(2,1)S(1)}, u32[]{:S(2)}, u32[]{:S(2)}) async-start(bf16[4,128,2048]{2,1,0:T(8,128)(2,1)} %bitcast.324), calls=%async_computation | async-start | bytes 4194304 | tf_op jit(solution)/shard_map/all_to_all | solution.py:707
  22.4 60.9 %collective-permute-start.1 = (bf16[128,512]{1,0:T(8,128)(2,1)}, bf16[128,512]{1,0:T(8,128)(2,1)}, u32[]{:S(2)}, u32[]{:S(2)}) collective-permute-start(bf16[128,512]{1,0:T(8,128)(2,1)} %get-tuple-element.260), channel_id=1, source_target_pairs={{0,1},{1,0},{2,3},{3,2},{4,5},{5,4},{6,7},{7,6},{8,9},{9,8},{10,11... | collective-permute-start | bytes 393224 | tf_op jit(solution)/shard_map/ppermute | solution.py:646
  23.6 61.6 %collective-permute-start.2 = (bf16[128,512]{1,0:T(8,128)(2,1)}, bf16[128,512]{1,0:T(8,128)(2,1)}, u32[]{:S(2)}, u32[]{:S(2)}) collective-permute-start(bf16[128,512]{1,0:T(8,128)(2,1)} %get-tuple-element.262), channel_id=1, source_target_pairs={{0,1},{1,0},{2,3},{3,2},{4,5},{5,4},{6,7},{7,6},{8,9},{9,8},{10,11... | collective-permute-start | bytes 393224 | tf_op jit(solution)/shard_map/ppermute | solution.py:646
  36.9 18.6 %collective-permute-start.7 = (bf16[2,2,9344]{2,1,0:T(2,128)(2,1)S(1)}, bf16[2,2,9344]{2,1,0:T(2,128)(2,1)S(1)}, u32[]{:S(2)}, u32[]{:S(2)}) collective-permute-start(bf16[2,2,9344]{2,1,0:T(2,128)(2,1)S(1)} %broadcast_select_fusion.3), channel_id=1, source_target_pairs={{0,12},{2,14},{4,0},{6,2},{8,4},{10,6},{12,8},{14,10},{1,13},{3,15... | collective-permute-start | bytes 224264 | tf_op jit(solution)/shard_map/ppermute | solution.py:699
  40.7 32.7 %collective-permute-start.6 = (bf16[2,2,9344]{2,1,0:T(2,128)(2,1)S(1)}, bf16[2,2,9344]{2,1,0:T(2,128)(2,1)S(1)}, u32[]{:S(2)}, u32[]{:S(2)}) collective-permute-start(bf16[2,2,9344]{2,1,0:T(2,128)(2,1)S(1)} %broadcast_select_fusion.3), channel_id=1, source_target_pairs={{0,8},{2,10},{4,12},{6,14},{8,0},{10,2},{12,4},{14,6},{1,9},{3,11}... | collective-permute-start | bytes 224264 | tf_op jit(solution)/shard_map/ppermute | solution.py:699
  40.7 32.7 %collective-permute-start.5 = (bf16[2,2,9344]{2,1,0:T(2,128)(2,1)S(1)}, bf16[2,2,9344]{2,1,0:T(2,128)(2,1)S(1)}, u32[]{:S(2)}, u32[]{:S(2)}) collective-permute-start(bf16[2,2,9344]{2,1,0:T(2,128)(2,1)S(1)} %broadcast_select_fusion.3), channel_id=1, source_target_pairs={{0,4},{2,6},{4,8},{6,10},{8,12},{10,14},{12,0},{14,2},{1,5},{3,7},... | collective-permute-start | bytes 224264 | tf_op jit(solution)/shard_map/ppermute | solution.py:699
  55.4 33.1 %collective-permute-start.13 = (bf16[3,512,512]{2,1,0:T(8,128)(2,1)}, bf16[3,512,512]{2,1,0:T(8,128)(2,1)}, u32[]{:S(2)}, u32[]{:S(2)}) collective-permute-start(bf16[3,512,512]{2,1,0:T(8,128)(2,1)} %pad_maximum_fusion.17), channel_id=1, source_target_pairs={{0,1},{1,0},{2,3},{3,2},{4,5},{5,4},{6,7},{7,6},{8,9},{9,8},{10,11... | collective-permute-start | bytes 4718600 | tf_op jit(solution)/shard_map/ppermute | solution.py:646
  94.8 71.4 %collective-permute-start.15 = (bf16[3,512,1024]{2,1,0:T(8,128)(2,1)}, bf16[3,512,1024]{2,1,0:T(8,128)(2,1)}, u32[]{:S(2)}, u32[]{:S(2)}) collective-permute-start(bf16[3,512,1024]{2,1,0:T(8,128)(2,1)} %get-tuple-element.185), channel_id=1, source_target_pairs={{0,16},{16,0},{1,17},{17,1},{2,18},{18,2},{3,19},{19,3},{4,20},{20... | collective-permute-start | bytes 9437192 | tf_op jit(solution)/shard_map/ppermute | solution.py:642
  103.4 28.7 %all-to-all-start.1 = ((bf16[4,256,512]{2,1,0:T(8,128)(2,1)}), bf16[4,256,512]{2,1,0:T(8,128)(2,1)}, u32[]{:S(2)}, u32[]{:S(2)}) async-start(bf16[4,256,512]{2,1,0:T(8,128)(2,1)} %broadcast_in_dim.53), calls=%async_computation.1 | async-start | bytes 2097152 | tf_op jit(solution)/shard_map/all_to_all | solution.py:707
  109.5 55.6 %collective-permute-start.11 = (bf16[512,2048]{1,0:T(8,128)(2,1)}, bf16[512,2048]{1,0:T(8,128)(2,1)}, u32[]{:S(2)}, u32[]{:S(2)}) collective-permute-start(bf16[512,2048]{1,0:T(8,128)(2,1)} %multiply_convert_fusion.1), channel_id=1, source_target_pairs={{0,2},{2,0},{4,6},{6,4},{8,10},{10,8},{12,14},{14,12},{1,3},{3,1},... | collective-permute-start | bytes 6291464 | tf_op jit(solution)/shard_map/ppermute | solution.py:692
  134.1 28.9 %all-to-all-start.2 = ((bf16[4,256,512]{2,1,0:T(8,128)(2,1)}), bf16[4,256,512]{2,1,0:T(8,128)(2,1)S(1)}, u32[]{:S(2)}, u32[]{:S(2)}) async-start(bf16[4,256,512]{2,1,0:T(8,128)(2,1)} %broadcast_in_dim.88), calls=%async_computation.2 | async-start | bytes 2097152 | tf_op jit(solution)/shard_map/all_to_all | solution.py:707
  144.8 30.8 %collective-permute-start.9 = (bf16[512,2048]{1,0:T(8,128)(2,1)}, bf16[512,2048]{1,0:T(8,128)(2,1)}, u32[]{:S(2)}, u32[]{:S(2)}) collective-permute-start(bf16[512,2048]{1,0:T(8,128)(2,1)} %multiply_convert_fusion.1), channel_id=1, source_target_pairs={{0,1},{1,0},{2,3},{3,2},{4,5},{5,4},{6,7},{7,6},{8,9},{9,8},{10,11... | collective-permute-start | bytes 6291464 | tf_op jit(solution)/shard_map/ppermute | solution.py:646
  153.9 46.0 %collective-permute-start.10 = (bf16[768,1024]{1,0:T(8,128)(2,1)}, bf16[768,1024]{1,0:T(8,128)(2,1)}, u32[]{:S(2)}, u32[]{:S(2)}) collective-permute-start(bf16[768,1024]{1,0:T(8,128)(2,1)} %pad_maximum_fusion.16), channel_id=1, source_target_pairs={{0,16},{16,0},{1,17},{17,1},{2,18},{18,2},{3,19},{19,3},{4,20},{20... | collective-permute-start | bytes 4718600 | tf_op jit(solution)/shard_map/ppermute | solution.py:642
  163.9 71.2 %collective-permute-start.14 = (bf16[3,512,1024]{2,1,0:T(8,128)(2,1)}, bf16[3,512,1024]{2,1,0:T(8,128)(2,1)}, u32[]{:S(2)}, u32[]{:S(2)}) collective-permute-start(bf16[3,512,1024]{2,1,0:T(8,128)(2,1)} %after.29), channel_id=1, source_target_pairs={{0,4},{2,6},{4,8},{6,10},{8,12},{10,14},{12,0},{14,2},{1,5},{3,7},... | collective-permute-start | bytes 9437192 | tf_op jit(solution)/shard_map/ppermute | solution.py:699
  165.2 42.9 %collective-permute-start.12 = (bf16[512,2048]{1,0:T(8,128)(2,1)}, bf16[512,2048]{1,0:T(8,128)(2,1)}, u32[]{:S(2)}, u32[]{:S(2)}) collective-permute-start(bf16[512,2048]{1,0:T(8,128)(2,1)} %collective-permute-done.11), channel_id=1, source_target_pairs={{0,1},{1,0},{2,3},{3,2},{4,5},{5,4},{6,7},{7,6},{8,9},{9,8},{10,11... | collective-permute-start | bytes 6291464 | tf_op jit(solution)/shard_map/ppermute | solution.py:646
  174.1 132.9 %collective-permute-start.17 = (bf16[512,1024]{1,0:T(8,128)(2,1)}, bf16[512,1024]{1,0:T(8,128)(2,1)}, u32[]{:S(2)}, u32[]{:S(2)}) collective-permute-start(bf16[512,1024]{1,0:T(8,128)(2,1)} %maximum_select_fusion.8), channel_id=1, source_target_pairs={{0,16},{16,0},{1,17},{17,1},{2,18},{18,2},{3,19},{19,3},{4,20},{20... | collective-permute-start | bytes 3145736 | tf_op jit(solution)/shard_map/ppermute | solution.py:642
  235.1 68.4 %collective-permute-start.20 = (bf16[3,512,1024]{2,1,0:T(8,128)(2,1)}, bf16[3,512,1024]{2,1,0:T(8,128)(2,1)S(1)}, u32[]{:S(2)}, u32[]{:S(2)}) collective-permute-start(bf16[3,512,1024]{2,1,0:T(8,128)(2,1)} %collective-permute-done.14.refs_11_), channel_id=1, source_target_pairs={{0,16},{16,0},{1,17},{17,1},{2,18},{18,2},{3,19},{19,3},{4,20},{20... | collective-permute-start | bytes 9437192 | tf_op jit(solution)/shard_map/ppermute | solution.py:642
  236.6 70.4 %collective-permute-start.19 = (bf16[3,512,1024]{2,1,0:T(8,128)(2,1)}, bf16[3,512,1024]{2,1,0:T(8,128)(2,1)}, u32[]{:S(2)}, u32[]{:S(2)}) collective-permute-start(bf16[3,512,1024]{2,1,0:T(8,128)(2,1)} %collective-permute-done.14.refs_11_), channel_id=1, source_target_pairs={{0,4},{2,6},{4,8},{6,10},{8,12},{10,14},{12,0},{14,2},{1,5},{3,7},... | collective-permute-start | bytes 9437192 | tf_op jit(solution)/shard_map/ppermute | solution.py:699
  317.1 50.1 %collective-permute-start.27 = (bf16[2,512,1024]{2,1,0:T(8,128)(2,1)S(1)}, bf16[2,512,1024]{2,1,0:T(8,128)(2,1)}, u32[]{:S(2)}, u32[]{:S(2)}) collective-permute-start(bf16[2,512,1024]{2,1,0:T(8,128)(2,1)S(1)} %slice.536), channel_id=1, source_target_pairs={{0,4},{2,6},{4,8},{6,10},{8,12},{10,14},{12,0},{14,2},{1,5},{3,7},... | collective-permute-start | bytes 6291464 | tf_op jit(solution)/shard_map/ppermute | solution.py:699
  317.4 81.3 %collective-permute-start.23 = (bf16[3,512,1024]{2,1,0:T(8,128)(2,1)}, bf16[3,512,1024]{2,1,0:T(8,128)(2,1)}, u32[]{:S(2)}, u32[]{:S(2)}) collective-permute-start(bf16[3,512,1024]{2,1,0:T(8,128)(2,1)} %collective-permute-done.19.refs_1_), channel_id=1, source_target_pairs={{0,16},{16,0},{1,17},{17,1},{2,18},{18,2},{3,19},{19,3},{4,20},{20... | collective-permute-start | bytes 9437192 | tf_op jit(solution)/shard_map/ppermute | solution.py:642
  324.7 74.0 %collective-permute-start.22 = (bf16[512,2048]{1,0:T(8,128)(2,1)}, bf16[512,2048]{1,0:T(8,128)(2,1)}, u32[]{:S(2)}, u32[]{:S(2)}) collective-permute-start(bf16[512,2048]{1,0:T(8,128)(2,1)} %add_convert_fusion.8), channel_id=1, source_target_pairs={{0,2},{2,0},{4,6},{6,4},{8,10},{10,8},{12,14},{14,12},{1,3},{3,1},... | collective-permute-start | bytes 6291464 | tf_op jit(solution)/shard_map/ppermute | solution.py:692
  327.7 71.0 %collective-permute-start.18 = (bf16[512,2048]{1,0:T(8,128)(2,1)}, bf16[512,2048]{1,0:T(8,128)(2,1)}, u32[]{:S(2)}, u32[]{:S(2)}) collective-permute-start(bf16[512,2048]{1,0:T(8,128)(2,1)} %slice.530), channel_id=1, source_target_pairs={{0,1},{1,0},{2,3},{3,2},{4,5},{5,4},{6,7},{7,6},{8,9},{9,8},{10,11... | collective-permute-start | bytes 6291464 | tf_op jit(solution)/shard_map/ppermute | solution.py:646
  367.3 26.9 %collective-permute-start.29 = (bf16[1,512,1024]{2,1,0:T(8,128)(2,1)}, bf16[1,512,1024]{2,1,0:T(8,128)(2,1)}, u32[]{:S(2)}, u32[]{:S(2)}) collective-permute-start(bf16[1,512,1024]{2,1,0:T(8,128)(2,1)} %after.35), channel_id=1, source_target_pairs={{0,4},{2,6},{4,8},{6,10},{8,12},{10,14},{12,0},{14,2},{1,5},{3,7},... | collective-permute-start | bytes 3145736 | tf_op jit(solution)/shard_map/ppermute | solution.py:699
  394.2 59.5 %all-to-all-start.4 = ((bf16[4,128,2048]{2,1,0:T(8,128)(2,1)}), bf16[4,128,2048]{2,1,0:T(8,128)(2,1)}, u32[]{:S(2)}, u32[]{:S(2)}) async-start(bf16[4,128,2048]{2,1,0:T(8,128)(2,1)} %after.36), calls=%async_computation.4 | async-start | bytes 4194304 | tf_op jit(solution)/shard_map/all_to_all | solution.py:707
  398.6 314.0 %reduce-scatter.4.cloned.1.call-start = ((), (), s32[]{:S(2)}) async-start(), calls=%async_computation.12 | async-start | bytes 12582912 | tf_op jit(solution)/shard_map/reduce_scatter | solution.py:1017
  407.0 46.7 %collective-permute-start.25 = (bf16[512,2048]{1,0:T(8,128)(2,1)}, bf16[512,2048]{1,0:T(8,128)(2,1)}, u32[]{:S(2)}, u32[]{:S(2)}) collective-permute-start(bf16[512,2048]{1,0:T(8,128)(2,1)} %multiply_convert_fusion.refs_0_), channel_id=1, source_target_pairs={{0,2},{2,0},{4,6},{6,4},{8,10},{10,8},{12,14},{14,12},{1,3},{3,1},... | collective-permute-start | bytes 6291464 | tf_op jit(solution)/shard_map/ppermute | solution.py:692
  412.1 77.3 %collective-permute-start.28 = (bf16[2,512,1024]{2,1,0:T(8,128)(2,1)}, bf16[2,512,1024]{2,1,0:T(8,128)(2,1)}, u32[]{:S(2)}, u32[]{:S(2)}) collective-permute-start(bf16[2,512,1024]{2,1,0:T(8,128)(2,1)} %collective-permute-done.27.refs_2_.refs_1_), channel_id=1, source_target_pairs={{0,16},{16,0},{1,17},{17,1},{2,18},{18,2},{3,19},{19,3},{4,20},{20... | collective-permute-start | bytes 6291464 | tf_op jit(solution)/shard_map/ppermute | solution.py:642
  412.7 66.5 %collective-permute-start.24 = (bf16[512,2048]{1,0:T(8,128)(2,1)}, bf16[512,2048]{1,0:T(8,128)(2,1)}, u32[]{:S(2)}, u32[]{:S(2)}) collective-permute-start(bf16[512,2048]{1,0:T(8,128)(2,1)} %multiply_convert_fusion.refs_0_), channel_id=1, source_target_pairs={{0,1},{1,0},{2,3},{3,2},{4,5},{5,4},{6,7},{7,6},{8,9},{9,8},{10,11... | collective-permute-start | bytes 6291464 | tf_op jit(solution)/shard_map/ppermute | solution.py:646
  453.7 25.5 %collective-permute-start.26 = (bf16[512,2048]{1,0:T(8,128)(2,1)}, bf16[512,2048]{1,0:T(8,128)(2,1)}, u32[]{:S(2)}, u32[]{:S(2)}) collective-permute-start(bf16[512,2048]{1,0:T(8,128)(2,1)} %collective-permute-done.25.refs_0_), channel_id=1, source_target_pairs={{0,1},{1,0},{2,3},{3,2},{4,5},{5,4},{6,7},{7,6},{8,9},{9,8},{10,11... | collective-permute-start | bytes 6291464 | tf_op jit(solution)/shard_map/ppermute | solution.py:646
  457.8 48.2 %collective-permute-start.35 = (bf16[512,2048]{1,0:T(8,128)(2,1)S(1)}, bf16[512,2048]{1,0:T(8,128)(2,1)}, u32[]{:S(2)}, u32[]{:S(2)}) collective-permute-start(bf16[512,2048]{1,0:T(8,128)(2,1)S(1)} %maximum_select_fusion.3.refs_0_), channel_id=1, source_target_pairs={{0,2},{2,0},{4,6},{6,4},{8,10},{10,8},{12,14},{14,12},{1,3},{3,1},... | collective-permute-start | bytes 6291464 | tf_op jit(solution)/shard_map/ppermute | solution.py:692
  475.1 38.4 %collective-permute-start.30 = (bf16[1,512,1024]{2,1,0:T(8,128)(2,1)}, bf16[1,512,1024]{2,1,0:T(8,128)(2,1)S(1)}, u32[]{:S(2)}, u32[]{:S(2)}) collective-permute-start(bf16[1,512,1024]{2,1,0:T(8,128)(2,1)} %collective-permute-done.29.refs_1_), channel_id=1, source_target_pairs={{0,16},{16,0},{1,17},{17,1},{2,18},{18,2},{3,19},{19,3},{4,20},{20... | collective-permute-start | bytes 3145736 | tf_op jit(solution)/shard_map/ppermute | solution.py:642
  479.2 77.1 %collective-permute-start.34 = (bf16[512,2048]{1,0:T(8,128)(2,1)S(1)}, bf16[512,2048]{1,0:T(8,128)(2,1)}, u32[]{:S(2)}, u32[]{:S(2)}) collective-permute-start(bf16[512,2048]{1,0:T(8,128)(2,1)S(1)} %maximum_select_fusion.3.refs_0_), channel_id=1, source_target_pairs={{0,1},{1,0},{2,3},{3,2},{4,5},{5,4},{6,7},{7,6},{8,9},{9,8},{10,11... | collective-permute-start | bytes 6291464 | tf_op jit(solution)/shard_map/ppermute | solution.py:646
  506.0 50.3 %collective-permute-start.36 = (bf16[512,2048]{1,0:T(8,128)(2,1)}, bf16[512,2048]{1,0:T(8,128)(2,1)}, u32[]{:S(2)}, u32[]{:S(2)}) collective-permute-start(bf16[512,2048]{1,0:T(8,128)(2,1)} %collective-permute-done.35.refs_2_), channel_id=1, source_target_pairs={{0,1},{1,0},{2,3},{3,2},{4,5},{5,4},{6,7},{7,6},{8,9},{9,8},{10,11... | collective-permute-start | bytes 6291464 | tf_op jit(solution)/shard_map/ppermute | solution.py:646
  590.2 292.7 %reduce-scatter.6.cloned.1.call-start = ((), (), s32[]{:S(2)}) async-start(), calls=%async_computation.13 | async-start | bytes 12582912 | tf_op jit(solution)/shard_map/reduce_scatter | solution.py:1017
  617.0 48.0 %collective-permute-start.33 = (bf16[512,2048]{1,0:T(8,128)(2,1)S(1)}, bf16[512,2048]{1,0:T(8,128)(2,1)S(1)}, u32[]{:S(2)}, u32[]{:S(2)}) collective-permute-start(bf16[512,2048]{1,0:T(8,128)(2,1)S(1)} %add_convert_fusion.7.refs_7_), channel_id=1, source_target_pairs={{0,2},{2,0},{4,6},{6,4},{8,10},{10,8},{12,14},{14,12},{1,3},{3,1},... | collective-permute-start | bytes 6291464 | tf_op jit(solution)/shard_map/ppermute | solution.py:692
  688.7 221.2 %reduce-scatter.8.cloned.1.call-start = ((), (), s32[]{:S(2)}) async-start(), calls=%async_computation.14 | async-start | bytes 12582912 | tf_op jit(solution)/shard_map/reduce_scatter | solution.py:1017
  717.7 98.5 %all-to-all-start.5 = ((bf16[4,512,1024]{2,1,0:T(8,128)(2,1)}), bf16[4,512,1024]{2,1,0:T(8,128)(2,1)}, u32[]{:S(2)}, u32[]{:S(2)}) async-start(bf16[4,512,1024]{2,1,0:T(8,128)(2,1)} %pad_maximum_fusion.6), calls=%async_computation.6 | async-start | bytes 8388608 | tf_op jit(solution)/shard_map/all_to_all | solution.py:707
  753.4 47.8 %collective-permute-start.39 = (bf16[512,2048]{1,0:T(8,128)(2,1)S(1)}, bf16[512,2048]{1,0:T(8,128)(2,1)}, u32[]{:S(2)}, u32[]{:S(2)}) collective-permute-start(bf16[512,2048]{1,0:T(8,128)(2,1)S(1)} %add_convert_fusion.5.refs_6_), channel_id=1, source_target_pairs={{0,2},{2,0},{4,6},{6,4},{8,10},{10,8},{12,14},{14,12},{1,3},{3,1},... | collective-permute-start | bytes 6291464 | tf_op jit(solution)/shard_map/ppermute | solution.py:692
  784.2 32.0 %collective-permute-start.38 = (bf16[512,2048]{1,0:T(8,128)(2,1)}, bf16[512,2048]{1,0:T(8,128)(2,1)}, u32[]{:S(2)}, u32[]{:S(2)}) collective-permute-start(bf16[512,2048]{1,0:T(8,128)(2,1)} %slice.570), channel_id=1, source_target_pairs={{0,1},{1,0},{2,3},{3,2},{4,5},{5,4},{6,7},{7,6},{8,9},{9,8},{10,11... | collective-permute-start | bytes 6291464 | tf_op jit(solution)/shard_map/ppermute | solution.py:646
  785.8 36.0 %collective-permute-start.31 = (bf16[512,2048]{1,0:T(8,128)(2,1)}, bf16[512,2048]{1,0:T(8,128)(2,1)}, u32[]{:S(2)}, u32[]{:S(2)}) collective-permute-start(bf16[512,2048]{1,0:T(8,128)(2,1)} %slice.560), channel_id=1, source_target_pairs={{0,1},{1,0},{2,3},{3,2},{4,5},{5,4},{6,7},{7,6},{8,9},{9,8},{10,11... | collective-permute-start | bytes 6291464 | tf_op jit(solution)/shard_map/ppermute | solution.py:646
  831.8 46.9 %collective-permute-start.41 = (bf16[512,2048]{1,0:T(8,128)(2,1)}, bf16[512,2048]{1,0:T(8,128)(2,1)}, u32[]{:S(2)}, u32[]{:S(2)}) collective-permute-start(bf16[512,2048]{1,0:T(8,128)(2,1)} %get-tuple-element.148.refs_0_), channel_id=1, source_target_pairs={{0,2},{2,0},{4,6},{6,4},{8,10},{10,8},{12,14},{14,12},{1,3},{3,1},... | collective-permute-start | bytes 6291464 | tf_op jit(solution)/shard_map/ppermute | solution.py:692
  835.7 52.2 %all-to-all-start.3 = ((bf16[4,128,2048]{2,1,0:T(8,128)(2,1)}), bf16[4,128,2048]{2,1,0:T(8,128)(2,1)S(1)}, u32[]{:S(2)}, u32[]{:S(2)}) async-start(bf16[4,128,2048]{2,1,0:T(8,128)(2,1)} %bitcast.313), calls=%async_computation.3 | async-start | bytes 4194304 | tf_op jit(solution)/shard_map/all_to_all | solution.py:707
  839.4 54.6 %collective-permute-start.40 = (bf16[512,2048]{1,0:T(8,128)(2,1)}, bf16[512,2048]{1,0:T(8,128)(2,1)}, u32[]{:S(2)}, u32[]{:S(2)}) collective-permute-start(bf16[512,2048]{1,0:T(8,128)(2,1)} %get-tuple-element.148.refs_0_), channel_id=1, source_target_pairs={{0,1},{1,0},{2,3},{3,2},{4,5},{5,4},{6,7},{7,6},{8,9},{9,8},{10,11... | collective-permute-start | bytes 6291464 | tf_op jit(solution)/shard_map/ppermute | solution.py:646
  878.7 15.4 %collective-permute-start.42 = (bf16[512,2048]{1,0:T(8,128)(2,1)}, bf16[512,2048]{1,0:T(8,128)(2,1)}, u32[]{:S(2)}, u32[]{:S(2)}) collective-permute-start(bf16[512,2048]{1,0:T(8,128)(2,1)} %collective-permute-done.41.refs_2_), channel_id=1, source_target_pairs={{0,1},{1,0},{2,3},{3,2},{4,5},{5,4},{6,7},{7,6},{8,9},{9,8},{10,11... | collective-permute-start | bytes 6291464 | tf_op jit(solution)/shard_map/ppermute | solution.py:646
  889.2 188.9 %all-to-all-start.6 = ((bf16[4,512,1024]{2,1,0:T(8,128)(2,1)}), bf16[4,512,1024]{2,1,0:T(8,128)(2,1)}, u32[]{:S(2)}, u32[]{:S(2)}) async-start(bf16[4,512,1024]{2,1,0:T(8,128)(2,1)} %after.40), calls=%async_computation.8 | async-start | bytes 8388608 | tf_op jit(solution)/shard_map/all_to_all | solution.py:707
  918.2 25.9 %collective-permute-start.43 = (bf16[512,1028]{0,1:T(8,128)(2,1)S(1)}, bf16[512,1028]{0,1:T(8,128)(2,1)}, u32[]{:S(2)}, u32[]{:S(2)}) collective-permute-start(bf16[512,1028]{0,1:T(8,128)(2,1)S(1)} %copy.227), channel_id=1, source_target_pairs={{0,16},{16,0},{1,17},{17,1},{2,18},{18,2},{3,19},{19,3},{4,20},{20... | collective-permute-start | bytes 3158024 | tf_op jit(solution)/shard_map/ppermute | solution.py:642
  923.4 130.8 %collective-permute-start.46 = (bf16[512,1024]{1,0:T(8,128)(2,1)}, bf16[512,1024]{1,0:T(8,128)(2,1)}, u32[]{:S(2)}, u32[]{:S(2)}) collective-permute-start(bf16[512,1024]{1,0:T(8,128)(2,1)} %get-tuple-element.154), channel_id=1, source_target_pairs={{0,12},{2,14},{4,0},{6,2},{8,4},{10,6},{12,8},{14,10},{1,13},{3,15... | collective-permute-start | bytes 3145736 | tf_op jit(solution)/shard_map/ppermute | solution.py:699
  927.1 151.0 %collective-permute-start.45 = (bf16[512,1024]{1,0:T(8,128)(2,1)}, bf16[512,1024]{1,0:T(8,128)(2,1)}, u32[]{:S(2)}, u32[]{:S(2)}) collective-permute-start(bf16[512,1024]{1,0:T(8,128)(2,1)} %get-tuple-element.155), channel_id=1, source_target_pairs={{0,8},{2,10},{4,12},{6,14},{8,0},{10,2},{12,4},{14,6},{1,9},{3,11}... | collective-permute-start | bytes 3145736 | tf_op jit(solution)/shard_map/ppermute | solution.py:699
  927.1 151.0 %collective-permute-start.44 = (bf16[512,1024]{1,0:T(8,128)(2,1)}, bf16[512,1024]{1,0:T(8,128)(2,1)}, u32[]{:S(2)}, u32[]{:S(2)}) collective-permute-start(bf16[512,1024]{1,0:T(8,128)(2,1)} %get-tuple-element.156), channel_id=1, source_target_pairs={{0,4},{2,6},{4,8},{6,10},{8,12},{10,14},{12,0},{14,2},{1,5},{3,7},... | collective-permute-start | bytes 3145736 | tf_op jit(solution)/shard_map/ppermute | solution.py:699
  1087.5 14.4 %collective-permute-start.48 = (bf16[512,2048]{1,0:T(8,128)(2,1)S(1)}, bf16[512,2048]{1,0:T(8,128)(2,1)S(1)}, u32[]{:S(2)}, u32[]{:S(2)}) collective-permute-start(bf16[512,2048]{1,0:T(8,128)(2,1)S(1)} %pad_maximum_fusion.10), channel_id=1, source_target_pairs={{0,1},{1,0},{2,3},{3,2},{4,5},{5,4},{6,7},{7,6},{8,9},{9,8},{10,11... | collective-permute-start | bytes 6291464 | tf_op jit(solution)/shard_map/ppermute | solution.py:646
  1101.9 69.3 %collective-permute-start.47 = (bf16[512,2048]{1,0:T(8,128)(2,1)}, bf16[512,2048]{1,0:T(8,128)(2,1)}, u32[]{:S(2)}, u32[]{:S(2)}) collective-permute-start(bf16[512,2048]{1,0:T(8,128)(2,1)} %pad_maximum_fusion.11), channel_id=1, source_target_pairs={{0,1},{1,0},{2,3},{3,2},{4,5},{5,4},{6,7},{7,6},{8,9},{9,8},{10,11... | collective-permute-start | bytes 6291464 | tf_op jit(solution)/shard_map/ppermute | solution.py:646
  1104.1 67.1 %collective-permute-start.49 = (bf16[512,2048]{1,0:T(8,128)(2,1)}, bf16[512,2048]{1,0:T(8,128)(2,1)}, u32[]{:S(2)}, u32[]{:S(2)}) collective-permute-start(bf16[512,2048]{1,0:T(8,128)(2,1)} %add_convert_fusion.3.refs_1_), channel_id=1, source_target_pairs={{0,2},{2,0},{4,6},{6,4},{8,10},{10,8},{12,14},{14,12},{1,3},{3,1},... | collective-permute-start | bytes 6291464 | tf_op jit(solution)/shard_map/ppermute | solution.py:692
  1129.2 38.1 %collective-permute-start.50 = (bf16[768,1060]{0,1:T(8,128)(2,1)}, bf16[768,1060]{0,1:T(8,128)(2,1)}, u32[]{:S(2)}, u32[]{:S(2)}) collective-permute-start(bf16[768,1060]{0,1:T(8,128)(2,1)} %copy.236), channel_id=1, source_target_pairs={{0,16},{16,0},{1,17},{17,1},{2,18},{18,2},{3,19},{19,3},{4,20},{20... | collective-permute-start | bytes 4884488 | tf_op jit(solution)/shard_map/ppermute | solution.py:642
  1150.5 39.8 %collective-permute-start.65 = (bf16[256,514]{1,0:T(8,128)(2,1)}, bf16[256,514]{1,0:T(8,128)(2,1)}, u32[]{:S(2)}, u32[]{:S(2)}) collective-permute-start(bf16[256,514]{1,0:T(8,128)(2,1)} %get-tuple-element.212), channel_id=1, source_target_pairs={{0,12},{2,14},{4,0},{6,2},{8,4},{10,6},{12,8},{14,10},{1,13},{3,15... | collective-permute-start | bytes 789512 | tf_op jit(solution)/shard_map/ppermute | solution.py:699
  1150.5 39.8 %collective-permute-start.64 = (bf16[256,514]{1,0:T(8,128)(2,1)}, bf16[256,514]{1,0:T(8,128)(2,1)}, u32[]{:S(2)}, u32[]{:S(2)}) collective-permute-start(bf16[256,514]{1,0:T(8,128)(2,1)} %get-tuple-element.213), channel_id=1, source_target_pairs={{0,8},{2,10},{4,12},{6,14},{8,0},{10,2},{12,4},{14,6},{1,9},{3,11}... | collective-permute-start | bytes 789512 | tf_op jit(solution)/shard_map/ppermute | solution.py:699
  1167.3 22.9 %collective-permute-start.63 = (bf16[256,514]{1,0:T(8,128)(2,1)}, bf16[256,514]{1,0:T(8,128)(2,1)}, u32[]{:S(2)}, u32[]{:S(2)}) collective-permute-start(bf16[256,514]{1,0:T(8,128)(2,1)} %get-tuple-element.214), channel_id=1, source_target_pairs={{0,4},{2,6},{4,8},{6,10},{8,12},{10,14},{12,0},{14,2},{1,5},{3,7},... | collective-permute-start | bytes 789512 | tf_op jit(solution)/shard_map/ppermute | solution.py:699
  1185.0 126.3 %all-to-all-start.7 = ((bf16[4,128,2048]{2,1,0:T(8,128)(2,1)}), bf16[4,128,2048]{2,1,0:T(8,128)(2,1)}, u32[]{:S(2)}, u32[]{:S(2)}) async-start(bf16[4,128,2048]{2,1,0:T(8,128)(2,1)} %bitcast.299), calls=%async_computation.10 | async-start | bytes 4194304 | tf_op jit(solution)/shard_map/all_to_all | solution.py:707
  1211.0 38.9 %collective-permute-start.66 = (bf16[512,512]{1,0:T(8,128)(2,1)}, bf16[512,512]{1,0:T(8,128)(2,1)}, u32[]{:S(2)}, u32[]{:S(2)}) collective-permute-start(bf16[512,512]{1,0:T(8,128)(2,1)} %get-tuple-element.234), channel_id=1, source_target_pairs={{0,1},{1,0},{2,3},{3,2},{4,5},{5,4},{6,7},{7,6},{8,9},{9,8},{10,11... | collective-permute-start | bytes 1572872 | tf_op jit(solution)/shard_map/ppermute | solution.py:646
  1226.2 17.7 %collective-permute-start.67 = (bf16[512,512]{1,0:T(8,128)(2,1)}, bf16[512,512]{1,0:T(8,128)(2,1)}, u32[]{:S(2)}, u32[]{:S(2)}) collective-permute-start(bf16[512,512]{1,0:T(8,128)(2,1)} %get-tuple-element.232), channel_id=1, source_target_pairs={{0,1},{1,0},{2,3},{3,2},{4,5},{5,4},{6,7},{7,6},{8,9},{9,8},{10,11... | collective-permute-start | bytes 1572872 | tf_op jit(solution)/shard_map/ppermute | solution.py:646
  1237.9 17.8 %collective-permute-start.52 = (bf16[384,530]{1,0:T(8,128)(2,1)}, bf16[384,530]{1,0:T(8,128)(2,1)S(1)}, u32[]{:S(2)}, u32[]{:S(2)}) collective-permute-start(bf16[384,530]{1,0:T(8,128)(2,1)} %get-tuple-element.203), channel_id=1, source_target_pairs={{0,4},{2,6},{4,8},{6,10},{8,12},{10,14},{12,0},{14,2},{1,5},{3,7},... | collective-permute-start | bytes 1221128 | tf_op jit(solution)/shard_map/ppermute | solution.py:699
  1239.9 24.2 %collective-permute-start.54 = (bf16[384,530]{1,0:T(8,128)(2,1)}, bf16[384,530]{1,0:T(8,128)(2,1)}, u32[]{:S(2)}, u32[]{:S(2)}) collective-permute-start(bf16[384,530]{1,0:T(8,128)(2,1)} %get-tuple-element.204), channel_id=1, source_target_pairs={{0,12},{2,14},{4,0},{6,2},{8,4},{10,6},{12,8},{14,10},{1,13},{3,15... | collective-permute-start | bytes 1221128 | tf_op jit(solution)/shard_map/ppermute | solution.py:699
  1241.7 43.8 %collective-permute-start.53 = (bf16[384,530]{1,0:T(8,128)(2,1)}, bf16[384,530]{1,0:T(8,128)(2,1)}, u32[]{:S(2)}, u32[]{:S(2)}) collective-permute-start(bf16[384,530]{1,0:T(8,128)(2,1)} %get-tuple-element.205), channel_id=1, source_target_pairs={{0,8},{2,10},{4,12},{6,14},{8,0},{10,2},{12,4},{14,6},{1,9},{3,11}... | collective-permute-start | bytes 1221128 | tf_op jit(solution)/shard_map/ppermute | solution.py:699
  1243.9 45.5 %collective-permute-start.68 = (bf16[512,512]{1,0:T(8,128)(2,1)}, bf16[512,512]{1,0:T(8,128)(2,1)}, u32[]{:S(2)}, u32[]{:S(2)}) collective-permute-start(bf16[512,512]{1,0:T(8,128)(2,1)} %get-tuple-element.230), channel_id=1, source_target_pairs={{0,1},{1,0},{2,3},{3,2},{4,5},{5,4},{6,7},{7,6},{8,9},{9,8},{10,11... | collective-permute-start | bytes 1572872 | tf_op jit(solution)/shard_map/ppermute | solution.py:646
  1313.5 33.3 %all-to-all-start.8 = ((bf16[4,2,2,64,514]{4,3,1,2,0:T(8,128)(2,1)}), bf16[4,2,2,64,514]{4,3,1,2,0:T(8,128)(2,1)}, u32[]{:S(2)}, u32[]{:S(2)}) async-start(bf16[4,2,2,64,514]{4,3,1,2,0:T(8,128)(2,1)} %broadcast_in_dim.98), calls=%async_computation.11 | async-start | bytes 2621440 | tf_op jit(solution)/shard_map/all_to_all | solution.py:707
  (168 other events, 2778.5 us)
Sparse Core Ops, SparseCore 0:
  590.4 99.5 reduce-scatter.3
  692.4 99.2 reduce-scatter.5
  794.0 99.2 reduce-scatter.7

commit v3 on v2

--- a/solution.py
+++ b/solution.py
@@ -978,19 +978,21 @@
 
     chip_part, other_part = slice(0, split), slice(split, length)
     last_own = [over_z(ffn_own[2][:2])]
-    last_own.append(over_z(after(ffn_own[2][2:], last_own[0])))
     next_half()
     branch_sum, _, _ = reduce_tokens(
-        branch(chip_part), branch(other_part, ffn_own[2], ffn_other[1]), (ffn_other[2],)
+        branch(chip_part), branch(other_part, ffn_own[2], ffn_other[1])
     )
     middle = layer_in + branch_sum
+    last_own.append(over_z(after(ffn_own[2][2:], last_own[0], branch_sum)))
     last_other = [over_x(part) for part in last_own]
 
     scale_two = rms(middle)
-    ffn_pieces = gather_tokens((middle * scale_two * gain_two).astype(BF16))
-    ffn_pieces = ffn_pieces[:2] + after(ffn_pieces[2:], last_own[0])
-    ffn_rows = stack_rows(ffn_pieces)
-    grad_out = trade_z(after(cotangent[:, 0, 0], last_own[1]))
+    ffn_rows = stack_rows(
+        gather_tokens(
+            after((middle * scale_two * gain_two).astype(BF16), ffn_other[2]), last_own[1]
+        )
+    )
+    grad_out = trade_z(after(cotangent[:, 0, 0], last_own[0], branch_sum))
     grad_out = rotate(after(grad_out, middle).reshape(held, width))
     grads = stack_rows(gather_tokens(grad_out))
     last_other[0] = after(last_other[0], ffn_rows)

time: 1380 us -> 1370 us (level)
    ppermute x19, waiting for transfers between devices: 176 us -> 148 us  [over_z(): lax.ppermute(value, 'heads', [(a * wide + b, (a + k) % depth * wide + b)...]
  transfers between devices with their start and end apart: 81 -> 81, of which waited for: 31 -> 34; matrix products, arithmetic and copies ran while one was open for 28% -> 28% of each run, Pallas kernels for 27% -> 27%
where the time goes in v3:
time: 1370 us; the launch traced here: 1360 us
  waiting for transfers between devices  409 us (30%)
  Pallas kernels  397 us (29%)
  local copies, waits for them, and re-layouts  202 us (15%)
  other arithmetic  154 us (11%)
  starting transfers between devices  90.9 us (7%)
  matrix products  85.7 us (6%)
  between operations  16.9 us (1%)
    ppermute x19, waiting for transfers between devices, over_z(): lax.ppermute(value, 'heads', [(a * wide + b, (a + k) % depth * wide + b)...  148 us
    ppermute x11, waiting for transfers between devices, over_y(): lax.ppermute(value, 'heads', [(a * wide + b, a * wide + (b ^ k)) for a in...  122 us
    pallas_call x1, Pallas kernels, attend_backward(): pl.pallas_call(ignoring(backward_kernel, 22, len(waits)), grid_spec=pltpu...  94.4 us
    dot_general x27, matrix products, mm(): lax.dot_general(left, right, (((left_dim,), (right_dim,)), ((), ())), pre...  85.7 us
    pallas_call x4, Pallas kernels, sum_products(): dense_call(kernel, (2 * across, tokens // tall), [left] * count + [own] *...  77.6 us
    pallas_call x3, Pallas kernels, weight_grad_halves(): pl.pallas_call(kernel, grid_spec=pltpu.PrefetchScalarGridSpec(num_scalar_...  71.5 us
    unnamed x333, local copies, waits for them, and re-layouts  68.8 us
    all_to_all x9, waiting for transfers between devices, trade_z(): lax.all_to_all(value, 'heads', split_axis=0, concat_axis=0, tiled=True, a...  66.3 us
  transfers between devices with their start and end apart: 81, of which 34 were waited for; matrix products, arithmetic and copies ran while one was open for 28% of the time, Pallas kernels for 27%

profile of v3, /device:TPU:0, one launch (start us, length us, event | category | flops | bytes accessed | tf_op | source)
XLA Modules:
  0.0 1356.5 jit_solution(1507862568379749897)
XLA Ops:
  12.1 6.5 all-to-all-start
  41.8 13.4 collective-permute-done.7
  55.3 17.9 %collective-permute-done.6 = bf16[2,2,9344]{2,1,0:T(2,128)(2,1)S(1)} collective-permute-done((bf16[2,2,9344]{2,1,0:T(2,128)(2,1)S(1)}, bf16[2,2,9344]{2,1,0:T(2,128)(2,1)S(1)}, u32[]{:S(2)}, u32[]{:S(2)}) %collective-permute-start.6) | collective-permute-done | bytes 74784 | tf_op jit(solution)/shard_map/ppermute | solution.py:699
  88.4 6.2 broadcast_select_fusion
  96.4 4.5 fusion.97
  103.1 4.2 all-to-all-start.1
  113.8 18.0 %all-to-all-done.1.refs_1_ = bf16[4,256,512]{2,1,0:T(8,128)(2,1)} async-done(((bf16[4,256,512]{2,1,0:T(8,128)(2,1)}), bf16[4,256,512]{2,1,0:T(8,128)(2,1)}, u32[]{:S(2)}, u32[]{:S(2)}) %all-to-all-start.1) | async-done | bytes 1048608 | tf_op jit(solution)/shard_map/all_to_all | solution.py:707
  155.7 7.0 all-to-all-done.2.refs_1_.refs_0_
  175.3 24.3 %collective-permute-done.10 = bf16[768,1024]{1,0:T(8,128)(2,1)} collective-permute-done((bf16[768,1024]{1,0:T(8,128)(2,1)}, bf16[768,1024]{1,0:T(8,128)(2,1)}, u32[]{:S(2)}, u32[]{:S(2)}) %collective-permute-start.10) | collective-permute-done | bytes 1572896 | tf_op jit(solution)/shard_map/ppermute | solution.py:642
  210.1 4.5 fusion.16
  214.6 20.3 %collective-permute-done.14.refs_11_ = bf16[3,512,1024]{2,1,0:T(8,128)(2,1)} collective-permute-done((bf16[3,512,1024]{2,1,0:T(8,128)(2,1)}, bf16[3,512,1024]{2,1,0:T(8,128)(2,1)}, u32[]{:S(2)}, u32[]{:S(2)}) %collective-permute-start.14) | collective-permute-done | bytes 3145760 | tf_op jit(solution)/shard_map/ppermute | solution.py:699
  240.4 50.8 %attend_forward.1 = (bf16[512,2048]{1,0:T(8,128)(2,1)S(1)}, f32[8,2048]{1,0:T(8,128)S(1)}, f32[8,2048]{1,0:T(8,128)S(1)}, bf16[8,128,2048]{2,1,0:T(8,128)(2,1)S(...) custom-call(s32[16]{0:T(128)S(1)} %slice_reduce_fusion.refs_0_, ...), custom_call_target="tpu_custom_call" | custom-call | flops 17367040000 | bytes 6553600 | tf_op jit(solution)/shard_map/attend_forward/pallas_call | solution.py:266
  292.7 4.6 fusion.77
  298.2 5.0 collective-permute-done.20.refs_2_
  306.7 6.7 add_convert_fusion
  315.1 4.2 add_convert_fusion.1
  325.1 43.5 %collective-permute-done.22 = bf16[512,2048]{1,0:T(8,128)(2,1)S(1)} collective-permute-done((bf16[512,2048]{1,0:T(8,128)(2,1)S(1)}, bf16[512,2048]{1,0:T(8,128)(2,1)S(1)}, u32[]{:S(2)}, u32[]{:S(2)}) %collective-permute-start.22) | collective-permute-done | bytes 2097184 | tf_op jit(solution)/shard_map/ppermute | solution.py:692
  368.6 4.5 multiply_reduce_fusion.4
  381.8 12.6 collective-permute-done.23.refs_1_
  395.1 4.2 slice_bitcast_fusion.36
  403.4 33.9 %collective-permute-done.27.refs_1_ = bf16[1,512,1024]{2,1,0:T(8,128)(2,1)} collective-permute-done((bf16[1,512,1024]{2,1,0:T(8,128)(2,1)}, bf16[1,512,1024]{2,1,0:T(8,128)(2,1)}, u32[]{:S(2)}, u32[]{:S(2)}) %collective-permute-start.27) | collective-permute-done | bytes 1048608 | tf_op jit(solution)/shard_map/ppermute | solution.py:699
  441.2 6.2 all-to-all-done.4.refs_0_
  473.3 10.2 stack_rows.3.refs_1_.refs_0_.right_ref
  483.6 15.0 %collective-permute-done.35.refs_2_ = bf16[512,2048]{1,0:T(8,128)(2,1)} collective-permute-done((bf16[512,2048]{1,0:T(8,128)(2,1)S(1)}, bf16[512,2048]{1,0:T(8,128)(2,1)}, u32[]{:S(2)}, u32[]{:S(2)}) %collective-permute-start.35) | collective-permute-done | bytes 2097184 | tf_op jit(solution)/shard_map/ppermute | solution.py:692
  507.4 41.6 %gate_forward.1 = (bf16[2048,2048]{1,0:T(8,128)(2,1)}, bf16[2048,2048]{1,0:T(8,128)(2,1)}, bf16[2048,2048]{1,0:T(8,128)(2,1)}) custom-call(bf16[2048,2048]{1,0:T(8,128)(2,1)} %stack_rows.3.refs_1_.refs_0_.right_ref, bf16[2048,1024]{1,0:T(8,128)(2,1)S(1)} %copy-done.2, bf16[2048,1024]{1,0:T(8,128)(2,1)} %pad_maximum_fusion.1.refs_2_.refs_4_, ...), custom_call_target="tpu_custom_call" | custom-call | flops 11453246464 | bytes 4294967 | tf_op jit(solution)/shard_map/gate_forward/pallas_call | solution.py:580
  549.0 10.1 stack_rows.4.right_ref.refs_0_
  559.1 23.8 %weight_grad_halves.3.refs_5_ = bf16[2,2048,1024]{2,1,0:T(8,128)(2,1)} custom-call(s32[1]{0:T(128)} %bitcast.82.swap_ref, bf16[2048,2048]{1,0:T(8,128)(2,1)} %get-tuple-element.41.refs_0_.left_ref, bf16[2048,2048]{1,0:T(8,128)(2,1)} %stack_rows.4.right_ref.refs_0_), custom_call_target="tpu_custom_call" | custom-call | flops 4294967296 | bytes 2097152 | tf_op jit(solution)/shard_map/weight_grad_halves/pallas_call | solution.py:474
  590.4 13.2 sum_products.5
  610.6 13.2 sum_products.4.refs_6_
  625.8 30.6 %gate_backward.1 = (bf16[2048,2048]{1,0:T(8,128)(2,1)}, bf16[2048,2048]{1,0:T(8,128)(2,1)}) custom-call(bf16[2048,2048]{1,0:T(8,128)(2,1)} %stack_rows.4.right_ref.refs_0_, bf16[2048,1024]{1,0:T(8,128)(2,1)} %pad_maximum_fusion.4.refs_1_, bf16[2048,1024]{1,0:T(8,128)(2,1)} %pad_maximum_fusion.5.refs_2_, bf16[2048,2048]{1,0:T(8,128)(2,1)} %get-tuple-element.42.refs_3_, ...), custom_call_target="tpu_custom_call" | custom-call | flops 5726623232 | bytes 2147483 | tf_op jit(solution)/shard_map/gate_backward/pallas_call | solution.py:598
  657.1 24.0 %weight_grad_halves.4.refs_0_.refs_1_ = bf16[2,2048,1024]{2,1,0:T(8,128)(2,1)} custom-call(s32[1]{0:T(128)} %bitcast.82.swap_ref, bf16[2048,2048]{1,0:T(8,128)(2,1)} %get-tuple-element.44.refs_0_.left_ref, bf16[2048,2048]{1,0:T(8,128)(2,1)} %stack_rows.3.refs_1_.refs_0_.right_ref, bf16[512,2048]{1,0:T(8,128)(2,1)S(1)} %collective-permute-done.33.refs_0_), custom_call_target="tpu_custom_call" | custom-call | flops 4294967296 | bytes 2097152 | tf_op jit(solution)/shard_map/weight_grad_halves/pallas_call | solution.py:474
  681.1 23.8 %weight_grad_halves.5.refs_2_ = bf16[2,2048,1024]{2,1,0:T(8,128)(2,1)} custom-call(s32[1]{0:T(128)} %bitcast.82.swap_ref, bf16[2048,2048]{1,0:T(8,128)(2,1)} %get-tuple-element.45.refs_1_.left_ref, bf16[2048,2048]{1,0:T(8,128)(2,1)} %stack_rows.3.refs_1_.refs_0_.right_ref, bf16[2,2048,1024]{2,1,0:T(8,128)(2,1)} %weight_grad_halves.4.refs_0_.refs_1_), custom_call_target="tpu_custom_call" | custom-call | flops 4294967296 | bytes 2097152 | tf_op jit(solution)/shard_map/weight_grad_halves/pallas_call | solution.py:474
  709.8 5.1 all-to-all-start.5
  714.9 25.2 %sum_products.6 = bf16[1024,2048]{1,0:T(8,128)(2,1)S(1)} custom-call(bf16[2048,2048]{1,0:T(8,128)(2,1)} %get-tuple-element.44.refs_0_.left_ref, bf16[2048,2048]{1,0:T(8,128)(2,1)} %get-tuple-element.45.refs_1_.left_ref, bf16[2048,1024]{1,0:T(8,128)(2,1)} %pad_maximum_fusion.refs_1_.refs_2_, bf16[2048,1024]{1,0:T(8,128)(2,1)} %pad_maximum_fusion.2.refs_3_, ...), custom_call_target="tpu_custom_call" | custom-call | flops 5726623232 | bytes 2147483 | tf_op jit(solution)/shard_map/sum_products/pallas_call | solution.py:624
  740.5 4.1 collective-permute-done.37
  747.0 25.9 %sum_products.7 = bf16[1024,2048]{1,0:T(8,128)(2,1)} custom-call(bf16[2048,2048]{1,0:T(8,128)(2,1)} %get-tuple-element.44.refs_0_.left_ref, bf16[2048,2048]{1,0:T(8,128)(2,1)} %get-tuple-element.45.refs_1_.left_ref, bf16[2048,1024]{1,0:T(8,128)(2,1)} %pad_maximum_fusion.refs_1_.refs_2_, bf16[2048,1024]{1,0:T(8,128)(2,1)} %pad_maximum_fusion.2.refs_3_, ...), custom_call_target="tpu_custom_call" | custom-call | flops 5726623232 | bytes 2147483 | tf_op jit(solution)/shard_map/sum_products/pallas_call | solution.py:624
  778.4 15.0 %collective-permute-done.39.refs_0_ = bf16[512,2048]{1,0:T(8,128)(2,1)} collective-permute-done((bf16[512,2048]{1,0:T(8,128)(2,1)S(1)}, bf16[512,2048]{1,0:T(8,128)(2,1)}, u32[]{:S(2)}, u32[]{:S(2)}) %collective-permute-start.39) | collective-permute-done | bytes 2097184 | tf_op jit(solution)/shard_map/ppermute | solution.py:692
  793.4 15.1 %all-to-all-done.5.refs_3_.refs_0_ = bf16[4,512,1024]{2,1,0:T(8,128)(2,1)} async-done(((bf16[4,512,1024]{2,1,0:T(8,128)(2,1)}), bf16[4,512,1024]{2,1,0:T(8,128)(2,1)}, u32[]{:S(2)}, u32[]{:S(2)}) %all-to-all-start.5) | async-done | bytes 4194336 | tf_op jit(solution)/shard_map/all_to_all | solution.py:707
  808.5 5.9 multiply_reduce_fusion
  815.9 8.4 fusion.96
  831.6 39.5 %collective-permute-done.41.refs_2_ = bf16[512,2048]{1,0:T(8,128)(2,1)} collective-permute-done((bf16[512,2048]{1,0:T(8,128)(2,1)}, bf16[512,2048]{1,0:T(8,128)(2,1)}, u32[]{:S(2)}, u32[]{:S(2)}) %collective-permute-start.41) | collective-permute-done | bytes 2097184 | tf_op jit(solution)/shard_map/ppermute | solution.py:692
  881.6 4.8 all-to-all-start.6
  886.5 10.2 stack_rows.5.refs_1_
  896.6 5.6 convolution_convert_fusion
  905.4 4.5 fusion.31
  921.9 10.0 add_convert_fusion.4.refs_13_
  931.9 4.6 collective-permute-done.43
  949.6 94.4 %attend_backward.1 = (bf16[800,2048]{1,0:T(8,128)(2,1)S(1)}, f32[8,64,64]{2,1,0:T(8,128)S(1)}) custom-call(s32[16]{0:T(128)S(1)} %copy-done.29, s32[16]{0:T(128)S(1)} %copy-done.31, s32[1,2048]{1,0:T(1,128)S(1)} %copy-done.27, s32[2048,1]{1,0:T(8,128)S(1)} %copy-done.21, s32[2048,1]{1,0:T(8,128)S(1)} %copy-done.21, bf16[768,2048]{1,0:T(8,128)(2,1)S(1)} %copy-done.19, ...), custom_call_target="tpu_custom_call" | custom-call | flops 34406400000 | bytes 9830400 | tf_op jit(solution)/shard_map/attend_backward/pallas_call | solution.py:342
  1046.5 24.0 %collective-permute-done.45.refs_3_.refs_1_ = bf16[512,1024]{1,0:T(8,128)(2,1)} collective-permute-done((bf16[512,1024]{1,0:T(8,128)(2,1)}, bf16[512,1024]{1,0:T(8,128)(2,1)}, u32[]{:S(2)}, u32[]{:S(2)}) %collective-permute-start.45) | collective-permute-done | bytes 1048608 | tf_op jit(solution)/shard_map/ppermute | solution.py:699
  1071.7 4.0 convolution_convert_fusion.3
  1097.6 4.4 fusion.39
  1125.1 4.0 fusion.41
  1142.7 16.4 %collective-permute-done.50 = bf16[768,1060]{0,1:T(8,128)(2,1)} collective-permute-done((bf16[768,1060]{0,1:T(8,128)(2,1)}, bf16[768,1060]{0,1:T(8,128)(2,1)}, u32[]{:S(2)}, u32[]{:S(2)}) %collective-permute-start.50) | collective-permute-done | bytes 1628192 | tf_op jit(solution)/shard_map/ppermute | solution.py:642
  1162.9 7.3 multiply_reduce_fusion.1
  1170.3 4.0 add_convert_fusion.2
  1176.6 5.3 all-to-all-start.7
  1191.0 4.4 reduce_sum.95
  1195.4 4.4 reduce_sum.94
  1222.9 4.1 maximum_select_fusion.5
  1247.3 8.4 collective-permute-done.54
  1255.8 21.4 %collective-permute-done.53 = bf16[384,530]{1,0:T(8,128)(2,1)} collective-permute-done((bf16[384,530]{1,0:T(8,128)(2,1)}, bf16[384,530]{1,0:T(8,128)(2,1)}, u32[]{:S(2)}, u32[]{:S(2)}) %collective-permute-start.53) | collective-permute-done | bytes 407072 | tf_op jit(solution)/shard_map/ppermute | solution.py:699
  1305.1 4.3 all-to-all-start.8
  1314.2 4.1 bitcast_convert_fusion
  1318.4 20.0 %all-to-all-done.8 = bf16[4,2,2,64,514]{4,3,1,2,0:T(8,128)(2,1)} async-done(((bf16[4,2,2,64,514]{4,3,1,2,0:T(8,128)(2,1)}), bf16[4,2,2,64,514]{4,3,1,2,0:T(8,128)(2,1)}, u32[]{:S(2)}, u32[]{:S(2)}) %all-to-all-start.8) | async-done | bytes 1052704 | tf_op jit(solution)/shard_map/all_to_all | solution.py:707
  (728 shorter events, 412.2 us)
Async XLA Ops:
  12.1 83.0 %all-to-all-start = ((bf16[4,128,2048]{2,1,0:T(8,128)(2,1)}), bf16[4,128,2048]{2,1,0:T(8,128)(2,1)S(1)}, u32[]{:S(2)}, u32[]{:S(2)}) async-start(bf16[4,128,2048]{2,1,0:T(8,128)(2,1)} %bitcast.325), calls=%async_computation | async-start | bytes 4194304 | tf_op jit(solution)/shard_map/all_to_all | solution.py:707
  19.9 12.4 collective-permute-start.3
  22.2 60.9 %collective-permute-start.1 = (bf16[128,512]{1,0:T(8,128)(2,1)}, bf16[128,512]{1,0:T(8,128)(2,1)}, u32[]{:S(2)}, u32[]{:S(2)}) collective-permute-start(bf16[128,512]{1,0:T(8,128)(2,1)} %get-tuple-element.257), channel_id=1, source_target_pairs={{0,1},{1,0},{2,3},{3,2},{4,5},{5,4},{6,7},{7,6},{8,9},{9,8},{10,11... | collective-permute-start | bytes 393224 | tf_op jit(solution)/shard_map/ppermute | solution.py:646
  23.4 61.6 %collective-permute-start.2 = (bf16[128,512]{1,0:T(8,128)(2,1)}, bf16[128,512]{1,0:T(8,128)(2,1)}, u32[]{:S(2)}, u32[]{:S(2)}) collective-permute-start(bf16[128,512]{1,0:T(8,128)(2,1)} %get-tuple-element.259), channel_id=1, source_target_pairs={{0,1},{1,0},{2,3},{3,2},{4,5},{5,4},{6,7},{7,6},{8,9},{9,8},{10,11... | collective-permute-start | bytes 393224 | tf_op jit(solution)/shard_map/ppermute | solution.py:646
  36.7 18.6 %collective-permute-start.7 = (bf16[2,2,9344]{2,1,0:T(2,128)(2,1)S(1)}, bf16[2,2,9344]{2,1,0:T(2,128)(2,1)S(1)}, u32[]{:S(2)}, u32[]{:S(2)}) collective-permute-start(bf16[2,2,9344]{2,1,0:T(2,128)(2,1)S(1)} %broadcast_select_fusion.3), channel_id=1, source_target_pairs={{0,12},{2,14},{4,0},{6,2},{8,4},{10,6},{12,8},{14,10},{1,13},{3,15... | collective-permute-start | bytes 224264 | tf_op jit(solution)/shard_map/ppermute | solution.py:699
  40.6 32.7 %collective-permute-start.6 = (bf16[2,2,9344]{2,1,0:T(2,128)(2,1)S(1)}, bf16[2,2,9344]{2,1,0:T(2,128)(2,1)S(1)}, u32[]{:S(2)}, u32[]{:S(2)}) collective-permute-start(bf16[2,2,9344]{2,1,0:T(2,128)(2,1)S(1)} %broadcast_select_fusion.3), channel_id=1, source_target_pairs={{0,8},{2,10},{4,12},{6,14},{8,0},{10,2},{12,4},{14,6},{1,9},{3,11}... | collective-permute-start | bytes 224264 | tf_op jit(solution)/shard_map/ppermute | solution.py:699
  40.6 32.7 %collective-permute-start.5 = (bf16[2,2,9344]{2,1,0:T(2,128)(2,1)S(1)}, bf16[2,2,9344]{2,1,0:T(2,128)(2,1)S(1)}, u32[]{:S(2)}, u32[]{:S(2)}) collective-permute-start(bf16[2,2,9344]{2,1,0:T(2,128)(2,1)S(1)} %broadcast_select_fusion.3), channel_id=1, source_target_pairs={{0,4},{2,6},{4,8},{6,10},{8,12},{10,14},{12,0},{14,2},{1,5},{3,7},... | collective-permute-start | bytes 224264 | tf_op jit(solution)/shard_map/ppermute | solution.py:699
  55.3 33.1 %collective-permute-start.13 = (bf16[3,512,512]{2,1,0:T(8,128)(2,1)}, bf16[3,512,512]{2,1,0:T(8,128)(2,1)}, u32[]{:S(2)}, u32[]{:S(2)}) collective-permute-start(bf16[3,512,512]{2,1,0:T(8,128)(2,1)} %pad_maximum_fusion.17), channel_id=1, source_target_pairs={{0,1},{1,0},{2,3},{3,2},{4,5},{5,4},{6,7},{7,6},{8,9},{9,8},{10,11... | collective-permute-start | bytes 4718600 | tf_op jit(solution)/shard_map/ppermute | solution.py:646
  94.6 71.4 %collective-permute-start.15 = (bf16[3,512,1024]{2,1,0:T(8,128)(2,1)}, bf16[3,512,1024]{2,1,0:T(8,128)(2,1)}, u32[]{:S(2)}, u32[]{:S(2)}) collective-permute-start(bf16[3,512,1024]{2,1,0:T(8,128)(2,1)} %get-tuple-element.182), channel_id=1, source_target_pairs={{0,16},{16,0},{1,17},{17,1},{2,18},{18,2},{3,19},{19,3},{4,20},{20... | collective-permute-start | bytes 9437192 | tf_op jit(solution)/shard_map/ppermute | solution.py:642
  103.1 28.7 %all-to-all-start.1 = ((bf16[4,256,512]{2,1,0:T(8,128)(2,1)}), bf16[4,256,512]{2,1,0:T(8,128)(2,1)}, u32[]{:S(2)}, u32[]{:S(2)}) async-start(bf16[4,256,512]{2,1,0:T(8,128)(2,1)} %broadcast_in_dim.53), calls=%async_computation.1 | async-start | bytes 2097152 | tf_op jit(solution)/shard_map/all_to_all | solution.py:707
  109.3 55.6 %collective-permute-start.11 = (bf16[512,2048]{1,0:T(8,128)(2,1)}, bf16[512,2048]{1,0:T(8,128)(2,1)}, u32[]{:S(2)}, u32[]{:S(2)}) collective-permute-start(bf16[512,2048]{1,0:T(8,128)(2,1)} %multiply_convert_fusion.1), channel_id=1, source_target_pairs={{0,2},{2,0},{4,6},{6,4},{8,10},{10,8},{12,14},{14,12},{1,3},{3,1},... | collective-permute-start | bytes 6291464 | tf_op jit(solution)/shard_map/ppermute | solution.py:692
  133.8 28.9 %all-to-all-start.2 = ((bf16[4,256,512]{2,1,0:T(8,128)(2,1)}), bf16[4,256,512]{2,1,0:T(8,128)(2,1)S(1)}, u32[]{:S(2)}, u32[]{:S(2)}) async-start(bf16[4,256,512]{2,1,0:T(8,128)(2,1)} %broadcast_in_dim.88), calls=%async_computation.2 | async-start | bytes 2097152 | tf_op jit(solution)/shard_map/all_to_all | solution.py:707
  144.5 30.8 %collective-permute-start.9 = (bf16[512,2048]{1,0:T(8,128)(2,1)}, bf16[512,2048]{1,0:T(8,128)(2,1)}, u32[]{:S(2)}, u32[]{:S(2)}) collective-permute-start(bf16[512,2048]{1,0:T(8,128)(2,1)} %multiply_convert_fusion.1), channel_id=1, source_target_pairs={{0,1},{1,0},{2,3},{3,2},{4,5},{5,4},{6,7},{7,6},{8,9},{9,8},{10,11... | collective-permute-start | bytes 6291464 | tf_op jit(solution)/shard_map/ppermute | solution.py:646
  153.6 46.0 %collective-permute-start.10 = (bf16[768,1024]{1,0:T(8,128)(2,1)}, bf16[768,1024]{1,0:T(8,128)(2,1)}, u32[]{:S(2)}, u32[]{:S(2)}) collective-permute-start(bf16[768,1024]{1,0:T(8,128)(2,1)} %pad_maximum_fusion.16), channel_id=1, source_target_pairs={{0,16},{16,0},{1,17},{17,1},{2,18},{18,2},{3,19},{19,3},{4,20},{20... | collective-permute-start | bytes 4718600 | tf_op jit(solution)/shard_map/ppermute | solution.py:642
  163.7 71.2 %collective-permute-start.14 = (bf16[3,512,1024]{2,1,0:T(8,128)(2,1)}, bf16[3,512,1024]{2,1,0:T(8,128)(2,1)}, u32[]{:S(2)}, u32[]{:S(2)}) collective-permute-start(bf16[3,512,1024]{2,1,0:T(8,128)(2,1)} %after.29), channel_id=1, source_target_pairs={{0,4},{2,6},{4,8},{6,10},{8,12},{10,14},{12,0},{14,2},{1,5},{3,7},... | collective-permute-start | bytes 9437192 | tf_op jit(solution)/shard_map/ppermute | solution.py:699
  164.9 42.9 %collective-permute-start.12 = (bf16[512,2048]{1,0:T(8,128)(2,1)}, bf16[512,2048]{1,0:T(8,128)(2,1)}, u32[]{:S(2)}, u32[]{:S(2)}) collective-permute-start(bf16[512,2048]{1,0:T(8,128)(2,1)} %collective-permute-done.11), channel_id=1, source_target_pairs={{0,1},{1,0},{2,3},{3,2},{4,5},{5,4},{6,7},{7,6},{8,9},{9,8},{10,11... | collective-permute-start | bytes 6291464 | tf_op jit(solution)/shard_map/ppermute | solution.py:646
  173.8 132.9 %collective-permute-start.17 = (bf16[512,1024]{1,0:T(8,128)(2,1)}, bf16[512,1024]{1,0:T(8,128)(2,1)}, u32[]{:S(2)}, u32[]{:S(2)}) collective-permute-start(bf16[512,1024]{1,0:T(8,128)(2,1)} %maximum_select_fusion.8), channel_id=1, source_target_pairs={{0,16},{16,0},{1,17},{17,1},{2,18},{18,2},{3,19},{19,3},{4,20},{20... | collective-permute-start | bytes 3145736 | tf_op jit(solution)/shard_map/ppermute | solution.py:642
  234.8 68.4 %collective-permute-start.20 = (bf16[3,512,1024]{2,1,0:T(8,128)(2,1)}, bf16[3,512,1024]{2,1,0:T(8,128)(2,1)S(1)}, u32[]{:S(2)}, u32[]{:S(2)}) collective-permute-start(bf16[3,512,1024]{2,1,0:T(8,128)(2,1)} %collective-permute-done.14.refs_11_), channel_id=1, source_target_pairs={{0,16},{16,0},{1,17},{17,1},{2,18},{18,2},{3,19},{19,3},{4,20},{20... | collective-permute-start | bytes 9437192 | tf_op jit(solution)/shard_map/ppermute | solution.py:642
  236.3 70.4 %collective-permute-start.19 = (bf16[3,512,1024]{2,1,0:T(8,128)(2,1)}, bf16[3,512,1024]{2,1,0:T(8,128)(2,1)}, u32[]{:S(2)}, u32[]{:S(2)}) collective-permute-start(bf16[3,512,1024]{2,1,0:T(8,128)(2,1)} %collective-permute-done.14.refs_11_), channel_id=1, source_target_pairs={{0,4},{2,6},{4,8},{6,10},{8,12},{10,14},{12,0},{14,2},{1,5},{3,7},... | collective-permute-start | bytes 9437192 | tf_op jit(solution)/shard_map/ppermute | solution.py:699
  321.0 47.6 %collective-permute-start.22 = (bf16[512,2048]{1,0:T(8,128)(2,1)S(1)}, bf16[512,2048]{1,0:T(8,128)(2,1)S(1)}, u32[]{:S(2)}, u32[]{:S(2)}) collective-permute-start(bf16[512,2048]{1,0:T(8,128)(2,1)S(1)} %add_convert_fusion.8), channel_id=1, source_target_pairs={{0,2},{2,0},{4,6},{6,4},{8,10},{10,8},{12,14},{14,12},{1,3},{3,1},... | collective-permute-start | bytes 6291464 | tf_op jit(solution)/shard_map/ppermute | solution.py:692
  324.3 70.1 %collective-permute-start.23 = (bf16[3,512,1024]{2,1,0:T(8,128)(2,1)}, bf16[3,512,1024]{2,1,0:T(8,128)(2,1)}, u32[]{:S(2)}, u32[]{:S(2)}) collective-permute-start(bf16[3,512,1024]{2,1,0:T(8,128)(2,1)} %collective-permute-done.19.refs_1_), channel_id=1, source_target_pairs={{0,16},{16,0},{1,17},{17,1},{2,18},{18,2},{3,19},{19,3},{4,20},{20... | collective-permute-start | bytes 9437192 | tf_op jit(solution)/shard_map/ppermute | solution.py:642
  324.9 49.1 %collective-permute-start.26 = (bf16[2,512,1024]{2,1,0:T(8,128)(2,1)S(1)}, bf16[2,512,1024]{2,1,0:T(8,128)(2,1)}, u32[]{:S(2)}, u32[]{:S(2)}) collective-permute-start(bf16[2,512,1024]{2,1,0:T(8,128)(2,1)S(1)} %slice.537), channel_id=1, source_target_pairs={{0,4},{2,6},{4,8},{6,10},{8,12},{10,14},{12,0},{14,2},{1,5},{3,7},... | collective-permute-start | bytes 6291464 | tf_op jit(solution)/shard_map/ppermute | solution.py:699
  374.0 73.4 %all-to-all-start.4 = ((bf16[4,128,2048]{2,1,0:T(8,128)(2,1)}), bf16[4,128,2048]{2,1,0:T(8,128)(2,1)S(1)}, u32[]{:S(2)}, u32[]{:S(2)}) async-start(bf16[4,128,2048]{2,1,0:T(8,128)(2,1)} %after.36), calls=%async_computation.4 | async-start | bytes 4194304 | tf_op jit(solution)/shard_map/all_to_all | solution.py:707
  377.8 327.2 %reduce-scatter.4.cloned.1.call-start = ((), (), s32[]{:S(2)}) async-start(), calls=%async_computation.12 | async-start | bytes 12582912 | tf_op jit(solution)/shard_map/reduce_scatter | solution.py:1019
  394.5 46.7 %collective-permute-start.25 = (bf16[512,2048]{1,0:T(8,128)(2,1)}, bf16[512,2048]{1,0:T(8,128)(2,1)}, u32[]{:S(2)}, u32[]{:S(2)}) collective-permute-start(bf16[512,2048]{1,0:T(8,128)(2,1)} %after.32.refs_0_), channel_id=1, source_target_pairs={{0,2},{2,0},{4,6},{6,4},{8,10},{10,8},{12,14},{14,12},{1,3},{3,1},... | collective-permute-start | bytes 6291464 | tf_op jit(solution)/shard_map/ppermute | solution.py:692
  399.3 38.0 %collective-permute-start.27 = (bf16[1,512,1024]{2,1,0:T(8,128)(2,1)}, bf16[1,512,1024]{2,1,0:T(8,128)(2,1)}, u32[]{:S(2)}, u32[]{:S(2)}) collective-permute-start(bf16[1,512,1024]{2,1,0:T(8,128)(2,1)} %after.33), channel_id=1, source_target_pairs={{0,4},{2,6},{4,8},{6,10},{8,12},{10,14},{12,0},{14,2},{1,5},{3,7},... | collective-permute-start | bytes 3145736 | tf_op jit(solution)/shard_map/ppermute | solution.py:699
  402.9 80.6 %collective-permute-start.29 = (bf16[2,512,1024]{2,1,0:T(8,128)(2,1)}, bf16[2,512,1024]{2,1,0:T(8,128)(2,1)}, u32[]{:S(2)}, u32[]{:S(2)}) collective-permute-start(bf16[2,512,1024]{2,1,0:T(8,128)(2,1)} %collective-permute-done.26.refs_1_), channel_id=1, source_target_pairs={{0,16},{16,0},{1,17},{17,1},{2,18},{18,2},{3,19},{19,3},{4,20},{20... | collective-permute-start | bytes 6291464 | tf_op jit(solution)/shard_map/ppermute | solution.py:642
  403.4 69.9 %collective-permute-start.24 = (bf16[512,2048]{1,0:T(8,128)(2,1)}, bf16[512,2048]{1,0:T(8,128)(2,1)}, u32[]{:S(2)}, u32[]{:S(2)}) collective-permute-start(bf16[512,2048]{1,0:T(8,128)(2,1)} %after.32.refs_0_), channel_id=1, source_target_pairs={{0,1},{1,0},{2,3},{3,2},{4,5},{5,4},{6,7},{7,6},{8,9},{9,8},{10,11... | collective-permute-start | bytes 6291464 | tf_op jit(solution)/shard_map/ppermute | solution.py:646
  441.2 32.1 %collective-permute-start.28 = (bf16[512,2048]{1,0:T(8,128)(2,1)}, bf16[512,2048]{1,0:T(8,128)(2,1)}, u32[]{:S(2)}, u32[]{:S(2)}) collective-permute-start(bf16[512,2048]{1,0:T(8,128)(2,1)} %after.34.refs_2_), channel_id=1, source_target_pairs={{0,1},{1,0},{2,3},{3,2},{4,5},{5,4},{6,7},{7,6},{8,9},{9,8},{10,11... | collective-permute-start | bytes 6291464 | tf_op jit(solution)/shard_map/ppermute | solution.py:646
  451.8 46.8 %collective-permute-start.35 = (bf16[512,2048]{1,0:T(8,128)(2,1)S(1)}, bf16[512,2048]{1,0:T(8,128)(2,1)}, u32[]{:S(2)}, u32[]{:S(2)}) collective-permute-start(bf16[512,2048]{1,0:T(8,128)(2,1)S(1)} %maximum_select_fusion.3.refs_0_), channel_id=1, source_target_pairs={{0,2},{2,0},{4,6},{6,4},{8,10},{10,8},{12,14},{14,12},{1,3},{3,1},... | collective-permute-start | bytes 6291464 | tf_op jit(solution)/shard_map/ppermute | solution.py:692
  472.4 33.7 %collective-permute-start.30 = (bf16[1,512,1024]{2,1,0:T(8,128)(2,1)}, bf16[1,512,1024]{2,1,0:T(8,128)(2,1)S(1)}, u32[]{:S(2)}, u32[]{:S(2)}) collective-permute-start(bf16[1,512,1024]{2,1,0:T(8,128)(2,1)} %collective-permute-done.27.refs_1_), channel_id=1, source_target_pairs={{0,16},{16,0},{1,17},{17,1},{2,18},{18,2},{3,19},{19,3},{4,20},{20... | collective-permute-start | bytes 3145736 | tf_op jit(solution)/shard_map/ppermute | solution.py:642
  473.3 75.7 %collective-permute-start.34 = (bf16[512,2048]{1,0:T(8,128)(2,1)S(1)}, bf16[512,2048]{1,0:T(8,128)(2,1)}, u32[]{:S(2)}, u32[]{:S(2)}) collective-permute-start(bf16[512,2048]{1,0:T(8,128)(2,1)S(1)} %maximum_select_fusion.3.refs_0_), channel_id=1, source_target_pairs={{0,1},{1,0},{2,3},{3,2},{4,5},{5,4},{6,7},{7,6},{8,9},{9,8},{10,11... | collective-permute-start | bytes 6291464 | tf_op jit(solution)/shard_map/ppermute | solution.py:646
  498.6 50.4 %collective-permute-start.36 = (bf16[512,2048]{1,0:T(8,128)(2,1)}, bf16[512,2048]{1,0:T(8,128)(2,1)}, u32[]{:S(2)}, u32[]{:S(2)}) collective-permute-start(bf16[512,2048]{1,0:T(8,128)(2,1)} %collective-permute-done.35.refs_2_), channel_id=1, source_target_pairs={{0,1},{1,0},{2,3},{3,2},{4,5},{5,4},{6,7},{7,6},{8,9},{9,8},{10,11... | collective-permute-start | bytes 6291464 | tf_op jit(solution)/shard_map/ppermute | solution.py:646
  582.9 292.5 %reduce-scatter.6.cloned.1.call-start = ((), (), s32[]{:S(2)}) async-start(), calls=%async_computation.13 | async-start | bytes 12582912 | tf_op jit(solution)/shard_map/reduce_scatter | solution.py:1019
  609.1 48.0 %collective-permute-start.33 = (bf16[512,2048]{1,0:T(8,128)(2,1)S(1)}, bf16[512,2048]{1,0:T(8,128)(2,1)S(1)}, u32[]{:S(2)}, u32[]{:S(2)}) collective-permute-start(bf16[512,2048]{1,0:T(8,128)(2,1)S(1)} %add_convert_fusion.7.refs_7_), channel_id=1, source_target_pairs={{0,2},{2,0},{4,6},{6,4},{8,10},{10,8},{12,14},{14,12},{1,3},{3,1},... | collective-permute-start | bytes 6291464 | tf_op jit(solution)/shard_map/ppermute | solution.py:692
  681.1 221.2 %reduce-scatter.8.cloned.1.call-start = ((), (), s32[]{:S(2)}) async-start(), calls=%async_computation.14 | async-start | bytes 12582912 | tf_op jit(solution)/shard_map/reduce_scatter | solution.py:1019
  709.8 98.6 %all-to-all-start.5 = ((bf16[4,512,1024]{2,1,0:T(8,128)(2,1)}), bf16[4,512,1024]{2,1,0:T(8,128)(2,1)}, u32[]{:S(2)}, u32[]{:S(2)}) async-start(bf16[4,512,1024]{2,1,0:T(8,128)(2,1)} %pad_maximum_fusion.6), calls=%async_computation.6 | async-start | bytes 8388608 | tf_op jit(solution)/shard_map/all_to_all | solution.py:707
  745.6 47.8 %collective-permute-start.39 = (bf16[512,2048]{1,0:T(8,128)(2,1)S(1)}, bf16[512,2048]{1,0:T(8,128)(2,1)}, u32[]{:S(2)}, u32[]{:S(2)}) collective-permute-start(bf16[512,2048]{1,0:T(8,128)(2,1)S(1)} %add_convert_fusion.5.refs_6_), channel_id=1, source_target_pairs={{0,2},{2,0},{4,6},{6,4},{8,10},{10,8},{12,14},{14,12},{1,3},{3,1},... | collective-permute-start | bytes 6291464 | tf_op jit(solution)/shard_map/ppermute | solution.py:692
  776.2 32.3 %collective-permute-start.38 = (bf16[512,2048]{1,0:T(8,128)(2,1)}, bf16[512,2048]{1,0:T(8,128)(2,1)}, u32[]{:S(2)}, u32[]{:S(2)}) collective-permute-start(bf16[512,2048]{1,0:T(8,128)(2,1)} %slice.570), channel_id=1, source_target_pairs={{0,1},{1,0},{2,3},{3,2},{4,5},{5,4},{6,7},{7,6},{8,9},{9,8},{10,11... | collective-permute-start | bytes 6291464 | tf_op jit(solution)/shard_map/ppermute | solution.py:646
  777.9 36.5 %collective-permute-start.31 = (bf16[512,2048]{1,0:T(8,128)(2,1)}, bf16[512,2048]{1,0:T(8,128)(2,1)}, u32[]{:S(2)}, u32[]{:S(2)}) collective-permute-start(bf16[512,2048]{1,0:T(8,128)(2,1)} %slice.560), channel_id=1, source_target_pairs={{0,1},{1,0},{2,3},{3,2},{4,5},{5,4},{6,7},{7,6},{8,9},{9,8},{10,11... | collective-permute-start | bytes 6291464 | tf_op jit(solution)/shard_map/ppermute | solution.py:646
  824.3 46.8 %collective-permute-start.41 = (bf16[512,2048]{1,0:T(8,128)(2,1)}, bf16[512,2048]{1,0:T(8,128)(2,1)}, u32[]{:S(2)}, u32[]{:S(2)}) collective-permute-start(bf16[512,2048]{1,0:T(8,128)(2,1)} %get-tuple-element.144.refs_0_), channel_id=1, source_target_pairs={{0,2},{2,0},{4,6},{6,4},{8,10},{10,8},{12,14},{14,12},{1,3},{3,1},... | collective-permute-start | bytes 6291464 | tf_op jit(solution)/shard_map/ppermute | solution.py:692
  827.7 52.5 %all-to-all-start.3 = ((bf16[4,128,2048]{2,1,0:T(8,128)(2,1)}), bf16[4,128,2048]{2,1,0:T(8,128)(2,1)S(1)}, u32[]{:S(2)}, u32[]{:S(2)}) async-start(bf16[4,128,2048]{2,1,0:T(8,128)(2,1)} %bitcast.314), calls=%async_computation.3 | async-start | bytes 4194304 | tf_op jit(solution)/shard_map/all_to_all | solution.py:707
  831.5 55.0 %collective-permute-start.40 = (bf16[512,2048]{1,0:T(8,128)(2,1)}, bf16[512,2048]{1,0:T(8,128)(2,1)}, u32[]{:S(2)}, u32[]{:S(2)}) collective-permute-start(bf16[512,2048]{1,0:T(8,128)(2,1)} %get-tuple-element.144.refs_0_), channel_id=1, source_target_pairs={{0,1},{1,0},{2,3},{3,2},{4,5},{5,4},{6,7},{7,6},{8,9},{9,8},{10,11... | collective-permute-start | bytes 6291464 | tf_op jit(solution)/shard_map/ppermute | solution.py:646
  871.1 15.4 %collective-permute-start.42 = (bf16[512,2048]{1,0:T(8,128)(2,1)}, bf16[512,2048]{1,0:T(8,128)(2,1)}, u32[]{:S(2)}, u32[]{:S(2)}) collective-permute-start(bf16[512,2048]{1,0:T(8,128)(2,1)} %collective-permute-done.41.refs_2_), channel_id=1, source_target_pairs={{0,1},{1,0},{2,3},{3,2},{4,5},{5,4},{6,7},{7,6},{8,9},{9,8},{10,11... | collective-permute-start | bytes 6291464 | tf_op jit(solution)/shard_map/ppermute | solution.py:646
  881.6 188.9 %all-to-all-start.6 = ((bf16[4,512,1024]{2,1,0:T(8,128)(2,1)}), bf16[4,512,1024]{2,1,0:T(8,128)(2,1)}, u32[]{:S(2)}, u32[]{:S(2)}) async-start(bf16[4,512,1024]{2,1,0:T(8,128)(2,1)} %after.40), calls=%async_computation.8 | async-start | bytes 8388608 | tf_op jit(solution)/shard_map/all_to_all | solution.py:707
  910.5 25.9 %collective-permute-start.43 = (bf16[512,1028]{0,1:T(8,128)(2,1)S(1)}, bf16[512,1028]{0,1:T(8,128)(2,1)}, u32[]{:S(2)}, u32[]{:S(2)}) collective-permute-start(bf16[512,1028]{0,1:T(8,128)(2,1)S(1)} %copy.226), channel_id=1, source_target_pairs={{0,16},{16,0},{1,17},{17,1},{2,18},{18,2},{3,19},{19,3},{4,20},{20... | collective-permute-start | bytes 3158024 | tf_op jit(solution)/shard_map/ppermute | solution.py:642
  915.8 130.7 %collective-permute-start.46 = (bf16[512,1024]{1,0:T(8,128)(2,1)}, bf16[512,1024]{1,0:T(8,128)(2,1)}, u32[]{:S(2)}, u32[]{:S(2)}) collective-permute-start(bf16[512,1024]{1,0:T(8,128)(2,1)} %get-tuple-element.151), channel_id=1, source_target_pairs={{0,12},{2,14},{4,0},{6,2},{8,4},{10,6},{12,8},{14,10},{1,13},{3,15... | collective-permute-start | bytes 3145736 | tf_op jit(solution)/shard_map/ppermute | solution.py:699
  919.5 150.9 %collective-permute-start.45 = (bf16[512,1024]{1,0:T(8,128)(2,1)}, bf16[512,1024]{1,0:T(8,128)(2,1)}, u32[]{:S(2)}, u32[]{:S(2)}) collective-permute-start(bf16[512,1024]{1,0:T(8,128)(2,1)} %get-tuple-element.152), channel_id=1, source_target_pairs={{0,8},{2,10},{4,12},{6,14},{8,0},{10,2},{12,4},{14,6},{1,9},{3,11}... | collective-permute-start | bytes 3145736 | tf_op jit(solution)/shard_map/ppermute | solution.py:699
  919.5 150.9 %collective-permute-start.44 = (bf16[512,1024]{1,0:T(8,128)(2,1)}, bf16[512,1024]{1,0:T(8,128)(2,1)}, u32[]{:S(2)}, u32[]{:S(2)}) collective-permute-start(bf16[512,1024]{1,0:T(8,128)(2,1)} %get-tuple-element.153), channel_id=1, source_target_pairs={{0,4},{2,6},{4,8},{6,10},{8,12},{10,14},{12,0},{14,2},{1,5},{3,7},... | collective-permute-start | bytes 3145736 | tf_op jit(solution)/shard_map/ppermute | solution.py:699
  1079.9 14.4 %collective-permute-start.48 = (bf16[512,2048]{1,0:T(8,128)(2,1)S(1)}, bf16[512,2048]{1,0:T(8,128)(2,1)S(1)}, u32[]{:S(2)}, u32[]{:S(2)}) collective-permute-start(bf16[512,2048]{1,0:T(8,128)(2,1)S(1)} %pad_maximum_fusion.10), channel_id=1, source_target_pairs={{0,1},{1,0},{2,3},{3,2},{4,5},{5,4},{6,7},{7,6},{8,9},{9,8},{10,11... | collective-permute-start | bytes 6291464 | tf_op jit(solution)/shard_map/ppermute | solution.py:646
  1094.2 68.6 %collective-permute-start.47 = (bf16[512,2048]{1,0:T(8,128)(2,1)}, bf16[512,2048]{1,0:T(8,128)(2,1)}, u32[]{:S(2)}, u32[]{:S(2)}) collective-permute-start(bf16[512,2048]{1,0:T(8,128)(2,1)} %pad_maximum_fusion.11), channel_id=1, source_target_pairs={{0,1},{1,0},{2,3},{3,2},{4,5},{5,4},{6,7},{7,6},{8,9},{9,8},{10,11... | collective-permute-start | bytes 6291464 | tf_op jit(solution)/shard_map/ppermute | solution.py:646
  1096.5 66.4 %collective-permute-start.49 = (bf16[512,2048]{1,0:T(8,128)(2,1)}, bf16[512,2048]{1,0:T(8,128)(2,1)}, u32[]{:S(2)}, u32[]{:S(2)}) collective-permute-start(bf16[512,2048]{1,0:T(8,128)(2,1)} %add_convert_fusion.3.refs_1_), channel_id=1, source_target_pairs={{0,2},{2,0},{4,6},{6,4},{8,10},{10,8},{12,14},{14,12},{1,3},{3,1},... | collective-permute-start | bytes 6291464 | tf_op jit(solution)/shard_map/ppermute | solution.py:692
  1121.0 38.0 %collective-permute-start.50 = (bf16[768,1060]{0,1:T(8,128)(2,1)}, bf16[768,1060]{0,1:T(8,128)(2,1)}, u32[]{:S(2)}, u32[]{:S(2)}) collective-permute-start(bf16[768,1060]{0,1:T(8,128)(2,1)} %copy.235), channel_id=1, source_target_pairs={{0,16},{16,0},{1,17},{17,1},{2,18},{18,2},{3,19},{19,3},{4,20},{20... | collective-permute-start | bytes 4884488 | tf_op jit(solution)/shard_map/ppermute | solution.py:642
  1142.1 39.8 %collective-permute-start.65 = (bf16[256,514]{1,0:T(8,128)(2,1)}, bf16[256,514]{1,0:T(8,128)(2,1)}, u32[]{:S(2)}, u32[]{:S(2)}) collective-permute-start(bf16[256,514]{1,0:T(8,128)(2,1)} %get-tuple-element.209), channel_id=1, source_target_pairs={{0,12},{2,14},{4,0},{6,2},{8,4},{10,6},{12,8},{14,10},{1,13},{3,15... | collective-permute-start | bytes 789512 | tf_op jit(solution)/shard_map/ppermute | solution.py:699
  1142.1 39.9 %collective-permute-start.64 = (bf16[256,514]{1,0:T(8,128)(2,1)}, bf16[256,514]{1,0:T(8,128)(2,1)}, u32[]{:S(2)}, u32[]{:S(2)}) collective-permute-start(bf16[256,514]{1,0:T(8,128)(2,1)} %get-tuple-element.210), channel_id=1, source_target_pairs={{0,8},{2,10},{4,12},{6,14},{8,0},{10,2},{12,4},{14,6},{1,9},{3,11}... | collective-permute-start | bytes 789512 | tf_op jit(solution)/shard_map/ppermute | solution.py:699
  1159.1 22.9 %collective-permute-start.63 = (bf16[256,514]{1,0:T(8,128)(2,1)}, bf16[256,514]{1,0:T(8,128)(2,1)}, u32[]{:S(2)}, u32[]{:S(2)}) collective-permute-start(bf16[256,514]{1,0:T(8,128)(2,1)} %get-tuple-element.211), channel_id=1, source_target_pairs={{0,4},{2,6},{4,8},{6,10},{8,12},{10,14},{12,0},{14,2},{1,5},{3,7},... | collective-permute-start | bytes 789512 | tf_op jit(solution)/shard_map/ppermute | solution.py:699
  1176.6 126.3 %all-to-all-start.7 = ((bf16[4,128,2048]{2,1,0:T(8,128)(2,1)}), bf16[4,128,2048]{2,1,0:T(8,128)(2,1)}, u32[]{:S(2)}, u32[]{:S(2)}) async-start(bf16[4,128,2048]{2,1,0:T(8,128)(2,1)} %bitcast.299), calls=%async_computation.10 | async-start | bytes 4194304 | tf_op jit(solution)/shard_map/all_to_all | solution.py:707
  1202.6 38.9 %collective-permute-start.66 = (bf16[512,512]{1,0:T(8,128)(2,1)}, bf16[512,512]{1,0:T(8,128)(2,1)}, u32[]{:S(2)}, u32[]{:S(2)}) collective-permute-start(bf16[512,512]{1,0:T(8,128)(2,1)} %get-tuple-element.231), channel_id=1, source_target_pairs={{0,1},{1,0},{2,3},{3,2},{4,5},{5,4},{6,7},{7,6},{8,9},{9,8},{10,11... | collective-permute-start | bytes 1572872 | tf_op jit(solution)/shard_map/ppermute | solution.py:646
  1217.9 17.7 %collective-permute-start.67 = (bf16[512,512]{1,0:T(8,128)(2,1)}, bf16[512,512]{1,0:T(8,128)(2,1)}, u32[]{:S(2)}, u32[]{:S(2)}) collective-permute-start(bf16[512,512]{1,0:T(8,128)(2,1)} %get-tuple-element.229), channel_id=1, source_target_pairs={{0,1},{1,0},{2,3},{3,2},{4,5},{5,4},{6,7},{7,6},{8,9},{9,8},{10,11... | collective-permute-start | bytes 1572872 | tf_op jit(solution)/shard_map/ppermute | solution.py:646
  1229.6 17.8 %collective-permute-start.52 = (bf16[384,530]{1,0:T(8,128)(2,1)}, bf16[384,530]{1,0:T(8,128)(2,1)S(1)}, u32[]{:S(2)}, u32[]{:S(2)}) collective-permute-start(bf16[384,530]{1,0:T(8,128)(2,1)} %get-tuple-element.200), channel_id=1, source_target_pairs={{0,4},{2,6},{4,8},{6,10},{8,12},{10,14},{12,0},{14,2},{1,5},{3,7},... | collective-permute-start | bytes 1221128 | tf_op jit(solution)/shard_map/ppermute | solution.py:699
  1231.6 24.2 %collective-permute-start.54 = (bf16[384,530]{1,0:T(8,128)(2,1)}, bf16[384,530]{1,0:T(8,128)(2,1)}, u32[]{:S(2)}, u32[]{:S(2)}) collective-permute-start(bf16[384,530]{1,0:T(8,128)(2,1)} %get-tuple-element.201), channel_id=1, source_target_pairs={{0,12},{2,14},{4,0},{6,2},{8,4},{10,6},{12,8},{14,10},{1,13},{3,15... | collective-permute-start | bytes 1221128 | tf_op jit(solution)/shard_map/ppermute | solution.py:699
  1233.4 43.8 %collective-permute-start.53 = (bf16[384,530]{1,0:T(8,128)(2,1)}, bf16[384,530]{1,0:T(8,128)(2,1)}, u32[]{:S(2)}, u32[]{:S(2)}) collective-permute-start(bf16[384,530]{1,0:T(8,128)(2,1)} %get-tuple-element.202), channel_id=1, source_target_pairs={{0,8},{2,10},{4,12},{6,14},{8,0},{10,2},{12,4},{14,6},{1,9},{3,11}... | collective-permute-start | bytes 1221128 | tf_op jit(solution)/shard_map/ppermute | solution.py:699
  1235.6 45.4 %collective-permute-start.68 = (bf16[512,512]{1,0:T(8,128)(2,1)}, bf16[512,512]{1,0:T(8,128)(2,1)}, u32[]{:S(2)}, u32[]{:S(2)}) collective-permute-start(bf16[512,512]{1,0:T(8,128)(2,1)} %get-tuple-element.227), channel_id=1, source_target_pairs={{0,1},{1,0},{2,3},{3,2},{4,5},{5,4},{6,7},{7,6},{8,9},{9,8},{10,11... | collective-permute-start | bytes 1572872 | tf_op jit(solution)/shard_map/ppermute | solution.py:646
  1305.1 33.3 %all-to-all-start.8 = ((bf16[4,2,2,64,514]{4,3,1,2,0:T(8,128)(2,1)}), bf16[4,2,2,64,514]{4,3,1,2,0:T(8,128)(2,1)}, u32[]{:S(2)}, u32[]{:S(2)}) async-start(bf16[4,2,2,64,514]{4,3,1,2,0:T(8,128)(2,1)} %broadcast_in_dim.98), calls=%async_computation.11 | async-start | bytes 2621440 | tf_op jit(solution)/shard_map/all_to_all | solution.py:707
  (168 other events, 2740.8 us)
Sparse Core Ops, SparseCore 0:
  583.0 98.4 reduce-scatter.3
  683.9 99.2 reduce-scatter.5
  785.5 99.2 reduce-scatter.7

commit v4 on v3

--- a/solution.py
+++ b/solution.py
@@ -994,7 +994,6 @@
     )
     grad_out = trade_z(after(cotangent[:, 0, 0], last_own[0], branch_sum))
     grad_out = rotate(after(grad_out, middle).reshape(held, width))
-    grads = stack_rows(gather_tokens(grad_out))
     last_other[0] = after(last_other[0], ffn_rows)
     own_gate, own_up, own_down = [
         jnp.concatenate([block[i] for block in ffn_own] + [last_own[i // 2][i % 2]], axis=0)
@@ -1010,6 +1009,8 @@
         ffn_rows, own_gate, other_gate, own_up, other_up, (last_other[1],)
     )
 
+    grads = stack_rows(gather_tokens(grad_out, hidden))
+
     def ffn_forward(place):
         return lambda *sent: sum_products([hidden], [own_down], [other_down], *place)
 
@@ -1038,9 +1039,10 @@
     output = trade_z(rotate((middle + ffn_out).astype(BF16)).reshape(depth, share, width))
     gate_full = weight_grad_halves(grad_gates, ffn_rows, swap, tuple(ffn_parts[1:]))
     gate_sums = sum_x(gate_full).reshape(depth, -1, half)
-    up_full = weight_grad_halves(grad_ups, ffn_rows, swap, (gate_full,))
+    down_turned = turn(down_sums, 0)
+    up_full = weight_grad_halves(grad_ups, ffn_rows, swap, (gate_full, down_turned))
     up_sums = sum_x(up_full).reshape(depth, -1, half)
-    down_traded = trade_z(turn(down_sums, 0))
+    down_traded = trade_z(down_turned)
     grad_ffn, grad_ffn_sent, _ = reduce_tokens(
         ffn_back(chip_place, ()),
         ffn_back(other_place, ()),

time: 1370 us -> 1380 us (level)
  starting transfers between devices: 90.9 us -> 144 us
  waiting for transfers between devices: 409 us -> 361 us
    ppermute x19, starting transfers between devices: 18.5 us -> 76.5 us  [over_z(): lax.ppermute(value, 'heads', [(a * wide + b, (a + k) % depth * wide + b)...]
    ppermute x19, waiting for transfers between devices: 148 us -> 121 us  [over_z(): lax.ppermute(value, 'heads', [(a * wide + b, (a + k) % depth * wide + b)...]
    ppermute x11, waiting for transfers between devices: 122 us -> 103 us  [over_y(): lax.ppermute(value, 'heads', [(a * wide + b, a * wide + (b ^ k)) for a in...]
    unnamed x333 -> x331, local copies, waits for them, and re-layouts: 68.8 us -> 68.2 us
  transfers between devices with their start and end apart: 81 -> 81, of which waited for: 34 -> 27; matrix products, arithmetic and copies ran while one was open for 28% -> 27% of each run, Pallas kernels for 27% -> 27%
where the time goes in v4:
time: 1380 us; the launch traced here: 1370 us
  Pallas kernels  398 us (29%)
  waiting for transfers between devices  361 us (26%)
  local copies, waits for them, and re-layouts  204 us (15%)
  other arithmetic  157 us (11%)
  starting transfers between devices  144 us (10%)
  matrix products  85.7 us (6%)
  between operations  16.5 us (1%)
    ppermute x19, waiting for transfers between devices, over_z(): lax.ppermute(value, 'heads', [(a * wide + b, (a + k) % depth * wide + b)...  121 us
    ppermute x11, waiting for transfers between devices, over_y(): lax.ppermute(value, 'heads', [(a * wide + b, a * wide + (b ^ k)) for a in...  103 us
    pallas_call x1, Pallas kernels, attend_backward(): pl.pallas_call(ignoring(backward_kernel, 22, len(waits)), grid_spec=pltpu...  94.4 us
    dot_general x27, matrix products, mm(): lax.dot_general(left, right, (((left_dim,), (right_dim,)), ((), ())), pre...  85.7 us
    pallas_call x4, Pallas kernels, sum_products(): dense_call(kernel, (2 * across, tokens // tall), [left] * count + [own] *...  77.9 us
    ppermute x19, starting transfers between devices, over_z(): lax.ppermute(value, 'heads', [(a * wide + b, (a + k) % depth * wide + b)...  76.5 us
    pallas_call x3, Pallas kernels, weight_grad_halves(): pl.pallas_call(kernel, grid_spec=pltpu.PrefetchScalarGridSpec(num_scalar_...  71.4 us
    unnamed x331, local copies, waits for them, and re-layouts  68.2 us
  transfers between devices with their start and end apart: 81, of which 27 were waited for; matrix products, arithmetic and copies ran while one was open for 27% of the time, Pallas kernels for 27%

profile of v4, /device:TPU:0, one launch (start us, length us, event | category | flops | bytes accessed | tf_op | source)
XLA Modules:
  0.0 1366.3 jit_solution(12499600085865379935)
XLA Ops:
  14.6 6.3 all-to-all-start
  44.7 17.2 %collective-permute-done.5 = bf16[2,2,9344]{2,1,0:T(2,128)(2,1)S(1)} collective-permute-done((bf16[2,2,9344]{2,1,0:T(2,128)(2,1)S(1)}, bf16[2,2,9344]{2,1,0:T(2,128)(2,1)S(1)}, u32[]{:S(2)}, u32[]{:S(2)}) %collective-permute-start.5) | collective-permute-done | bytes 74784 | tf_op jit(solution)/shard_map/ppermute | solution.py:699
  61.9 13.0 collective-permute-done.6
  88.4 5.4 broadcast_select_fusion
  95.6 4.6 fusion.97
  102.4 4.2 all-to-all-start.1
  115.8 15.4 %all-to-all-done.1.refs_1_ = bf16[4,256,512]{2,1,0:T(8,128)(2,1)} async-done(((bf16[4,256,512]{2,1,0:T(8,128)(2,1)}), bf16[4,256,512]{2,1,0:T(8,128)(2,1)}, u32[]{:S(2)}, u32[]{:S(2)}) %all-to-all-start.1) | async-done | bytes 1048608 | tf_op jit(solution)/shard_map/all_to_all | solution.py:707
  152.9 9.7 all-to-all-done.2.refs_1_.refs_0_
  174.4 24.4 %collective-permute-done.10 = bf16[768,1024]{1,0:T(8,128)(2,1)} collective-permute-done((bf16[768,1024]{1,0:T(8,128)(2,1)}, bf16[768,1024]{1,0:T(8,128)(2,1)}, u32[]{:S(2)}, u32[]{:S(2)}) %collective-permute-start.10) | collective-permute-done | bytes 1572896 | tf_op jit(solution)/shard_map/ppermute | solution.py:642
  198.8 4.0 fusion.62
  209.3 4.5 fusion.16
  213.8 20.9 %collective-permute-done.14.refs_11_ = bf16[3,512,1024]{2,1,0:T(8,128)(2,1)} collective-permute-done((bf16[3,512,1024]{2,1,0:T(8,128)(2,1)}, bf16[3,512,1024]{2,1,0:T(8,128)(2,1)}, u32[]{:S(2)}, u32[]{:S(2)}) %collective-permute-start.14) | collective-permute-done | bytes 3145760 | tf_op jit(solution)/shard_map/ppermute | solution.py:699
  239.9 50.8 %attend_forward.1 = (bf16[512,2048]{1,0:T(8,128)(2,1)S(1)}, f32[8,2048]{1,0:T(8,128)S(1)}, f32[8,2048]{1,0:T(8,128)S(1)}, bf16[8,128,2048]{2,1,0:T(8,128)(2,1)S(...) custom-call(s32[16]{0:T(128)S(1)} %slice_reduce_fusion.refs_0_, ...), custom_call_target="tpu_custom_call" | custom-call | flops 17367040000 | bytes 6553600 | tf_op jit(solution)/shard_map/attend_forward/pallas_call | solution.py:266
  292.3 4.6 fusion.77
  297.7 7.7 collective-permute-done.19.refs_1_
  305.4 6.7 add_convert_fusion
  313.8 4.2 add_convert_fusion.1
  327.8 42.3 %collective-permute-done.22 = bf16[512,2048]{1,0:T(8,128)(2,1)} collective-permute-done((bf16[512,2048]{1,0:T(8,128)(2,1)}, bf16[512,2048]{1,0:T(8,128)(2,1)}, u32[]{:S(2)}, u32[]{:S(2)}) %collective-permute-start.22) | collective-permute-done | bytes 2097184 | tf_op jit(solution)/shard_map/ppermute | solution.py:692
  370.1 6.0 multiply_reduce_fusion.4
  378.8 15.0 %collective-permute-done.23.refs_1_ = bf16[3,512,1024]{2,1,0:T(8,128)(2,1)} collective-permute-done((bf16[3,512,1024]{2,1,0:T(8,128)(2,1)}, bf16[3,512,1024]{2,1,0:T(8,128)(2,1)}, u32[]{:S(2)}, u32[]{:S(2)}) %collective-permute-start.23) | collective-permute-done | bytes 3145760 | tf_op jit(solution)/shard_map/ppermute | solution.py:642
  418.8 38.7 %collective-permute-done.27.refs_1_ = bf16[1,512,1024]{2,1,0:T(8,128)(2,1)} collective-permute-done((bf16[1,512,1024]{2,1,0:T(8,128)(2,1)}, bf16[1,512,1024]{2,1,0:T(8,128)(2,1)}, u32[]{:S(2)}, u32[]{:S(2)}) %collective-permute-start.27) | collective-permute-done | bytes 1048608 | tf_op jit(solution)/shard_map/ppermute | solution.py:699
  475.1 10.2 stack_rows.3.refs_1_.refs_0_.right_ref
  494.9 41.6 %gate_forward.1 = (bf16[2048,2048]{1,0:T(8,128)(2,1)}, bf16[2048,2048]{1,0:T(8,128)(2,1)}, bf16[2048,2048]{1,0:T(8,128)(2,1)}) custom-call(bf16[2048,2048]{1,0:T(8,128)(2,1)} %stack_rows.3.refs_1_.refs_0_.right_ref, bf16[2048,1024]{1,0:T(8,128)(2,1)S(1)} %copy-done.2, bf16[2048,1024]{1,0:T(8,128)(2,1)} %pad_maximum_fusion.1.refs_2_.refs_4_, ...), custom_call_target="tpu_custom_call" | custom-call | flops 11453246464 | bytes 4294967 | tf_op jit(solution)/shard_map/gate_forward/pallas_call | solution.py:580
  537.0 4.1 collective-permute-done.36.refs_3_
  541.2 10.0 stack_rows.4.right_ref.refs_0_
  551.2 23.8 %weight_grad_halves.3.refs_5_ = bf16[2,2048,1024]{2,1,0:T(8,128)(2,1)} custom-call(s32[1]{0:T(128)} %bitcast.82.swap_ref, bf16[2048,2048]{1,0:T(8,128)(2,1)} %get-tuple-element.41.refs_0_.refs_1_.left_ref, bf16[2048,2048]{1,0:T(8,128)(2,1)} %stack_rows.4.right_ref.refs_0_), custom_call_target="tpu_custom_call" | custom-call | flops 4294967296 | bytes 2097152 | tf_op jit(solution)/shard_map/weight_grad_halves/pallas_call | solution.py:474
  582.4 13.2 sum_products.5
  601.6 13.5 sum_products.4.refs_6_
  617.1 31.3 %gate_backward.1 = (bf16[2048,2048]{1,0:T(8,128)(2,1)}, bf16[2048,2048]{1,0:T(8,128)(2,1)}) custom-call(bf16[2048,2048]{1,0:T(8,128)(2,1)} %stack_rows.4.right_ref.refs_0_, bf16[2048,1024]{1,0:T(8,128)(2,1)} %pad_maximum_fusion.4.refs_1_, bf16[2048,1024]{1,0:T(8,128)(2,1)} %pad_maximum_fusion.5.refs_2_, bf16[2048,2048]{1,0:T(8,128)(2,1)} %get-tuple-element.42.refs_3_, ...), custom_call_target="tpu_custom_call" | custom-call | flops 5726623232 | bytes 2147483 | tf_op jit(solution)/shard_map/gate_backward/pallas_call | solution.py:598
  649.0 23.8 %weight_grad_halves.4.refs_0_.refs_1_ = bf16[2,2048,1024]{2,1,0:T(8,128)(2,1)} custom-call(s32[1]{0:T(128)} %bitcast.82.swap_ref, bf16[2048,2048]{1,0:T(8,128)(2,1)} %get-tuple-element.44.refs_0_.left_ref, bf16[2048,2048]{1,0:T(8,128)(2,1)} %stack_rows.3.refs_1_.refs_0_.right_ref, bf16[512,2048]{1,0:T(8,128)(2,1)S(1)} %collective-permute-done.33.refs_0_), custom_call_target="tpu_custom_call" | custom-call | flops 4294967296 | bytes 2097152 | tf_op jit(solution)/shard_map/weight_grad_halves/pallas_call | solution.py:474
  672.9 8.8 reduce-scatter.4.cloned.1.call-done
  684.9 23.8 %weight_grad_halves.5.refs_2_ = bf16[2,2048,1024]{2,1,0:T(8,128)(2,1)} custom-call(s32[1]{0:T(128)} %bitcast.82.swap_ref, bf16[2048,2048]{1,0:T(8,128)(2,1)} %get-tuple-element.45.refs_1_.left_ref, bf16[2048,2048]{1,0:T(8,128)(2,1)} %stack_rows.3.refs_1_.refs_0_.right_ref, bf16[2,2048,1024]{2,1,0:T(8,128)(2,1)} %weight_grad_halves.4.refs_0_.refs_1_, ...), custom_call_target="tpu_custom_call" | custom-call | flops 4294967296 | bytes 2097152 | tf_op jit(solution)/shard_map/weight_grad_halves/pallas_call | solution.py:474
  710.7 5.0 all-to-all-start.5
  715.7 25.2 %sum_products.6 = bf16[1024,2048]{1,0:T(8,128)(2,1)S(1)} custom-call(bf16[2048,2048]{1,0:T(8,128)(2,1)} %get-tuple-element.44.refs_0_.left_ref, bf16[2048,2048]{1,0:T(8,128)(2,1)} %get-tuple-element.45.refs_1_.left_ref, bf16[2048,1024]{1,0:T(8,128)(2,1)} %pad_maximum_fusion.refs_1_.refs_2_, bf16[2048,1024]{1,0:T(8,128)(2,1)} %pad_maximum_fusion.2.refs_3_, ...), custom_call_target="tpu_custom_call" | custom-call | flops 5726623232 | bytes 2147483 | tf_op jit(solution)/shard_map/sum_products/pallas_call | solution.py:624
  741.3 4.1 collective-permute-done.37
  747.9 25.9 %sum_products.7 = bf16[1024,2048]{1,0:T(8,128)(2,1)} custom-call(bf16[2048,2048]{1,0:T(8,128)(2,1)} %get-tuple-element.44.refs_0_.left_ref, bf16[2048,2048]{1,0:T(8,128)(2,1)} %get-tuple-element.45.refs_1_.left_ref, bf16[2048,1024]{1,0:T(8,128)(2,1)} %pad_maximum_fusion.refs_1_.refs_2_, bf16[2048,1024]{1,0:T(8,128)(2,1)} %pad_maximum_fusion.2.refs_3_, ...), custom_call_target="tpu_custom_call" | custom-call | flops 5726623232 | bytes 2147483 | tf_op jit(solution)/shard_map/sum_products/pallas_call | solution.py:624
  779.2 15.0 %collective-permute-done.39.refs_0_ = bf16[512,2048]{1,0:T(8,128)(2,1)} collective-permute-done((bf16[512,2048]{1,0:T(8,128)(2,1)S(1)}, bf16[512,2048]{1,0:T(8,128)(2,1)}, u32[]{:S(2)}, u32[]{:S(2)}) %collective-permute-start.39) | collective-permute-done | bytes 2097184 | tf_op jit(solution)/shard_map/ppermute | solution.py:692
  794.2 15.0 %all-to-all-done.5.refs_3_.refs_0_ = bf16[4,512,1024]{2,1,0:T(8,128)(2,1)} async-done(((bf16[4,512,1024]{2,1,0:T(8,128)(2,1)}), bf16[4,512,1024]{2,1,0:T(8,128)(2,1)}, u32[]{:S(2)}, u32[]{:S(2)}) %all-to-all-start.5) | async-done | bytes 4194336 | tf_op jit(solution)/shard_map/all_to_all | solution.py:707
  809.2 5.9 multiply_reduce_fusion
  816.6 8.6 fusion.96
  832.9 39.3 %collective-permute-done.41.refs_2_ = bf16[512,2048]{1,0:T(8,128)(2,1)} collective-permute-done((bf16[512,2048]{1,0:T(8,128)(2,1)}, bf16[512,2048]{1,0:T(8,128)(2,1)}, u32[]{:S(2)}, u32[]{:S(2)}) %collective-permute-start.41) | collective-permute-done | bytes 2097184 | tf_op jit(solution)/shard_map/ppermute | solution.py:692
  882.1 4.9 all-to-all-start.6
  887.0 10.2 stack_rows.5.refs_1_
  897.2 5.8 convolution_convert_fusion
  909.5 9.9 add_convert_fusion.4.refs_13_
  919.4 13.9 %collective-permute-done.43 = bf16[512,1028]{0,1:T(8,128)(2,1)S(1)} collective-permute-done((bf16[512,1028]{0,1:T(8,128)(2,1)S(1)}, bf16[512,1028]{0,1:T(8,128)(2,1)S(1)}, u32[]{:S(2)}, u32[]{:S(2)}) %collective-permute-start.43) | collective-permute-done | bytes 1052704 | tf_op jit(solution)/shard_map/ppermute | solution.py:642
  934.1 4.0 slice_bitcast_fusion.3
  951.1 94.4 %attend_backward.1 = (bf16[800,2048]{1,0:T(8,128)(2,1)S(1)}, f32[8,64,64]{2,1,0:T(8,128)S(1)}) custom-call(s32[16]{0:T(128)S(1)} %copy-done.30, s32[16]{0:T(128)S(1)} %copy-done.32, s32[1,2048]{1,0:T(1,128)S(1)} %copy-done.28, s32[2048,1]{1,0:T(8,128)S(1)} %copy-done.22, s32[2048,1]{1,0:T(8,128)S(1)} %copy-done.22, bf16[768,2048]{1,0:T(8,128)(2,1)S(1)} %copy-done.20, ...), custom_call_target="tpu_custom_call" | custom-call | flops 34406400000 | bytes 9830400 | tf_op jit(solution)/shard_map/attend_backward/pallas_call | solution.py:342
  1050.2 4.1 convolution_convert_fusion.3
  1054.3 3.9 convolution_convert_fusion.2
  1083.0 4.0 fusion.39
  1107.0 4.0 fusion.41
  1122.2 22.6 %collective-permute-start.63 = (bf16[256,514]{1,0:T(8,128)(2,1)}, bf16[256,514]{1,0:T(8,128)(2,1)}, u32[]{:S(2)}, u32[]{:S(2)}) collective-permute-start(bf16[256,514]{1,0:T(8,128)(2,1)} %get-tuple-element.211), channel_id=1, source_target_pairs={{0,4},{2,6},{4,8},{6,10},{8,12},{10,14},{12,0},{14,2},{1,5},{3,7},... | collective-permute-start | bytes 789512 | tf_op jit(solution)/shard_map/ppermute | solution.py:699
  1146.3 19.1 %collective-permute-start.65 = (bf16[256,514]{1,0:T(8,128)(2,1)}, bf16[256,514]{1,0:T(8,128)(2,1)}, u32[]{:S(2)}, u32[]{:S(2)}) collective-permute-start(bf16[256,514]{1,0:T(8,128)(2,1)} %get-tuple-element.209), channel_id=1, source_target_pairs={{0,12},{2,14},{4,0},{6,2},{8,4},{10,6},{12,8},{14,10},{1,13},{3,15... | collective-permute-start | bytes 789512 | tf_op jit(solution)/shard_map/ppermute | solution.py:699
  1169.2 7.3 multiply_reduce_fusion.1
  1176.6 4.0 add_convert_fusion.2
  1188.4 4.6 all-to-all-start.7
  1193.1 4.4 reduce_sum.95
  1201.6 4.4 reduce_sum.94
  1255.1 18.7 %collective-permute-done.53 = bf16[384,530]{1,0:T(8,128)(2,1)} collective-permute-done((bf16[384,530]{1,0:T(8,128)(2,1)}, bf16[384,530]{1,0:T(8,128)(2,1)}, u32[]{:S(2)}, u32[]{:S(2)}) %collective-permute-start.53) | collective-permute-done | bytes 407072 | tf_op jit(solution)/shard_map/ppermute | solution.py:699
  1287.2 11.1 collective-permute-start.56
  1313.3 4.3 all-to-all-start.8
  1322.4 4.1 bitcast_convert_fusion
  1326.5 20.6 %all-to-all-done.8 = bf16[4,2,2,64,514]{4,3,1,2,0:T(8,128)(2,1)} async-done(((bf16[4,2,2,64,514]{4,3,1,2,0:T(8,128)(2,1)}), bf16[4,2,2,64,514]{4,3,1,2,0:T(8,128)(2,1)}, u32[]{:S(2)}, u32[]{:S(2)}) %all-to-all-start.8) | async-done | bytes 1052704 | tf_op jit(solution)/shard_map/all_to_all | solution.py:707
  (727 shorter events, 411.4 us)
Async XLA Ops:
  13.4 69.6 %collective-permute-start.1 = (bf16[128,512]{1,0:T(8,128)(2,1)}, bf16[128,512]{1,0:T(8,128)(2,1)}, u32[]{:S(2)}, u32[]{:S(2)}) collective-permute-start(bf16[128,512]{1,0:T(8,128)(2,1)} %get-tuple-element.257), channel_id=1, source_target_pairs={{0,1},{1,0},{2,3},{3,2},{4,5},{5,4},{6,7},{7,6},{8,9},{9,8},{10,11... | collective-permute-start | bytes 393224 | tf_op jit(solution)/shard_map/ppermute | solution.py:646
  14.6 70.5 %collective-permute-start.2 = (bf16[128,512]{1,0:T(8,128)(2,1)}, bf16[128,512]{1,0:T(8,128)(2,1)}, u32[]{:S(2)}, u32[]{:S(2)}) collective-permute-start(bf16[128,512]{1,0:T(8,128)(2,1)} %get-tuple-element.259), channel_id=1, source_target_pairs={{0,1},{1,0},{2,3},{3,2},{4,5},{5,4},{6,7},{7,6},{8,9},{9,8},{10,11... | collective-permute-start | bytes 393224 | tf_op jit(solution)/shard_map/ppermute | solution.py:646
  14.6 79.7 %all-to-all-start = ((bf16[4,128,2048]{2,1,0:T(8,128)(2,1)}), bf16[4,128,2048]{2,1,0:T(8,128)(2,1)S(1)}, u32[]{:S(2)}, u32[]{:S(2)}) async-start(bf16[4,128,2048]{2,1,0:T(8,128)(2,1)} %bitcast.321), calls=%async_computation | async-start | bytes 4194304 | tf_op jit(solution)/shard_map/all_to_all | solution.py:707
  22.2 12.1 collective-permute-start.3
  38.7 23.2 %collective-permute-start.5 = (bf16[2,2,9344]{2,1,0:T(2,128)(2,1)S(1)}, bf16[2,2,9344]{2,1,0:T(2,128)(2,1)S(1)}, u32[]{:S(2)}, u32[]{:S(2)}) collective-permute-start(bf16[2,2,9344]{2,1,0:T(2,128)(2,1)S(1)} %broadcast_select_fusion.3), channel_id=1, source_target_pairs={{0,4},{2,6},{4,8},{6,10},{8,12},{10,14},{12,0},{14,2},{1,5},{3,7},... | collective-permute-start | bytes 224264 | tf_op jit(solution)/shard_map/ppermute | solution.py:699
  40.7 34.2 %collective-permute-start.6 = (bf16[2,2,9344]{2,1,0:T(2,128)(2,1)S(1)}, bf16[2,2,9344]{2,1,0:T(2,128)(2,1)S(1)}, u32[]{:S(2)}, u32[]{:S(2)}) collective-permute-start(bf16[2,2,9344]{2,1,0:T(2,128)(2,1)S(1)} %broadcast_select_fusion.3), channel_id=1, source_target_pairs={{0,8},{2,10},{4,12},{6,14},{8,0},{10,2},{12,4},{14,6},{1,9},{3,11}... | collective-permute-start | bytes 224264 | tf_op jit(solution)/shard_map/ppermute | solution.py:699
  43.1 31.8 %collective-permute-start.7 = (bf16[2,2,9344]{2,1,0:T(2,128)(2,1)S(1)}, bf16[2,2,9344]{2,1,0:T(2,128)(2,1)S(1)}, u32[]{:S(2)}, u32[]{:S(2)}) collective-permute-start(bf16[2,2,9344]{2,1,0:T(2,128)(2,1)S(1)} %broadcast_select_fusion.3), channel_id=1, source_target_pairs={{0,12},{2,14},{4,0},{6,2},{8,4},{10,6},{12,8},{14,10},{1,13},{3,15... | collective-permute-start | bytes 224264 | tf_op jit(solution)/shard_map/ppermute | solution.py:699
  61.9 26.5 %collective-permute-start.13 = (bf16[3,512,512]{2,1,0:T(8,128)(2,1)}, bf16[3,512,512]{2,1,0:T(8,128)(2,1)}, u32[]{:S(2)}, u32[]{:S(2)}) collective-permute-start(bf16[3,512,512]{2,1,0:T(8,128)(2,1)} %pad_maximum_fusion.17), channel_id=1, source_target_pairs={{0,1},{1,0},{2,3},{3,2},{4,5},{5,4},{6,7},{7,6},{8,9},{9,8},{10,11... | collective-permute-start | bytes 4718600 | tf_op jit(solution)/shard_map/ppermute | solution.py:646
  93.8 71.7 %collective-permute-start.15 = (bf16[3,512,1024]{2,1,0:T(8,128)(2,1)}, bf16[3,512,1024]{2,1,0:T(8,128)(2,1)}, u32[]{:S(2)}, u32[]{:S(2)}) collective-permute-start(bf16[3,512,1024]{2,1,0:T(8,128)(2,1)} %get-tuple-element.182), channel_id=1, source_target_pairs={{0,16},{16,0},{1,17},{17,1},{2,18},{18,2},{3,19},{19,3},{4,20},{20... | collective-permute-start | bytes 9437192 | tf_op jit(solution)/shard_map/ppermute | solution.py:642
  102.4 28.7 %all-to-all-start.1 = ((bf16[4,256,512]{2,1,0:T(8,128)(2,1)}), bf16[4,256,512]{2,1,0:T(8,128)(2,1)}, u32[]{:S(2)}, u32[]{:S(2)}) async-start(bf16[4,256,512]{2,1,0:T(8,128)(2,1)} %broadcast_in_dim.53), calls=%async_computation.1 | async-start | bytes 2097152 | tf_op jit(solution)/shard_map/all_to_all | solution.py:707
  111.5 53.2 %collective-permute-start.11 = (bf16[512,2048]{1,0:T(8,128)(2,1)}, bf16[512,2048]{1,0:T(8,128)(2,1)}, u32[]{:S(2)}, u32[]{:S(2)}) collective-permute-start(bf16[512,2048]{1,0:T(8,128)(2,1)} %multiply_convert_fusion.1), channel_id=1, source_target_pairs={{0,2},{2,0},{4,6},{6,4},{8,10},{10,8},{12,14},{14,12},{1,3},{3,1},... | collective-permute-start | bytes 6291464 | tf_op jit(solution)/shard_map/ppermute | solution.py:692
  133.2 29.4 %all-to-all-start.2 = ((bf16[4,256,512]{2,1,0:T(8,128)(2,1)}), bf16[4,256,512]{2,1,0:T(8,128)(2,1)S(1)}, u32[]{:S(2)}, u32[]{:S(2)}) async-start(bf16[4,256,512]{2,1,0:T(8,128)(2,1)} %broadcast_in_dim.88), calls=%async_computation.2 | async-start | bytes 2097152 | tf_op jit(solution)/shard_map/all_to_all | solution.py:707
  143.3 31.1 %collective-permute-start.9 = (bf16[512,2048]{1,0:T(8,128)(2,1)}, bf16[512,2048]{1,0:T(8,128)(2,1)}, u32[]{:S(2)}, u32[]{:S(2)}) collective-permute-start(bf16[512,2048]{1,0:T(8,128)(2,1)} %multiply_convert_fusion.1), channel_id=1, source_target_pairs={{0,1},{1,0},{2,3},{3,2},{4,5},{5,4},{6,7},{7,6},{8,9},{9,8},{10,11... | collective-permute-start | bytes 6291464 | tf_op jit(solution)/shard_map/ppermute | solution.py:646
  151.8 47.1 %collective-permute-start.10 = (bf16[768,1024]{1,0:T(8,128)(2,1)}, bf16[768,1024]{1,0:T(8,128)(2,1)}, u32[]{:S(2)}, u32[]{:S(2)}) collective-permute-start(bf16[768,1024]{1,0:T(8,128)(2,1)} %pad_maximum_fusion.16), channel_id=1, source_target_pairs={{0,16},{16,0},{1,17},{17,1},{2,18},{18,2},{3,19},{19,3},{4,20},{20... | collective-permute-start | bytes 4718600 | tf_op jit(solution)/shard_map/ppermute | solution.py:642
  163.6 71.2 %collective-permute-start.14 = (bf16[3,512,1024]{2,1,0:T(8,128)(2,1)}, bf16[3,512,1024]{2,1,0:T(8,128)(2,1)}, u32[]{:S(2)}, u32[]{:S(2)}) collective-permute-start(bf16[3,512,1024]{2,1,0:T(8,128)(2,1)} %after.30), channel_id=1, source_target_pairs={{0,4},{2,6},{4,8},{6,10},{8,12},{10,14},{12,0},{14,2},{1,5},{3,7},... | collective-permute-start | bytes 9437192 | tf_op jit(solution)/shard_map/ppermute | solution.py:699
  164.7 42.3 %collective-permute-start.12 = (bf16[512,2048]{1,0:T(8,128)(2,1)}, bf16[512,2048]{1,0:T(8,128)(2,1)}, u32[]{:S(2)}, u32[]{:S(2)}) collective-permute-start(bf16[512,2048]{1,0:T(8,128)(2,1)} %collective-permute-done.11), channel_id=1, source_target_pairs={{0,1},{1,0},{2,3},{3,2},{4,5},{5,4},{6,7},{7,6},{8,9},{9,8},{10,11... | collective-permute-start | bytes 6291464 | tf_op jit(solution)/shard_map/ppermute | solution.py:646
  173.7 131.7 %collective-permute-start.17 = (bf16[512,1024]{1,0:T(8,128)(2,1)}, bf16[512,1024]{1,0:T(8,128)(2,1)}, u32[]{:S(2)}, u32[]{:S(2)}) collective-permute-start(bf16[512,1024]{1,0:T(8,128)(2,1)} %maximum_select_fusion.8), channel_id=1, source_target_pairs={{0,16},{16,0},{1,17},{17,1},{2,18},{18,2},{3,19},{19,3},{4,20},{20... | collective-permute-start | bytes 3145736 | tf_op jit(solution)/shard_map/ppermute | solution.py:642
  234.7 70.6 %collective-permute-start.19 = (bf16[3,512,1024]{2,1,0:T(8,128)(2,1)}, bf16[3,512,1024]{2,1,0:T(8,128)(2,1)}, u32[]{:S(2)}, u32[]{:S(2)}) collective-permute-start(bf16[3,512,1024]{2,1,0:T(8,128)(2,1)} %collective-permute-done.14.refs_11_), channel_id=1, source_target_pairs={{0,4},{2,6},{4,8},{6,10},{8,12},{10,14},{12,0},{14,2},{1,5},{3,7},... | collective-permute-start | bytes 9437192 | tf_op jit(solution)/shard_map/ppermute | solution.py:699
  235.1 70.2 %collective-permute-start.20 = (bf16[3,512,1024]{2,1,0:T(8,128)(2,1)}, bf16[3,512,1024]{2,1,0:T(8,128)(2,1)}, u32[]{:S(2)}, u32[]{:S(2)}) collective-permute-start(bf16[3,512,1024]{2,1,0:T(8,128)(2,1)} %collective-permute-done.14.refs_11_), channel_id=1, source_target_pairs={{0,16},{16,0},{1,17},{17,1},{2,18},{18,2},{3,19},{19,3},{4,20},{20... | collective-permute-start | bytes 9437192 | tf_op jit(solution)/shard_map/ppermute | solution.py:642
  322.2 47.9 %collective-permute-start.22 = (bf16[512,2048]{1,0:T(8,128)(2,1)}, bf16[512,2048]{1,0:T(8,128)(2,1)}, u32[]{:S(2)}, u32[]{:S(2)}) collective-permute-start(bf16[512,2048]{1,0:T(8,128)(2,1)} %add_convert_fusion.8), channel_id=1, source_target_pairs={{0,2},{2,0},{4,6},{6,4},{8,10},{10,8},{12,14},{14,12},{1,3},{3,1},... | collective-permute-start | bytes 6291464 | tf_op jit(solution)/shard_map/ppermute | solution.py:692
  323.7 70.1 %collective-permute-start.23 = (bf16[3,512,1024]{2,1,0:T(8,128)(2,1)}, bf16[3,512,1024]{2,1,0:T(8,128)(2,1)}, u32[]{:S(2)}, u32[]{:S(2)}) collective-permute-start(bf16[3,512,1024]{2,1,0:T(8,128)(2,1)} %collective-permute-done.19.refs_1_), channel_id=1, source_target_pairs={{0,16},{16,0},{1,17},{17,1},{2,18},{18,2},{3,19},{19,3},{4,20},{20... | collective-permute-start | bytes 9437192 | tf_op jit(solution)/shard_map/ppermute | solution.py:642
  327.5 66.7 %collective-permute-start.26 = (bf16[2,512,1024]{2,1,0:T(8,128)(2,1)}, bf16[2,512,1024]{2,1,0:T(8,128)(2,1)}, u32[]{:S(2)}, u32[]{:S(2)}) collective-permute-start(bf16[2,512,1024]{2,1,0:T(8,128)(2,1)} %slice.537), channel_id=1, source_target_pairs={{0,4},{2,6},{4,8},{6,10},{8,12},{10,14},{12,0},{14,2},{1,5},{3,7},... | collective-permute-start | bytes 6291464 | tf_op jit(solution)/shard_map/ppermute | solution.py:699
  393.8 63.7 %collective-permute-start.25 = (bf16[512,2048]{1,0:T(8,128)(2,1)}, bf16[512,2048]{1,0:T(8,128)(2,1)}, u32[]{:S(2)}, u32[]{:S(2)}) collective-permute-start(bf16[512,2048]{1,0:T(8,128)(2,1)} %after.33.refs_0_), channel_id=1, source_target_pairs={{0,2},{2,0},{4,6},{6,4},{8,10},{10,8},{12,14},{14,12},{1,3},{3,1},... | collective-permute-start | bytes 6291464 | tf_op jit(solution)/shard_map/ppermute | solution.py:692
  394.3 74.8 %all-to-all-start.4 = ((bf16[4,128,2048]{2,1,0:T(8,128)(2,1)}), bf16[4,128,2048]{2,1,0:T(8,128)(2,1)S(1)}, u32[]{:S(2)}, u32[]{:S(2)}) async-start(bf16[4,128,2048]{2,1,0:T(8,128)(2,1)} %after.37), calls=%async_computation.4 | async-start | bytes 4194304 | tf_op jit(solution)/shard_map/all_to_all | solution.py:707
  397.9 283.8 %reduce-scatter.4.cloned.1.call-start = ((), (), s32[]{:S(2)}) async-start(), calls=%async_computation.12 | async-start | bytes 12582912 | tf_op jit(solution)/shard_map/reduce_scatter | solution.py:1020
  401.8 55.7 %collective-permute-start.27 = (bf16[1,512,1024]{2,1,0:T(8,128)(2,1)}, bf16[1,512,1024]{2,1,0:T(8,128)(2,1)}, u32[]{:S(2)}, u32[]{:S(2)}) collective-permute-start(bf16[1,512,1024]{2,1,0:T(8,128)(2,1)} %after.34), channel_id=1, source_target_pairs={{0,4},{2,6},{4,8},{6,10},{8,12},{10,14},{12,0},{14,2},{1,5},{3,7},... | collective-permute-start | bytes 3145736 | tf_op jit(solution)/shard_map/ppermute | solution.py:699
  418.1 67.2 %collective-permute-start.29 = (bf16[2,512,1024]{2,1,0:T(8,128)(2,1)}, bf16[2,512,1024]{2,1,0:T(8,128)(2,1)}, u32[]{:S(2)}, u32[]{:S(2)}) collective-permute-start(bf16[2,512,1024]{2,1,0:T(8,128)(2,1)} %collective-permute-done.26.refs_1_), channel_id=1, source_target_pairs={{0,16},{16,0},{1,17},{17,1},{2,18},{18,2},{3,19},{19,3},{4,20},{20... | collective-permute-start | bytes 6291464 | tf_op jit(solution)/shard_map/ppermute | solution.py:642
  418.8 56.3 %collective-permute-start.24 = (bf16[512,2048]{1,0:T(8,128)(2,1)}, bf16[512,2048]{1,0:T(8,128)(2,1)}, u32[]{:S(2)}, u32[]{:S(2)}) collective-permute-start(bf16[512,2048]{1,0:T(8,128)(2,1)} %after.33.refs_0_), channel_id=1, source_target_pairs={{0,1},{1,0},{2,3},{3,2},{4,5},{5,4},{6,7},{7,6},{8,9},{9,8},{10,11... | collective-permute-start | bytes 6291464 | tf_op jit(solution)/shard_map/ppermute | solution.py:646
  457.5 17.6 %collective-permute-start.28 = (bf16[512,2048]{1,0:T(8,128)(2,1)}, bf16[512,2048]{1,0:T(8,128)(2,1)}, u32[]{:S(2)}, u32[]{:S(2)}) collective-permute-start(bf16[512,2048]{1,0:T(8,128)(2,1)} %after.35.refs_2_), channel_id=1, source_target_pairs={{0,1},{1,0},{2,3},{3,2},{4,5},{5,4},{6,7},{7,6},{8,9},{9,8},{10,11... | collective-permute-start | bytes 6291464 | tf_op jit(solution)/shard_map/ppermute | solution.py:646
  468.3 25.2 %collective-permute-start.30 = (bf16[1,512,1024]{2,1,0:T(8,128)(2,1)}, bf16[1,512,1024]{2,1,0:T(8,128)(2,1)S(1)}, u32[]{:S(2)}, u32[]{:S(2)}) collective-permute-start(bf16[1,512,1024]{2,1,0:T(8,128)(2,1)} %collective-permute-done.27.refs_1_), channel_id=1, source_target_pairs={{0,16},{16,0},{1,17},{17,1},{2,18},{18,2},{3,19},{19,3},{4,20},{20... | collective-permute-start | bytes 3145736 | tf_op jit(solution)/shard_map/ppermute | solution.py:642
  473.5 63.0 %collective-permute-start.35 = (bf16[512,2048]{1,0:T(8,128)(2,1)S(1)}, bf16[512,2048]{1,0:T(8,128)(2,1)}, u32[]{:S(2)}, u32[]{:S(2)}) collective-permute-start(bf16[512,2048]{1,0:T(8,128)(2,1)S(1)} %maximum_select_fusion.3.refs_0_), channel_id=1, source_target_pairs={{0,2},{2,0},{4,6},{6,4},{8,10},{10,8},{12,14},{14,12},{1,3},{3,1},... | collective-permute-start | bytes 6291464 | tf_op jit(solution)/shard_map/ppermute | solution.py:692
  475.1 61.9 %collective-permute-start.34 = (bf16[512,2048]{1,0:T(8,128)(2,1)S(1)}, bf16[512,2048]{1,0:T(8,128)(2,1)}, u32[]{:S(2)}, u32[]{:S(2)}) collective-permute-start(bf16[512,2048]{1,0:T(8,128)(2,1)S(1)} %maximum_select_fusion.3.refs_0_), channel_id=1, source_target_pairs={{0,1},{1,0},{2,3},{3,2},{4,5},{5,4},{6,7},{7,6},{8,9},{9,8},{10,11... | collective-permute-start | bytes 6291464 | tf_op jit(solution)/shard_map/ppermute | solution.py:646
  575.0 300.8 %reduce-scatter.6.cloned.1.call-start = ((), (), s32[]{:S(2)}) async-start(), calls=%async_computation.13 | async-start | bytes 12582912 | tf_op jit(solution)/shard_map/reduce_scatter | solution.py:1020
  601.0 48.0 %collective-permute-start.33 = (bf16[512,2048]{1,0:T(8,128)(2,1)S(1)}, bf16[512,2048]{1,0:T(8,128)(2,1)S(1)}, u32[]{:S(2)}, u32[]{:S(2)}) collective-permute-start(bf16[512,2048]{1,0:T(8,128)(2,1)S(1)} %add_convert_fusion.7.refs_7_), channel_id=1, source_target_pairs={{0,2},{2,0},{4,6},{6,4},{8,10},{10,8},{12,14},{14,12},{1,3},{3,1},... | collective-permute-start | bytes 6291464 | tf_op jit(solution)/shard_map/ppermute | solution.py:692
  672.9 261.2 %reduce-scatter.8.cloned.1.call-start = ((), (), s32[]{:S(2)}) async-start(), calls=%async_computation.14 | async-start | bytes 12582912 | tf_op jit(solution)/shard_map/reduce_scatter | solution.py:1020
  710.7 98.5 %all-to-all-start.5 = ((bf16[4,512,1024]{2,1,0:T(8,128)(2,1)}), bf16[4,512,1024]{2,1,0:T(8,128)(2,1)}, u32[]{:S(2)}, u32[]{:S(2)}) async-start(bf16[4,512,1024]{2,1,0:T(8,128)(2,1)} %copy-done.6), calls=%async_computation.6 | async-start | bytes 8388608 | tf_op jit(solution)/shard_map/all_to_all | solution.py:707
  746.3 47.8 %collective-permute-start.39 = (bf16[512,2048]{1,0:T(8,128)(2,1)S(1)}, bf16[512,2048]{1,0:T(8,128)(2,1)}, u32[]{:S(2)}, u32[]{:S(2)}) collective-permute-start(bf16[512,2048]{1,0:T(8,128)(2,1)S(1)} %add_convert_fusion.5.refs_6_), channel_id=1, source_target_pairs={{0,2},{2,0},{4,6},{6,4},{8,10},{10,8},{12,14},{14,12},{1,3},{3,1},... | collective-permute-start | bytes 6291464 | tf_op jit(solution)/shard_map/ppermute | solution.py:692
  777.1 32.1 %collective-permute-start.38 = (bf16[512,2048]{1,0:T(8,128)(2,1)}, bf16[512,2048]{1,0:T(8,128)(2,1)}, u32[]{:S(2)}, u32[]{:S(2)}) collective-permute-start(bf16[512,2048]{1,0:T(8,128)(2,1)} %slice.570), channel_id=1, source_target_pairs={{0,1},{1,0},{2,3},{3,2},{4,5},{5,4},{6,7},{7,6},{8,9},{9,8},{10,11... | collective-permute-start | bytes 6291464 | tf_op jit(solution)/shard_map/ppermute | solution.py:646
  778.7 36.4 %collective-permute-start.31 = (bf16[512,2048]{1,0:T(8,128)(2,1)}, bf16[512,2048]{1,0:T(8,128)(2,1)}, u32[]{:S(2)}, u32[]{:S(2)}) collective-permute-start(bf16[512,2048]{1,0:T(8,128)(2,1)} %slice.560), channel_id=1, source_target_pairs={{0,1},{1,0},{2,3},{3,2},{4,5},{5,4},{6,7},{7,6},{8,9},{9,8},{10,11... | collective-permute-start | bytes 6291464 | tf_op jit(solution)/shard_map/ppermute | solution.py:646
  825.2 47.0 %collective-permute-start.41 = (bf16[512,2048]{1,0:T(8,128)(2,1)}, bf16[512,2048]{1,0:T(8,128)(2,1)}, u32[]{:S(2)}, u32[]{:S(2)}) collective-permute-start(bf16[512,2048]{1,0:T(8,128)(2,1)} %get-tuple-element.144.refs_0_), channel_id=1, source_target_pairs={{0,2},{2,0},{4,6},{6,4},{8,10},{10,8},{12,14},{14,12},{1,3},{3,1},... | collective-permute-start | bytes 6291464 | tf_op jit(solution)/shard_map/ppermute | solution.py:692
  829.0 51.7 %all-to-all-start.3 = ((bf16[4,128,2048]{2,1,0:T(8,128)(2,1)}), bf16[4,128,2048]{2,1,0:T(8,128)(2,1)S(1)}, u32[]{:S(2)}, u32[]{:S(2)}) async-start(bf16[4,128,2048]{2,1,0:T(8,128)(2,1)} %bitcast.314), calls=%async_computation.3 | async-start | bytes 4194304 | tf_op jit(solution)/shard_map/all_to_all | solution.py:707
  832.8 54.2 %collective-permute-start.40 = (bf16[512,2048]{1,0:T(8,128)(2,1)}, bf16[512,2048]{1,0:T(8,128)(2,1)}, u32[]{:S(2)}, u32[]{:S(2)}) collective-permute-start(bf16[512,2048]{1,0:T(8,128)(2,1)} %get-tuple-element.144.refs_0_), channel_id=1, source_target_pairs={{0,1},{1,0},{2,3},{3,2},{4,5},{5,4},{6,7},{7,6},{8,9},{9,8},{10,11... | collective-permute-start | bytes 6291464 | tf_op jit(solution)/shard_map/ppermute | solution.py:646
  872.2 14.8 %collective-permute-start.42 = (bf16[512,2048]{1,0:T(8,128)(2,1)}, bf16[512,2048]{1,0:T(8,128)(2,1)}, u32[]{:S(2)}, u32[]{:S(2)}) collective-permute-start(bf16[512,2048]{1,0:T(8,128)(2,1)} %collective-permute-done.41.refs_2_), channel_id=1, source_target_pairs={{0,1},{1,0},{2,3},{3,2},{4,5},{5,4},{6,7},{7,6},{8,9},{9,8},{10,11... | collective-permute-start | bytes 6291464 | tf_op jit(solution)/shard_map/ppermute | solution.py:646
  882.1 165.8 %all-to-all-start.6 = ((bf16[4,512,1024]{2,1,0:T(8,128)(2,1)}), bf16[4,512,1024]{2,1,0:T(8,128)(2,1)}, u32[]{:S(2)}, u32[]{:S(2)}) async-start(bf16[4,512,1024]{2,1,0:T(8,128)(2,1)} %after.42), calls=%async_computation.8 | async-start | bytes 8388608 | tf_op jit(solution)/shard_map/all_to_all | solution.py:707
  907.5 25.7 %collective-permute-start.43 = (bf16[512,1028]{0,1:T(8,128)(2,1)S(1)}, bf16[512,1028]{0,1:T(8,128)(2,1)S(1)}, u32[]{:S(2)}, u32[]{:S(2)}) collective-permute-start(bf16[512,1028]{0,1:T(8,128)(2,1)S(1)} %copy.227), channel_id=1, source_target_pairs={{0,16},{16,0},{1,17},{17,1},{2,18},{18,2},{3,19},{19,3},{4,20},{20... | collective-permute-start | bytes 3158024 | tf_op jit(solution)/shard_map/ppermute | solution.py:642
  938.1 109.8 %collective-permute-start.44 = (bf16[512,1024]{1,0:T(8,128)(2,1)}, bf16[512,1024]{1,0:T(8,128)(2,1)}, u32[]{:S(2)}, u32[]{:S(2)}) collective-permute-start(bf16[512,1024]{1,0:T(8,128)(2,1)} %get-tuple-element.153), channel_id=1, source_target_pairs={{0,4},{2,6},{4,8},{6,10},{8,12},{10,14},{12,0},{14,2},{1,5},{3,7},... | collective-permute-start | bytes 3145736 | tf_op jit(solution)/shard_map/ppermute | solution.py:699
  939.8 109.2 %collective-permute-start.45 = (bf16[512,1024]{1,0:T(8,128)(2,1)}, bf16[512,1024]{1,0:T(8,128)(2,1)}, u32[]{:S(2)}, u32[]{:S(2)}) collective-permute-start(bf16[512,1024]{1,0:T(8,128)(2,1)} %get-tuple-element.152), channel_id=1, source_target_pairs={{0,8},{2,10},{4,12},{6,14},{8,0},{10,2},{12,4},{14,6},{1,9},{3,11}... | collective-permute-start | bytes 3145736 | tf_op jit(solution)/shard_map/ppermute | solution.py:699
  942.2 106.8 %collective-permute-start.46 = (bf16[512,1024]{1,0:T(8,128)(2,1)}, bf16[512,1024]{1,0:T(8,128)(2,1)}, u32[]{:S(2)}, u32[]{:S(2)}) collective-permute-start(bf16[512,1024]{1,0:T(8,128)(2,1)} %get-tuple-element.151), channel_id=1, source_target_pairs={{0,12},{2,14},{4,0},{6,2},{8,4},{10,6},{12,8},{14,10},{1,13},{3,15... | collective-permute-start | bytes 3145736 | tf_op jit(solution)/shard_map/ppermute | solution.py:699
  1058.5 14.9 %collective-permute-start.48 = (bf16[512,2048]{1,0:T(8,128)(2,1)S(1)}, bf16[512,2048]{1,0:T(8,128)(2,1)S(1)}, u32[]{:S(2)}, u32[]{:S(2)}) collective-permute-start(bf16[512,2048]{1,0:T(8,128)(2,1)S(1)} %pad_maximum_fusion.10), channel_id=1, source_target_pairs={{0,1},{1,0},{2,3},{3,2},{4,5},{5,4},{6,7},{7,6},{8,9},{9,8},{10,11... | collective-permute-start | bytes 6291464 | tf_op jit(solution)/shard_map/ppermute | solution.py:646
  1073.3 95.8 %collective-permute-start.47 = (bf16[512,2048]{1,0:T(8,128)(2,1)}, bf16[512,2048]{1,0:T(8,128)(2,1)}, u32[]{:S(2)}, u32[]{:S(2)}) collective-permute-start(bf16[512,2048]{1,0:T(8,128)(2,1)} %pad_maximum_fusion.11), channel_id=1, source_target_pairs={{0,1},{1,0},{2,3},{3,2},{4,5},{5,4},{6,7},{7,6},{8,9},{9,8},{10,11... | collective-permute-start | bytes 6291464 | tf_op jit(solution)/shard_map/ppermute | solution.py:646
  1075.9 93.3 %collective-permute-start.49 = (bf16[512,2048]{1,0:T(8,128)(2,1)}, bf16[512,2048]{1,0:T(8,128)(2,1)}, u32[]{:S(2)}, u32[]{:S(2)}) collective-permute-start(bf16[512,2048]{1,0:T(8,128)(2,1)} %add_convert_fusion.3.refs_1_), channel_id=1, source_target_pairs={{0,2},{2,0},{4,6},{6,4},{8,10},{10,8},{12,14},{14,12},{1,3},{3,1},... | collective-permute-start | bytes 6291464 | tf_op jit(solution)/shard_map/ppermute | solution.py:692
  1103.8 42.5 %collective-permute-start.50 = (bf16[768,1060]{0,1:T(8,128)(2,1)}, bf16[768,1060]{0,1:T(8,128)(2,1)}, u32[]{:S(2)}, u32[]{:S(2)}) collective-permute-start(bf16[768,1060]{0,1:T(8,128)(2,1)} %copy.236), channel_id=1, source_target_pairs={{0,16},{16,0},{1,17},{17,1},{2,18},{18,2},{3,19},{19,3},{4,20},{20... | collective-permute-start | bytes 4884488 | tf_op jit(solution)/shard_map/ppermute | solution.py:642
  1122.2 97.6 %collective-permute-start.63 = (bf16[256,514]{1,0:T(8,128)(2,1)}, bf16[256,514]{1,0:T(8,128)(2,1)}, u32[]{:S(2)}, u32[]{:S(2)}) collective-permute-start(bf16[256,514]{1,0:T(8,128)(2,1)} %get-tuple-element.211), channel_id=1, source_target_pairs={{0,4},{2,6},{4,8},{6,10},{8,12},{10,14},{12,0},{14,2},{1,5},{3,7},... | collective-permute-start | bytes 789512 | tf_op jit(solution)/shard_map/ppermute | solution.py:699
  1144.8 75.1 %collective-permute-start.64 = (bf16[256,514]{1,0:T(8,128)(2,1)}, bf16[256,514]{1,0:T(8,128)(2,1)}, u32[]{:S(2)}, u32[]{:S(2)}) collective-permute-start(bf16[256,514]{1,0:T(8,128)(2,1)} %get-tuple-element.210), channel_id=1, source_target_pairs={{0,8},{2,10},{4,12},{6,14},{8,0},{10,2},{12,4},{14,6},{1,9},{3,11}... | collective-permute-start | bytes 789512 | tf_op jit(solution)/shard_map/ppermute | solution.py:699
  1146.3 73.6 %collective-permute-start.65 = (bf16[256,514]{1,0:T(8,128)(2,1)}, bf16[256,514]{1,0:T(8,128)(2,1)}, u32[]{:S(2)}, u32[]{:S(2)}) collective-permute-start(bf16[256,514]{1,0:T(8,128)(2,1)} %get-tuple-element.209), channel_id=1, source_target_pairs={{0,12},{2,14},{4,0},{6,2},{8,4},{10,6},{12,8},{14,10},{1,13},{3,15... | collective-permute-start | bytes 789512 | tf_op jit(solution)/shard_map/ppermute | solution.py:699
  1188.4 122.6 %all-to-all-start.7 = ((bf16[4,128,2048]{2,1,0:T(8,128)(2,1)}), bf16[4,128,2048]{2,1,0:T(8,128)(2,1)}, u32[]{:S(2)}, u32[]{:S(2)}) async-start(bf16[4,128,2048]{2,1,0:T(8,128)(2,1)} %bitcast.300), calls=%async_computation.10 | async-start | bytes 4194304 | tf_op jit(solution)/shard_map/all_to_all | solution.py:707
  1201.6 41.9 %collective-permute-start.67 = (bf16[512,512]{1,0:T(8,128)(2,1)}, bf16[512,512]{1,0:T(8,128)(2,1)}, u32[]{:S(2)}, u32[]{:S(2)}) collective-permute-start(bf16[512,512]{1,0:T(8,128)(2,1)} %get-tuple-element.229), channel_id=1, source_target_pairs={{0,1},{1,0},{2,3},{3,2},{4,5},{5,4},{6,7},{7,6},{8,9},{9,8},{10,11... | collective-permute-start | bytes 1572872 | tf_op jit(solution)/shard_map/ppermute | solution.py:646
  1219.9 29.5 %collective-permute-start.66 = (bf16[512,512]{1,0:T(8,128)(2,1)}, bf16[512,512]{1,0:T(8,128)(2,1)}, u32[]{:S(2)}, u32[]{:S(2)}) collective-permute-start(bf16[512,512]{1,0:T(8,128)(2,1)} %get-tuple-element.231), channel_id=1, source_target_pairs={{0,1},{1,0},{2,3},{3,2},{4,5},{5,4},{6,7},{7,6},{8,9},{9,8},{10,11... | collective-permute-start | bytes 1572872 | tf_op jit(solution)/shard_map/ppermute | solution.py:646
  1236.7 18.4 %collective-permute-start.52 = (bf16[384,530]{1,0:T(8,128)(2,1)}, bf16[384,530]{1,0:T(8,128)(2,1)S(1)}, u32[]{:S(2)}, u32[]{:S(2)}) collective-permute-start(bf16[384,530]{1,0:T(8,128)(2,1)} %get-tuple-element.200), channel_id=1, source_target_pairs={{0,4},{2,6},{4,8},{6,10},{8,12},{10,14},{12,0},{14,2},{1,5},{3,7},... | collective-permute-start | bytes 1221128 | tf_op jit(solution)/shard_map/ppermute | solution.py:699
  1238.7 35.2 %collective-permute-start.53 = (bf16[384,530]{1,0:T(8,128)(2,1)}, bf16[384,530]{1,0:T(8,128)(2,1)}, u32[]{:S(2)}, u32[]{:S(2)}) collective-permute-start(bf16[384,530]{1,0:T(8,128)(2,1)} %get-tuple-element.202), channel_id=1, source_target_pairs={{0,8},{2,10},{4,12},{6,14},{8,0},{10,2},{12,4},{14,6},{1,9},{3,11}... | collective-permute-start | bytes 1221128 | tf_op jit(solution)/shard_map/ppermute | solution.py:699
  1241.0 32.8 %collective-permute-start.54 = (bf16[384,530]{1,0:T(8,128)(2,1)}, bf16[384,530]{1,0:T(8,128)(2,1)}, u32[]{:S(2)}, u32[]{:S(2)}) collective-permute-start(bf16[384,530]{1,0:T(8,128)(2,1)} %get-tuple-element.201), channel_id=1, source_target_pairs={{0,12},{2,14},{4,0},{6,2},{8,4},{10,6},{12,8},{14,10},{1,13},{3,15... | collective-permute-start | bytes 1221128 | tf_op jit(solution)/shard_map/ppermute | solution.py:699
  1243.6 33.3 %collective-permute-start.68 = (bf16[512,512]{1,0:T(8,128)(2,1)}, bf16[512,512]{1,0:T(8,128)(2,1)}, u32[]{:S(2)}, u32[]{:S(2)}) collective-permute-start(bf16[512,512]{1,0:T(8,128)(2,1)} %get-tuple-element.227), channel_id=1, source_target_pairs={{0,1},{1,0},{2,3},{3,2},{4,5},{5,4},{6,7},{7,6},{8,9},{9,8},{10,11... | collective-permute-start | bytes 1572872 | tf_op jit(solution)/shard_map/ppermute | solution.py:646
  1287.2 15.0 %collective-permute-start.56 = (f32[2,2,34,64]{3,1,2,0:T(2,128)S(1)}, f32[2,2,34,64]{3,1,2,0:T(2,128)S(1)}, u32[]{:S(2)}, u32[]{:S(2)}) collective-permute-start(f32[2,2,34,64]{3,1,2,0:T(2,128)S(1)} %bitcast.351), channel_id=1, source_target_pairs={{0,4},{2,6},{4,8},{6,10},{8,12},{10,14},{12,0},{14,2},{1,5},{3,7},... | collective-permute-start | bytes 104456 | tf_op jit(solution)/shard_map/ppermute | solution.py:699
  1313.3 33.9 %all-to-all-start.8 = ((bf16[4,2,2,64,514]{4,3,1,2,0:T(8,128)(2,1)}), bf16[4,2,2,64,514]{4,3,1,2,0:T(8,128)(2,1)}, u32[]{:S(2)}, u32[]{:S(2)}) async-start(bf16[4,2,2,64,514]{4,3,1,2,0:T(8,128)(2,1)} %broadcast_in_dim.98), calls=%async_computation.11 | async-start | bytes 2621440 | tf_op jit(solution)/shard_map/all_to_all | solution.py:707
  (167 other events, 2725.7 us)
Sparse Core Ops, SparseCore 0:
  575.1 106.5 reduce-scatter.3
  684.1 99.2 reduce-scatter.5
  785.7 99.2 reduce-scatter.7
